TPU v7x, 1024 devices: a whole 8x8x8 slice. The times are simulated.
1024 devices in a mesh: prow: 32 (over z_lo, y), pcol: 32 (over x, z_hi, core).
Axes of the slice: x: 8, y: 8, z: 8 (z_hi: 2, z_lo: 4; z = z_hi * 4 + z_lo), core: 2. Of those that a mesh axis runs over, the one named last changes fastest.
Arguments:
- inverse_blocks: float32 [16384, 16384], P('prow', 'pcol'), may hold values from -6 to 6
- panel_one: float32 [16384, 256], P(('prow', 'pcol')), may hold values from -0.046875 to 0.046875
- panel_two: float32 [16384, 256], P(('prow', 'pcol')), may hold values from -0.046875 to 0.046875
- tile_mask: int32 [2, 64], replicated, may hold values 0 or 1
- diag_one: float32 [256, 256], replicated, may hold values from -6 to 6
- diag_two: float32 [256, 256], replicated, may hold values from -6 to 6
- link_block: float32 [256, 256], replicated, may hold values from -0.375 to 0.375
Outputs:
- column_one: float32 [16384, 256], P(('prow', 'pcol'))
- corner_one: float32 [256, 256], replicated
- column_two: float32 [16384, 256], P(('prow', 'pcol'))
- link_two: float32 [256, 256], replicated
- corner_two: float32 [256, 256], replicated
All inputs are finite; a program needn't handle non-finite values.
Results may differ from a plain program's by a relative error of at most 0.000071.
Values sent between devices are 32-bit elements; how exact they have to be, the bound alone decides.
No kernel may reach another device: no remote copies, remote signals or barrier semaphores. Data moves between devices by JAX's collectives and lax.ppermute only.
A program may use at most 32 MiB of HBM per device.

v0:
```python
import jax
import jax.numpy as jnp
from jax import lax
from jax.sharding import PartitionSpec as P


def from_root(value, axis, source):
    kept = jnp.where(lax.axis_index(axis) == source, value, 0).astype(value.dtype)
    return lax.psum(kept, axis)


def prod(a, b):
    return jnp.dot(a, b, precision=lax.Precision.HIGHEST, preferred_element_type=jnp.float32)


def inner(a, b):
    return lax.dot_general(
        a,
        b,
        (((0,), (0,)), ((), ())),
        precision=lax.Precision.HIGHEST,
        preferred_element_type=jnp.float32,
    )


def local(inverse_blocks, panel_one, panel_two, tile_mask, diag_one, diag_two, link_block):
    span = panel_one.shape[0]
    width = panel_one.shape[1]
    n_rows = lax.axis_size("prow")
    n_cols = lax.axis_size("pcol")
    ratio = n_rows // n_cols
    row_index = lax.axis_index("prow")
    col_index = lax.axis_index("pcol")
    begin = (row_index * n_cols + col_index) * span
    spread = jnp.repeat(tile_mask.astype(jnp.float32), width, axis=1)
    live_one = panel_one * lax.dynamic_slice_in_dim(spread[0], begin, span)[:, None]
    live_two = panel_two * lax.dynamic_slice_in_dim(spread[1], begin, span)[:, None]

    def column_panel(live):
        group = lax.all_gather(live, "pcol", axis=0, tiled=True)
        pieces = from_root(group, "prow", col_index * ratio + 0)
        return pieces

    def product(live):
        panel = column_panel(live)
        return lax.psum_scatter(
            -prod(inverse_blocks, panel), "pcol", scatter_dimension=0, tiled=True
        )

    def grid_sum(value):
        return lax.psum(value, ("prow", "pcol"))

    column_one = product(live_one)
    plain_two = product(live_two)
    column_two = plain_two - prod(column_one, link_block)
    corner_one = diag_one - grid_sum(inner(live_one, column_one))
    crossed = grid_sum(inner(column_one, live_two))
    folded = grid_sum(inner(live_two, column_two))
    link_two = -(crossed + prod(corner_one, link_block))
    corner_two = diag_two - folded - inner(link_block, link_two)
    return (column_one, corner_one, column_two, link_two, corner_two)


def solution(mesh):
    placed = (
        P("prow", "pcol"),
        P(("prow", "pcol"), None),
        P(("prow", "pcol"), None),
        P(),
        P(),
        P(),
        P(),
    )
    return jax.shard_map(
        local,
        mesh=mesh,
        in_specs=placed,
        out_specs=(P(("prow", "pcol"), None), P(), P(("prow", "pcol"), None), P(), P()),
        check_vma=False,
    )
```

profile of v0, /device:TPU:1, one launch (start us, length us, event | category | flops | bytes accessed | tf_op | source)
XLA Modules:
  0.0 1018.5 jit_solution(826327276101516045)
XLA Ops:
  7.2 0.0 copy-start
  7.2 0.0 all-reduce.7.cloned.1.call-start
  7.2 0.0 copy-start.13
  7.2 0.7 copy-done.13
  8.0 0.1 broadcast_bitcast_fusion
  8.1 0.0 copy-start.11
  8.2 0.1 dynamic_slice.7
  8.3 0.1 dynamic_slice.6
  8.3 0.5 copy-done.11
  8.9 0.1 broadcast_multiply_fusion.1
  8.9 0.0 copy-start.12
  8.9 64.1 %all_gather.6 = f32[512,256]{1,0:T(8,128)S(1)} all-gather(f32[16,256]{1,0:T(8,128)S(1)} %broadcast_multiply_fusion.1), channel_id=1, replica_groups=mesh['prow'=32,'pcol'=32] {'pcol'}, dimensions={0}, use_global_device_ids=true | all-gather | bytes 540672 | tf_op jit(solution)/shard_map/all_gather | solution.py:40
  73.0 0.0 copy-done.12
  73.0 0.1 broadcast_multiply_fusion
  73.1 51.0 %all_gather.7 = f32[512,256]{1,0:T(8,128)S(1)} all-gather(f32[16,256]{1,0:T(8,128)S(1)} %broadcast_multiply_fusion), channel_id=1, replica_groups=mesh['prow'=32,'pcol'=32] {'pcol'}, dimensions={0}, use_global_device_ids=true | all-gather | bytes 540672 | tf_op jit(solution)/shard_map/all_gather | solution.py:40
  124.1 0.8 broadcast_select_fusion.1
  125.0 0.9 broadcast_select_fusion
  125.8 0.0 all-reduce.7.cloned.1.call-update
  125.8 0.0 reduce-scatter.7.cloned.1.call-start
  125.9 293.3 %all-reduce.7.cloned.1.call-done = (f32[512,256]{1,0:T(8,128)}, f32[512,256]{1,0:T(8,128)}) async-done(((f32[512,256]{1,0:T(8,128)}, f32[512,256]{1,0:T(8,128)}), (f32[512,256]{1,0:T(8,128)}, f32[512,256]{1,0:T(8,128)})) %all-reduce.7.cloned.1.call-update) | async-done | bytes 1048592 | tf_op jit(solution)/shard_map/psum | solution.py:9
  419.2 0.0 copy-done
  419.2 2.9 fusion.1
  422.1 1.0 copy.20
  423.1 0.0 copy-start.4
  423.1 0.0 reduce-scatter.7.cloned.1.call-update
  423.1 0.0 reduce-scatter.9.cloned.1.call-start
  423.1 1.0 copy-done.4
  424.1 1.9 fusion
  426.0 1.0 copy.22
  427.0 0.0 copy-start.1
  427.0 0.0 reduce-scatter.9.cloned.1.call-update
  427.0 0.0 all-reduce.5.cloned.1.call-start
  427.1 147.2 %reduce-scatter.7.cloned.1.call-done = f32[16,256]{1,0:T(8,128)} async-done(((f32[512,256]{1,0:T(8,128)}), f32[16,256]{1,0:T(8,128)}) %reduce-scatter.7.cloned.1.call-update) | async-done | bytes 16400
  574.3 137.2 %reduce-scatter.9.cloned.1.call-done = f32[16,256]{1,0:T(8,128)} async-done(((f32[512,256]{1,0:T(8,128)}), f32[16,256]{1,0:T(8,128)}) %reduce-scatter.9.cloned.1.call-update) | async-done | bytes 16400 | tf_op jit(solution)/shard_map/reduce_scatter | solution.py:46
  711.5 0.0 copy-done.1
  711.5 1.0 convolution_subtract_fusion
  712.5 0.0 copy-start.10
  712.5 0.0 copy-start.9
  712.5 1.1 fusion.6
  713.6 0.0 copy-done.10
  713.6 0.0 copy-done.9
  713.6 1.1 fusion.4
  714.8 1.1 fusion.5
  715.9 0.0 copy-start.5
  715.9 0.0 all-reduce.5.cloned.1.call-update
  715.9 292.6 %all-reduce.5.cloned.1.call-done = (f32[256,256]{1,0:T(8,128)}, f32[256,256]{1,0:T(8,128)}, f32[256,256]{1,0:T(8,128)}) async-done(((f32[256,256]{1,0:T(8,128)}, f32[256,256]{1,0:T(8,128)}, f32[256,256]{1,0:T(8,128)}), (f32[256,256]{1,0:T(8,128)}, f32[256,256]{1,0:T(8,128)}, f32[256,256]{1,0:T(8,128)})) %all-reduce.5.cloned.1.call-update) | async-done | bytes 786448 | tf_op jit(solution)/shard_map/psum | solution.py:51
  1008.5 0.0 copy-done.5
  1008.5 0.0 copy-start.8
  1008.5 1.0 sub.12
  1009.5 0.0 copy-start.2
  1009.5 0.0 copy-done.8
  1009.5 0.0 copy-start.6
  1009.6 0.0 copy-start.7
  1009.6 0.4 fusion.3
  1009.9 0.3 copy-done.2
  1010.2 0.0 copy-start.3
  1010.2 0.4 copy-done.6
  1010.6 0.1 copy-done.7
  1010.7 1.3 fusion.2
  1012.0 0.0 copy-done.3
  (4 shorter events, 0.1 us)
Async XLA Ops:
  7.2 412.0 %copy-start = (f32[512,512]{1,0:T(8,128)S(1)}, f32[512,512]{1,0:T(8,128)}, u32[]{:S(2)}) copy-start(f32[512,512]{1,0:T(8,128)} %param.7) | copy-start | bytes 3145732
  7.2 412.0 %all-reduce.7.cloned.1.call-start = ((), (), s32[]{:S(2)}) async-start(), calls=%async_computation.5 | async-start | bytes 2097152 | tf_op jit(solution)/shard_map/psum | solution.py:9
  7.2 0.8 copy-start.13
  8.1 0.7 copy-start.11
  8.9 64.1 %copy-start.12 = (f32[16,256]{1,0:T(8,128)S(1)}, f32[16,256]{1,0:T(8,128)}, u32[]{:S(2)}) copy-start(f32[16,256]{1,0:T(8,128)} %param.9) | copy-start | bytes 49156
  125.8 448.4 %reduce-scatter.7.cloned.1.call-start = ((), (), s32[]{:S(2)}) async-start(), calls=%async_computation.2 | async-start | bytes 540672
  423.1 1.0 copy-start.4
  423.1 288.4 %reduce-scatter.9.cloned.1.call-start = ((), (), s32[]{:S(2)}) async-start(), calls=%async_computation.3 | async-start | bytes 540672 | tf_op jit(solution)/shard_map/reduce_scatter | solution.py:46
  427.0 284.5 %copy-start.1 = (f32[256,256]{1,0:T(8,128)S(1)}, f32[256,256]{1,0:T(8,128)}, u32[]{:S(2)}) copy-start(f32[256,256]{1,0:T(8,128)} %param.13) | copy-start | bytes 786436
  427.0 581.5 %all-reduce.5.cloned.1.call-start = ((), (), s32[]{:S(2)}) async-start(), calls=%async_computation.4 | async-start | bytes 1572864 | tf_op jit(solution)/shard_map/psum | solution.py:51
  712.5 1.1 copy-start.10
  712.5 1.1 copy-start.9
  715.9 292.6 %copy-start.5 = (f32[256,256]{1,0:T(8,128)S(1)}, f32[256,256]{1,0:T(8,128)}, u32[]{:S(2)}) copy-start(f32[256,256]{1,0:T(8,128)} %param.11) | copy-start | bytes 786436
  1008.5 1.0 copy-start.8
  1009.5 0.7 copy-start.2
  1009.5 1.0 copy-start.6
  1009.6 1.1 copy-start.7
  1010.2 1.8 copy-start.3
Sparse Core Ops, SparseCore 0:
  126.0 293.1 all-reduce.6
  426.4 147.7 reduce-scatter.6
  580.0 131.4 reduce-scatter.8
  717.8 290.6 all-reduce.4
where the time goes:
time: 1020 us
  waiting for transfers between devices  870 us (85%)
  blocking collectives  115 us (11%)
  between operations  13.9 us (1%)
  matrix products  10.8 us (1%)
    psum x1, waiting for transfers between devices, from_root(): return lax.psum(kept, axis)  293 us
    psum x1, waiting for transfers between devices, grid_sum(): return lax.psum(value, ('prow', 'pcol'))  293 us
    unnamed x5, waiting for transfers between devices  147 us
    reduce_scatter x1, waiting for transfers between devices, product(): lax.psum_scatter(-prod(inverse_blocks, panel), 'pcol', scatter_dimension=...  137 us
    all_gather x2, blocking collectives, column_panel(): group = lax.all_gather(live, 'pcol', axis=0, tiled=True)  115 us
  transfers between devices with their start and end apart: 4, of which 4 were waited for; matrix products, arithmetic and copies ran while one was open for 0% of the time, Pallas kernels for 0%

commit v1 on v0

v1 whole, which is shorter than its diff:
```python
import jax
import jax.numpy as jnp
from jax import lax
from jax.sharding import Mesh
from jax.sharding import PartitionSpec as P

ROW = (("zl", 4), ("y", 8))
COL = (("x", 8), ("zh", 2), ("core", 2))
PROW = tuple(n for n, _ in ROW)
PCOL = tuple(n for n, _ in COL)
ALL = PROW + PCOL
SWAP = [(0, 1), (1, 0)]


def mm(a, b, dims=((1,), (0,))):
    return lax.dot_general(
        a,
        b,
        (dims, ((), ())),
        precision=lax.Precision.HIGH,
        preferred_element_type=jnp.float32,
    )


def inner(a, b):
    return mm(a, b, ((0,), (0,)))


def local(inverse_blocks, panel_one, panel_two, tile_mask, diag_one, diag_two, link_block):
    span, width = panel_one.shape
    nzl, ny, nx = lax.axis_size("zl"), lax.axis_size("y"), lax.axis_size("x")
    n = nzl * ny
    core, zh = lax.axis_index("core"), lax.axis_index("zh")
    begin = (lax.axis_index(PROW) * n + lax.axis_index(PCOL)) * span
    spread = lax.dynamic_slice_in_dim(tile_mask, begin // width, 1, axis=1).astype(jnp.float32)
    live = jnp.concatenate([panel_one * spread[0], panel_two * spread[1]], axis=1)
    live_one, live_two = live[:, :width], live[:, width:]

    perm = [(c * n + j, ((j % nzl) * ny + j // nzl) * n + c) for c in range(n) for j in range(n)]
    panel = lax.ppermute(live, ALL, perm)
    panel = lax.all_gather(panel, "zl", axis=0, tiled=True)
    panel = lax.all_gather(panel, "y", axis=0, tiled=True)

    blocks = inverse_blocks.reshape(nx, 2, 2, span, n * span)
    theirs = lax.dynamic_index_in_dim(blocks, 1 - core, 2, keepdims=False).reshape(-1, n * span)
    mine = lax.dynamic_index_in_dim(blocks, core, 2, keepdims=False).reshape(-1, n * span)
    came = lax.ppermute(mm(theirs, panel), "core", SWAP)
    total = came + mm(mine, panel)
    total = lax.all_to_all(total.reshape(nx, 2 * span, 2 * width), "x", 0, 0, tiled=True)
    total = jnp.sum(total, axis=0).reshape(2, span, 2 * width)
    came = lax.ppermute(lax.dynamic_index_in_dim(total, 1 - zh, 0, keepdims=False), "zh", SWAP)
    total = -(came + lax.dynamic_index_in_dim(total, zh, 0, keepdims=False))
    column_one = total[:, :width]
    column_two = total[:, width:] - mm(column_one, link_block)

    half = width // 2

    def halves(which):
        def cut(a):
            return lax.dynamic_slice_in_dim(a, which * half, half, axis=1)

        return jnp.stack(
            [
                inner(cut(live_one), column_one),
                inner(cut(column_one), live_two),
                inner(cut(live_two), column_two),
            ]
        )

    came = lax.ppermute(halves(1 - core), "core", SWAP)
    grams = came + halves(core)
    part = 3 * half // nx
    grams = lax.all_to_all(grams.reshape(nx, part, width), "x", 0, 0, tiled=True)
    grams = jnp.sum(grams, axis=0)
    grams = jnp.sum(lax.all_gather(grams, "y", axis=0), axis=0)
    grams = jnp.sum(lax.all_gather(grams, ("zh", "zl"), axis=0), axis=0)
    grams = lax.all_gather(grams, "x", axis=0, tiled=True).reshape(3, half, width)
    other = lax.ppermute(grams, "core", SWAP)
    first = jnp.where(core == 0, grams, other)
    second = jnp.where(core == 0, other, grams)
    grams = jnp.concatenate([first, second], axis=1)

    corner_one = diag_one - grams[0]
    link_two = -(grams[1] + mm(corner_one, link_block))
    corner_two = diag_two - grams[2] - inner(link_block, link_two)
    return (column_one, corner_one, column_two, link_two, corner_two)


def solution(mesh):
    fine = Mesh(mesh.devices.reshape([k for _, k in ROW + COL]), ALL)
    rows = P(ALL, None)
    return jax.shard_map(
        local,
        mesh=fine,
        in_specs=(P(PROW, PCOL), rows, rows, P(), P(), P(), P()),
        out_specs=(rows, P(), rows, P(), P()),
        check_vma=False,
    )
```

time: 1020 us -> 247 us (0.24)
  waiting for transfers between devices: 870 us -> 70.3 us
  starting transfers between devices: 0.16 us -> 53.2 us
  blocking collectives: 115 us -> 97.5 us
    psum x2 -> x0, waiting for transfers between devices: 586 us -> none  [the longest x1 293 us: from_root(): return lax.psum(kept, axis)]
    unnamed x5 -> x1, waiting for transfers between devices: 147 us -> 0.02 us
    reduce_scatter x1 -> x0, waiting for transfers between devices: 137 us -> none  [product(): lax.psum_scatter(-prod(inverse_blocks, panel), 'pcol', scatter_dimension=...]
    all_gather x0 -> x1, waiting for transfers between devices: none -> 47.4 us  [local(): panel = lax.all_gather(panel, 'y', axis=0, tiled=True)]
    ppermute x0 -> x5, starting transfers between devices: none -> 46.9 us  [the longest x1 21.2 us: local(): other = lax.ppermute(grams, 'core', SWAP)]
    all_gather x2 -> x4, blocking collectives: 115 us -> 79.9 us  [the longest x1 21.3 us: local(): grams = jnp.sum(lax.all_gather(grams, ('zh', 'zl'), axis=0), axis=0)]
    all_to_all x0 -> x1, waiting for transfers between devices: none -> 18 us  [local(): lax.all_to_all(total.reshape(nx, 2 * span, 2 * width), 'x', 0, 0, tiled=T...]
    all_to_all x0 -> x1, blocking collectives: none -> 17.5 us  [local(): lax.all_to_all(grams.reshape(nx, part, width), 'x', 0, 0, tiled=True)]
  transfers between devices with their start and end apart: 4 -> 7, of which waited for: 4 -> 7; matrix products, arithmetic and copies ran while one was open for 0% -> 1% of each run, Pallas kernels for 0% -> 0%
where the time goes in v1:
time: 247 us
  blocking collectives  97.5 us (39%)
  waiting for transfers between devices  70.3 us (28%)
  starting transfers between devices  53.2 us (22%)
  between operations  14.4 us (6%)
  matrix products  5.68 us (2%)
  local copies, waits for them, and re-layouts  3.31 us (1%)
  other arithmetic  2.55 us (1%)
    all_gather x1, waiting for transfers between devices, local(): panel = lax.all_gather(panel, 'y', axis=0, tiled=True)  47.4 us
    all_gather x1, blocking collectives, local(): grams = jnp.sum(lax.all_gather(grams, ('zh', 'zl'), axis=0), axis=0)  21.3 us
    ppermute x1, starting transfers between devices, local(): other = lax.ppermute(grams, 'core', SWAP)  21.2 us
    all_gather x1, blocking collectives, local(): panel = lax.all_gather(panel, 'zl', axis=0, tiled=True)  21 us
    all_gather x1, blocking collectives, local(): lax.all_gather(grams, 'x', axis=0, tiled=True).reshape(3, half, width)  19 us
    all_gather x1, blocking collectives, local(): grams = jnp.sum(lax.all_gather(grams, 'y', axis=0), axis=0)  18.7 us
    all_to_all x1, waiting for transfers between devices, local(): lax.all_to_all(total.reshape(nx, 2 * span, 2 * width), 'x', 0, 0, tiled=T...  18 us
    all_to_all x1, blocking collectives, local(): lax.all_to_all(grams.reshape(nx, part, width), 'x', 0, 0, tiled=True)  17.5 us
  transfers between devices with their start and end apart: 7, of which 7 were waited for; matrix products, arithmetic and copies ran while one was open for 1% of the time, Pallas kernels for 0%

profile of v1, /device:TPU:1, one launch (start us, length us, event | category | flops | bytes accessed | tf_op | source)
XLA Modules:
  0.0 247.0 jit_solution(12887132071859038726)
XLA Ops:
  7.2 0.0 copy-start
  7.2 0.0 all-gather.4.cloned.1.call-start
  7.2 0.0 copy-start.10
  7.3 0.0 copy-start.9
  7.3 0.0 copy-start.8
  7.3 0.7 copy-done.10
  8.0 0.1 fusion.23
  8.0 0.5 fusion.24
  8.5 0.0 copy-done.9
  8.6 0.0 copy-done.8
  8.6 1.3 broadcast_multiply_fusion
  9.9 6.3 %collective-permute-start = (f32[16,512]{1,0:T(8,128)S(1)}, f32[16,512]{1,0:T(8,128)S(1)}, u32[]{:S(2)}, u32[]{:S(2)}) collective-permute-start(f32[16,512]{1,0:T(8,128)S(1)} %pad_maximum_fusion.2), channel_id=1, source_target_pairs={{0,0},{1,256},{2,512},{3,768},{4,32},{5,288},{6,544},{7,800},{8,64... | collective-permute-start | bytes 98312 | tf_op jit(solution)/shard_map/ppermute | solution.py:40
  16.2 1.0 collective-permute-done
  17.2 21.0 %all_gather.21 = f32[64,512]{1,0:T(8,128)} all-gather(f32[16,512]{1,0:T(8,128)S(1)} %collective-permute-done), channel_id=1, replica_groups=mesh['zl'=4,'y'=8,'x'=8,'zh'=2,'core'=2] {'zl'}, dimensions={0}, use_global_device_ids=true | all-gather | bytes 163840 | tf_op jit(solution)/shard_map/all_gather | solution.py:41
  38.2 0.0 all-gather.4.cloned.1.call-update
  38.2 1.3 constant_dynamic-slice_fusion
  39.5 47.4 %all-gather.4.cloned.1.call-done = f32[512,512]{1,0:T(8,128)} async-done(((f32[64,512]{1,0:T(8,128)}), f32[512,512]{1,0:T(8,128)}) %all-gather.4.cloned.1.call-update) | async-done | bytes 1048592 | tf_op jit(solution)/shard_map/all_gather | solution.py:42
  86.9 0.0 copy-start.1
  86.9 1.9 fusion.25
  88.9 7.5 %collective-permute-start.1 = (f32[256,512]{1,0:T(8,128)S(1)}, f32[256,512]{1,0:T(8,128)S(1)}, u32[]{:S(2)}, u32[]{:S(2)}) collective-permute-start(f32[256,512]{1,0:T(8,128)S(1)} %fusion.25), channel_id=1, source_target_pairs={{0,1},{1,0},{2,3},{3,2},{4,5},{5,4},{6,7},{7,6},{8,9},{9,8},{10,11... | collective-permute-start | bytes 1572872 | tf_op jit(solution)/shard_map/ppermute | solution.py:47
  96.4 0.0 copy-done.1
  96.4 0.6 fusion.26
  97.1 0.9 collective-permute-done.1
  97.9 0.9 add.61
  98.8 6.3 %all-to-all-start = ((f32[8,32,512]{2,1,0:T(8,128)}), f32[8,32,512]{2,1,0:T(8,128)S(1)}, u32[]{:S(2)}, u32[]{:S(2)}) async-start(f32[8,32,512]{2,1,0:T(8,128)} %bitcast.5), calls=%async_computation | async-start | bytes 1048576 | tf_op jit(solution)/shard_map/all_to_all | solution.py:49
  105.1 18.0 %all-to-all-done = f32[8,32,512]{2,1,0:T(8,128)S(1)} async-done(((f32[8,32,512]{2,1,0:T(8,128)}), f32[8,32,512]{2,1,0:T(8,128)S(1)}, u32[]{:S(2)}, u32[]{:S(2)}) %all-to-all-start) | async-done | bytes 524320 | tf_op jit(solution)/shard_map/all_to_all | solution.py:49
  123.1 8.5 %collective-permute-start.2 = (f32[16,512]{1,0:T(8,128)S(1)}, f32[16,512]{1,0:T(8,128)S(1)}, u32[]{:S(2)}, u32[]{:S(2)}) collective-permute-start(f32[16,512]{1,0:T(8,128)S(1)} %dynamic-slice_bitcast_fusion), channel_id=1, source_target_pairs={{0,2},{2,0},{1,3},{3,1},{4,6},{6,4},{5,7},{7,5},{8,10},{10,8},{9,1... | collective-permute-start | bytes 98312 | tf_op jit(solution)/shard_map/ppermute | solution.py:51
  131.6 1.3 collective-permute-done.2
  132.9 0.0 copy-start.4
  132.9 0.3 convolution_bitcast_fusion.6
  133.2 0.3 convolution_bitcast_fusion.5
  133.5 0.0 copy-done
  133.5 0.1 slice_subtract_fusion
  133.6 0.0 copy-start.7
  133.6 0.3 convolution_bitcast_fusion.4
  134.0 3.4 %collective-permute-start.3 = (f32[3,128,256]{2,1,0:T(8,128)S(1)}, f32[3,128,256]{2,1,0:T(8,128)S(1)}, u32[]{:S(2)}, u32[]{:S(2)}) collective-permute-start(f32[3,128,256]{2,1,0:T(8,128)S(1)} %pad_maximum_fusion), channel_id=1, source_target_pairs={{0,1},{1,0},{2,3},{3,2},{4,5},{5,4},{6,7},{7,6},{8,9},{9,8},{10,11... | collective-permute-start | bytes 1179656 | tf_op jit(solution)/shard_map/ppermute | solution.py:70
  137.4 0.0 copy-done.7
  137.4 0.3 convolution_bitcast_fusion.1
  137.6 0.3 convolution_bitcast_fusion.2
  137.9 0.0 copy-done.4
  137.9 0.3 convolution_bitcast_fusion.3
  138.2 0.5 collective-permute-done.3
  138.7 0.1 maximum_add_fusion
  138.7 17.5 %all_to_all.10 = f32[8,48,256]{2,1,0:T(8,128)S(1)} all-to-all(f32[8,48,256]{2,1,0:T(8,128)S(1)} %bitcast.69), channel_id=1, replica_groups=mesh['zl'=4,'y'=8,'x'=8,'zh'=2,'core'=2] {'x'}, dimensions={0} | all-to-all | bytes 786432 | tf_op jit(solution)/shard_map/all_to_all | solution.py:73
  156.3 18.7 %all-gather = f32[384,256]{1,0:T(8,128)S(1)} all-gather(f32[48,256]{1,0:T(8,128)S(1)} %reduce_sum.37), channel_id=2, replica_groups=mesh['zl'=4,'y'=8,'x'=8,'zh'=2,'core'=2] {'y'}, dimensions={0}, use_global_device_ids=true | all-gather | bytes 442368 | tf_op jit(solution)/shard_map/all_gather | solution.py:75
  175.0 21.3 %all-gather.1 = f32[384,256]{1,0:T(8,128)S(1)} all-gather(f32[48,256]{1,0:T(8,128)S(1)} %reduce_sum.38), channel_id=3, replica_groups=mesh['zl'=4,'y'=8,'x'=8,'zh'=2,'core'=2] {'zh','zl'}, dimensions={0}, use_global_device_ids=true | all-gather | bytes 442368 | tf_op jit(solution)/shard_map/all_gather | solution.py:76
  196.3 19.0 %all_gather.27 = f32[384,256]{1,0:T(8,128)S(1)} all-gather(f32[48,256]{1,0:T(8,128)S(1)} %reduce_sum.39), channel_id=1, replica_groups=mesh['zl'=4,'y'=8,'x'=8,'zh'=2,'core'=2] {'x'}, dimensions={0}, use_global_device_ids=true | all-gather | bytes 442368 | tf_op jit(solution)/shard_map/all_gather | solution.py:77
  215.3 21.2 %collective-permute-start.4 = (f32[3,128,256]{2,1,0:T(8,128)S(1)}, f32[3,128,256]{2,1,0:T(8,128)S(1)}, u32[]{:S(2)}, u32[]{:S(2)}) collective-permute-start(f32[3,128,256]{2,1,0:T(8,128)S(1)} %bitcast.67), channel_id=1, source_target_pairs={{0,1},{1,0},{2,3},{3,2},{4,5},{5,4},{6,7},{7,6},{8,9},{9,8},{10,11... | collective-permute-start | bytes 1179656 | tf_op jit(solution)/shard_map/ppermute | solution.py:78
  236.5 0.0 copy-start.5
  236.5 1.3 collective-permute-done.4
  237.9 0.1 broadcast_select_fusion
  237.9 0.0 copy-done.5
  238.0 0.0 copy-start.2
  238.0 0.0 copy-start.6
  238.0 0.3 fusion.3
  238.3 0.4 copy-done.2
  238.7 0.4 copy-done.6
  239.0 0.0 copy-start.3
  239.0 1.1 fusion.9
  240.1 0.0 copy-done.3
  (10 shorter events, 0.2 us)
Async XLA Ops:
  7.2 126.3 %copy-start = (f32[256,256]{1,0:T(8,128)S(1)}, f32[256,256]{1,0:T(8,128)}, u32[]{:S(2)}) copy-start(f32[256,256]{1,0:T(8,128)} %param.13) | copy-start | bytes 786436
  7.2 79.8 %all-gather.4.cloned.1.call-start = ((), (), s32[]{:S(2)}) async-start(), calls=%async_computation.2 | async-start | bytes 1179648 | tf_op jit(solution)/shard_map/all_gather | solution.py:42
  7.2 0.7 copy-start.10
  7.3 1.3 copy-start.9
  7.3 1.3 copy-start.8
  9.9 7.3 %collective-permute-start = (f32[16,512]{1,0:T(8,128)S(1)}, f32[16,512]{1,0:T(8,128)S(1)}, u32[]{:S(2)}, u32[]{:S(2)}) collective-permute-start(f32[16,512]{1,0:T(8,128)S(1)} %pad_maximum_fusion.2), channel_id=1, source_target_pairs={{0,0},{1,256},{2,512},{3,768},{4,32},{5,288},{6,544},{7,800},{8,64... | collective-permute-start | bytes 98312 | tf_op jit(solution)/shard_map/ppermute | solution.py:40
  86.9 9.5 %copy-start.1 = (f32[512,512]{1,0:T(8,128)S(1)}, f32[512,512]{1,0:T(8,128)}, u32[]{:S(2)}) copy-start(f32[512,512]{1,0:T(8,128)} %all-gather.4.cloned.1.call-done) | copy-start | bytes 3145732
  88.9 9.1 %collective-permute-start.1 = (f32[256,512]{1,0:T(8,128)S(1)}, f32[256,512]{1,0:T(8,128)S(1)}, u32[]{:S(2)}, u32[]{:S(2)}) collective-permute-start(f32[256,512]{1,0:T(8,128)S(1)} %fusion.25), channel_id=1, source_target_pairs={{0,1},{1,0},{2,3},{3,2},{4,5},{5,4},{6,7},{7,6},{8,9},{9,8},{10,11... | collective-permute-start | bytes 1572872 | tf_op jit(solution)/shard_map/ppermute | solution.py:47
  98.8 24.2 %all-to-all-start = ((f32[8,32,512]{2,1,0:T(8,128)}), f32[8,32,512]{2,1,0:T(8,128)S(1)}, u32[]{:S(2)}, u32[]{:S(2)}) async-start(f32[8,32,512]{2,1,0:T(8,128)} %bitcast.5), calls=%async_computation | async-start | bytes 1048576 | tf_op jit(solution)/shard_map/all_to_all | solution.py:49
  123.1 9.8 %collective-permute-start.2 = (f32[16,512]{1,0:T(8,128)S(1)}, f32[16,512]{1,0:T(8,128)S(1)}, u32[]{:S(2)}, u32[]{:S(2)}) collective-permute-start(f32[16,512]{1,0:T(8,128)S(1)} %dynamic-slice_bitcast_fusion), channel_id=1, source_target_pairs={{0,2},{2,0},{1,3},{3,1},{4,6},{6,4},{5,7},{7,5},{8,10},{10,8},{9,1... | collective-permute-start | bytes 98312 | tf_op jit(solution)/shard_map/ppermute | solution.py:51
  132.9 5.0 %copy-start.4 = (f32[16,256]{1,0:T(8,128)}, f32[16,256]{1,0:T(8,128)S(1)}, u32[]{:S(2)}) copy-start(f32[16,256]{1,0:T(8,128)S(1)} %slice.28) | copy-start | bytes 49156
  133.6 3.7 %copy-start.7 = (f32[16,256]{1,0:T(8,128)}, f32[16,256]{1,0:T(8,128)S(1)}, u32[]{:S(2)}) copy-start(f32[16,256]{1,0:T(8,128)S(1)} %slice_subtract_fusion) | copy-start | bytes 49156
  134.0 4.7 %collective-permute-start.3 = (f32[3,128,256]{2,1,0:T(8,128)S(1)}, f32[3,128,256]{2,1,0:T(8,128)S(1)}, u32[]{:S(2)}, u32[]{:S(2)}) collective-permute-start(f32[3,128,256]{2,1,0:T(8,128)S(1)} %pad_maximum_fusion), channel_id=1, source_target_pairs={{0,1},{1,0},{2,3},{3,2},{4,5},{5,4},{6,7},{7,6},{8,9},{9,8},{10,11... | collective-permute-start | bytes 1179656 | tf_op jit(solution)/shard_map/ppermute | solution.py:70
  215.3 22.6 %collective-permute-start.4 = (f32[3,128,256]{2,1,0:T(8,128)S(1)}, f32[3,128,256]{2,1,0:T(8,128)S(1)}, u32[]{:S(2)}, u32[]{:S(2)}) collective-permute-start(f32[3,128,256]{2,1,0:T(8,128)S(1)} %bitcast.67), channel_id=1, source_target_pairs={{0,1},{1,0},{2,3},{3,2},{4,5},{5,4},{6,7},{7,6},{8,9},{9,8},{10,11... | collective-permute-start | bytes 1179656 | tf_op jit(solution)/shard_map/ppermute | solution.py:78
  236.5 1.4 copy-start.5
  238.0 0.7 copy-start.2
  238.0 1.0 copy-start.6
  239.0 1.1 copy-start.3
Sparse Core Ops, SparseCore 0:
  38.3 48.5 all-gather.3

commit v2 on v1

v2 whole, which is shorter than its diff:
```python
import jax
import jax.numpy as jnp
from jax import lax
from jax.sharding import Mesh
from jax.sharding import PartitionSpec as P

ROW = (("zl", 4), ("y", 8))
COL = (("x", 8), ("zh", 2), ("core", 2))
PROW = tuple(n for n, _ in ROW)
PCOL = tuple(n for n, _ in COL)
ALL = PROW + PCOL
SWAP = [(0, 1), (1, 0)]


def mm(a, b, dims=((1,), (0,))):
    return lax.dot_general(
        a,
        b,
        (dims, ((), ())),
        precision=lax.Precision.HIGH,
        preferred_element_type=jnp.float32,
    )


def inner(a, b):
    return mm(a, b, ((0,), (0,)))


def swap(a, axis):
    return lax.ppermute(a, axis, SWAP)


def exchange(a, axes):
    return lax.all_to_all(a, axes, 0, 0, tiled=True)


def gather(a, axes):
    return exchange(jnp.broadcast_to(a[None], (lax.axis_size(axes),) + a.shape), axes)


def pick(a, index):
    return lax.dynamic_index_in_dim(a, index, 0, keepdims=False)


def local(inverse_blocks, panel_one, panel_two, tile_mask, diag_one, diag_two, link_block):
    span, width = panel_one.shape
    half = width // 2
    ny, nx, n = lax.axis_size("y"), lax.axis_size("x"), lax.axis_size(PROW)
    core, zh = lax.axis_index("core"), lax.axis_index("zh")
    first = core == 0
    row = lax.axis_index(PROW)
    begin = (row * n + lax.axis_index(PCOL)) * span
    spread = lax.dynamic_slice_in_dim(tile_mask, begin // width, 1, axis=1).astype(jnp.float32)
    live_one, live_two = panel_one * spread[0], panel_two * spread[1]

    even = row % 2 == 0
    to_own = [(c * n + j, j * n + c) for c in range(n) for j in range(n)]
    to_other = [(c * n + j, j * n + (c ^ 1)) for c in range(n) for j in range(n)]
    own = lax.ppermute(jnp.where(even, live_one, live_two), ALL, to_own)
    other = lax.ppermute(jnp.where(even, live_two, live_one), ALL, to_other)
    panel = gather(jnp.stack([own, other]), PROW)
    own, other = panel[:, 0].reshape(-1, width), panel[:, 1].reshape(-1, width)

    total = mm(inverse_blocks, own) + mm(swap(inverse_blocks, "core"), other)
    total = exchange(total.reshape(nx, 4 * span, width), "x")
    total = jnp.sum(total, axis=0).reshape(2, 2 * span, width)
    column = -(swap(pick(total, 1 - zh), "zh") + pick(total, zh))
    sibling = swap(column, "core")
    live = jnp.stack([live_one, live_two])
    came = swap(live, "core")
    lower, upper = jnp.where(first, live, came), jnp.where(first, came, live)
    pair = jnp.concatenate([lower, upper], axis=1)

    col_one = jnp.where(first, column, sibling)
    col_two = jnp.where(first, sibling, column)
    column_one = pick(col_one.reshape(2, span, width), core)
    column_two = pick(col_two.reshape(2, span, width), core) - mm(column_one, link_block)

    grams = jnp.concatenate(
        [
            inner(pick(pair, core), column),
            inner(lax.dynamic_slice_in_dim(col_one, core * half, half, axis=1), pair[1]),
        ]
    )
    grams = jnp.sum(exchange(grams.reshape(nx, -1, width), "x"), axis=0)
    grams = jnp.sum(gather(grams, "y"), axis=0)
    grams = jnp.sum(gather(grams, ("zh", "zl")), axis=0)
    grams = gather(grams, "x").reshape(-1, width)
    came = swap(grams, "core")
    lower, upper = jnp.where(first, grams, came), jnp.where(first, came, grams)
    crossed = jnp.concatenate([lower[width:], upper[width:]])

    corner_one = diag_one - lower[:width]
    link_two = -(crossed + mm(corner_one, link_block))
    folded = upper[:width] - inner(crossed, link_block)
    corner_two = diag_two - folded - inner(link_block, link_two)
    return (column_one, corner_one, column_two, link_two, corner_two)


def solution(mesh):
    fine = Mesh(mesh.devices.reshape([k for _, k in ROW + COL]), ALL)
    rows = P(ALL, None)
    return jax.shard_map(
        local,
        mesh=fine,
        in_specs=(P(PROW, PCOL), rows, rows, P(), P(), P(), P()),
        out_specs=(rows, P(), rows, P(), P()),
        check_vma=False,
    )
```

time: 247 us -> 192 us (0.78)
  blocking collectives: 97.5 us -> 65.1 us
  waiting for transfers between devices: 70.3 us -> 43.8 us
  starting transfers between devices: 53.2 us -> 68.9 us
  between operations: 14.4 us -> 1.01 us
    all_gather x4 -> x0, blocking collectives: 79.9 us -> none  [the longest x1 21.3 us: local(): grams = jnp.sum(lax.all_gather(grams, ('zh', 'zl'), axis=0), axis=0)]
    all_to_all x1 -> x4, blocking collectives: 17.5 us -> 65.1 us  [exchange(): return lax.all_to_all(a, axes, 0, 0, tiled=True)]
    all_gather x1 -> x0, waiting for transfers between devices: 47.4 us -> none  [local(): panel = lax.all_gather(panel, 'y', axis=0, tiled=True)]
    all_to_all x1 -> x2, starting transfers between devices: 6.28 us -> 31.2 us  [exchange(): return lax.all_to_all(a, axes, 0, 0, tiled=True)]
    ppermute x5 -> x7, waiting for transfers between devices: 4.96 us -> 15.6 us  [the longest x1 10.7 us: local(): other = lax.ppermute(jnp.where(even, live_two, live_one), ALL, to_other)]
    all_to_all x1 -> x2, waiting for transfers between devices: 18 us -> 28.2 us  [exchange(): return lax.all_to_all(a, axes, 0, 0, tiled=True)]
    ppermute x5 -> x7, starting transfers between devices: 46.9 us -> 37.7 us  [the longest x5 31.1 us: swap(): return lax.ppermute(a, axis, SWAP)]
    dot_general x11 -> x8, matrix products: 5.68 us -> 5.25 us  [mm(): lax.dot_general(a, b, (dims, ((), ())), precision=lax.Precision.HIGH, pre...]
  transfers between devices with their start and end apart: 7 -> 9, of which waited for: 7 -> 6; matrix products, arithmetic and copies ran while one was open for 1% -> 1% of each run, Pallas kernels for 0% -> 0%
where the time goes in v2:
time: 192 us; the launch traced here: 191 us
  starting transfers between devices  68.9 us (36%)
  blocking collectives  65.1 us (34%)
  waiting for transfers between devices  43.8 us (23%)
  local copies, waits for them, and re-layouts  5.5 us (3%)
  matrix products  5.25 us (3%)
    all_to_all x4, blocking collectives, exchange(): return lax.all_to_all(a, axes, 0, 0, tiled=True)  65.1 us
    all_to_all x2, starting transfers between devices, exchange(): return lax.all_to_all(a, axes, 0, 0, tiled=True)  31.2 us
    ppermute x5, starting transfers between devices, swap(): return lax.ppermute(a, axis, SWAP)  31.1 us
    all_to_all x2, waiting for transfers between devices, exchange(): return lax.all_to_all(a, axes, 0, 0, tiled=True)  28.2 us
    ppermute x1, waiting for transfers between devices, local(): other = lax.ppermute(jnp.where(even, live_two, live_one), ALL, to_other)  10.7 us
    dot_general x8, matrix products, mm(): lax.dot_general(a, b, (dims, ((), ())), precision=lax.Precision.HIGH, pre...  5.25 us
    ppermute x5, waiting for transfers between devices, swap(): return lax.ppermute(a, axis, SWAP)  4.81 us
    ppermute x1, starting transfers between devices, local(): own = lax.ppermute(jnp.where(even, live_one, live_two), ALL, to_own)  4.71 us
  transfers between devices with their start and end apart: 9, of which 6 were waited for; matrix products, arithmetic and copies ran while one was open for 1% of the time, Pallas kernels for 0%

profile of v2, /device:TPU:1, one launch (start us, length us, event | category | flops | bytes accessed | tf_op | source)
XLA Modules:
  0.0 191.1 jit_solution(12016072626033102928)
XLA Ops:
  0.6 0.0 copy-start
  0.7 0.0 copy-start.9
  0.7 0.0 copy-start.8
  0.7 0.0 copy-start.7
  0.7 0.7 copy-done.9
  1.4 0.1 fusion.17
  1.5 0.5 fusion.22
  2.0 0.0 copy-done.8
  2.0 0.0 copy-done.7
  2.0 1.3 multiply_select_fusion.1
  3.3 4.7 %collective-permute-start = (f32[16,256]{1,0:T(8,128)S(1)}, f32[16,256]{1,0:T(8,128)S(1)}, u32[]{:S(2)}, u32[]{:S(2)}) collective-permute-start(f32[16,256]{1,0:T(8,128)S(1)} %get-tuple-element.13), channel_id=1, source_target_pairs={{0,0},{1,32},{2,64},{3,96},{4,128},{5,160},{6,192},{7,224},{8,256}... | collective-permute-start | bytes 49160 | tf_op jit(solution)/shard_map/ppermute | solution.py:59
  8.0 1.9 %collective-permute-start.1 = (f32[16,256]{1,0:T(8,128)S(1)}, f32[16,256]{1,0:T(8,128)S(1)}, u32[]{:S(2)}, u32[]{:S(2)}) collective-permute-start(f32[16,256]{1,0:T(8,128)S(1)} %get-tuple-element.14), channel_id=1, source_target_pairs={{0,1},{1,33},{2,65},{3,97},{4,129},{5,161},{6,193},{7,225},{8,257}... | collective-permute-start | bytes 49160 | tf_op jit(solution)/shard_map/ppermute | solution.py:60
  9.9 0.0 collective-permute-done
  10.0 10.7 %collective-permute-done.1 = f32[16,256]{1,0:T(8,128)S(1)} collective-permute-done((f32[16,256]{1,0:T(8,128)S(1)}, f32[16,256]{1,0:T(8,128)S(1)}, u32[]{:S(2)}, u32[]{:S(2)}) %collective-permute-start.1) | collective-permute-done | bytes 16416 | tf_op jit(solution)/shard_map/ppermute | solution.py:60
  20.7 1.1 broadcast_in_dim.8
  21.8 0.0 copy-start.1
  21.8 22.9 %all-to-all-start = ((f32[32,2,16,256]{3,2,1,0:T(8,128)}), f32[32,2,16,256]{3,2,1,0:T(8,128)S(1)}, u32[]{:S(2)}, u32[]{:S(2)}) async-start(f32[32,2,16,256]{3,2,1,0:T(8,128)} %broadcast_in_dim.8), calls=%async_computation | async-start | bytes 2097152 | tf_op jit(solution)/shard_map/all_to_all | solution.py:34
  44.7 0.0 copy-done.1
  44.7 2.8 %collective-permute-start.2 = (f32[512,512]{1,0:T(8,128)S(1)}, f32[512,512]{1,0:T(8,128)S(1)}, u32[]{:S(2)}, u32[]{:S(2)}) collective-permute-start(f32[512,512]{1,0:T(8,128)S(1)} %copy-done.1), channel_id=1, source_target_pairs={{0,1},{1,0},{2,3},{3,2},{4,5},{5,4},{6,7},{7,6},{8,9},{9,8},{10,11... | collective-permute-start | bytes 3145736 | tf_op jit(solution)/shard_map/ppermute | solution.py:30
  47.5 23.1 %all-to-all-done = f32[32,2,16,256]{3,2,1,0:T(8,128)S(1)} async-done(((f32[32,2,16,256]{3,2,1,0:T(8,128)}), f32[32,2,16,256]{3,2,1,0:T(8,128)S(1)}, u32[]{:S(2)}, u32[]{:S(2)}) %all-to-all-start) | async-done | bytes 1048608 | tf_op jit(solution)/shard_map/all_to_all | solution.py:34
  70.6 0.1 fusion.21
  70.7 1.0 fusion.23
  71.8 0.0 collective-permute-done.2
  71.8 1.0 fusion
  72.9 1.0 copy.15
  73.8 8.3 %all-to-all-start.1 = ((f32[8,64,256]{2,1,0:T(8,128)}), f32[8,64,256]{2,1,0:T(8,128)S(1)}, u32[]{:S(2)}, u32[]{:S(2)}) async-start(f32[8,64,256]{2,1,0:T(8,128)} %bitcast.7), calls=%async_computation.1 | async-start | bytes 1048576 | tf_op jit(solution)/shard_map/all_to_all | solution.py:34
  82.2 6.6 %collective-permute-start.5 = (f32[2,16,256]{2,1,0:T(8,128)S(1)}, f32[2,16,256]{2,1,0:T(8,128)S(1)}, u32[]{:S(2)}, u32[]{:S(2)}) collective-permute-start(f32[2,16,256]{2,1,0:T(8,128)S(1)} %pad_maximum_fusion.7), channel_id=1, source_target_pairs={{0,1},{1,0},{2,3},{3,2},{4,5},{5,4},{6,7},{7,6},{8,9},{9,8},{10,11... | collective-permute-start | bytes 98312 | tf_op jit(solution)/shard_map/ppermute | solution.py:30
  88.7 5.1 %all-to-all-done.1 = f32[8,64,256]{2,1,0:T(8,128)S(1)} async-done(((f32[8,64,256]{2,1,0:T(8,128)}), f32[8,64,256]{2,1,0:T(8,128)S(1)}, u32[]{:S(2)}, u32[]{:S(2)}) %all-to-all-start.1) | async-done | bytes 524320 | tf_op jit(solution)/shard_map/all_to_all | solution.py:34
  93.8 4.7 %collective-permute-start.3 = (f32[32,256]{1,0:T(8,128)S(1)}, f32[32,256]{1,0:T(8,128)S(1)}, u32[]{:S(2)}, u32[]{:S(2)}) collective-permute-start(f32[32,256]{1,0:T(8,128)S(1)} %dynamic-slice_bitcast_fusion), channel_id=1, source_target_pairs={{0,2},{2,0},{1,3},{3,1},{4,6},{6,4},{5,7},{7,5},{8,10},{10,8},{9,1... | collective-permute-start | bytes 98312 | tf_op jit(solution)/shard_map/ppermute | solution.py:30
  98.6 0.0 collective-permute-done.5
  98.6 3.8 %collective-permute-done.3 = f32[32,256]{1,0:T(8,128)S(1)} collective-permute-done((f32[32,256]{1,0:T(8,128)S(1)}, f32[32,256]{1,0:T(8,128)S(1)}, u32[]{:S(2)}, u32[]{:S(2)}) %collective-permute-start.3) | collective-permute-done | bytes 32800 | tf_op jit(solution)/shard_map/ppermute | solution.py:30
  102.4 9.9 %collective-permute-start.4 = (f32[32,256]{1,0:T(8,128)S(1)}, f32[32,256]{1,0:T(8,128)S(1)}, u32[]{:S(2)}, u32[]{:S(2)}) collective-permute-start(f32[32,256]{1,0:T(8,128)S(1)} %fusion.13), channel_id=1, source_target_pairs={{0,1},{1,0},{2,3},{3,2},{4,5},{5,4},{6,7},{7,6},{8,9},{9,8},{10,11... | collective-permute-start | bytes 98312 | tf_op jit(solution)/shard_map/ppermute | solution.py:30
  112.4 0.3 fusion.7
  112.7 0.5 collective-permute-done.4
  113.2 0.3 fusion.10
  113.5 17.6 %all_to_all.30 = f32[8,48,256]{2,1,0:T(8,128)S(1)} all-to-all(f32[8,48,256]{2,1,0:T(8,128)S(1)} %bitcast.52), channel_id=1, replica_groups=mesh['zl'=4,'y'=8,'x'=8,'zh'=2,'core'=2] {'x'}, dimensions={0} | all-to-all | bytes 786432 | tf_op jit(solution)/shard_map/all_to_all | solution.py:34
  131.1 17.3 %all_to_all.31 = f32[8,48,256]{2,1,0:T(8,128)S(1)} all-to-all(f32[8,48,256]{2,1,0:T(8,128)S(1)} %broadcast_in_dim.9), channel_id=1, replica_groups=mesh['zl'=4,'y'=8,'x'=8,'zh'=2,'core'=2] {'y'}, dimensions={0} | all-to-all | bytes 786432 | tf_op jit(solution)/shard_map/all_to_all | solution.py:34
  148.5 17.0 %all_to_all.32 = f32[8,48,256]{2,1,0:T(8,128)S(1)} all-to-all(f32[8,48,256]{2,1,0:T(8,128)S(1)} %broadcast_in_dim.10), channel_id=1, replica_groups=mesh['zl'=4,'y'=8,'x'=8,'zh'=2,'core'=2] {'zh','zl'}, dimensions={0} | all-to-all | bytes 786432 | tf_op jit(solution)/shard_map/all_to_all | solution.py:34
  165.6 13.2 %all_to_all.33 = f32[8,48,256]{2,1,0:T(8,128)S(1)} all-to-all(f32[8,48,256]{2,1,0:T(8,128)S(1)} %broadcast_in_dim.11), channel_id=1, replica_groups=mesh['zl'=4,'y'=8,'x'=8,'zh'=2,'core'=2] {'x'}, dimensions={0} | all-to-all | bytes 786432 | tf_op jit(solution)/shard_map/all_to_all | solution.py:34
  178.8 7.1 %collective-permute-start.6 = (f32[384,256]{1,0:T(8,128)S(1)}, f32[384,256]{1,0:T(8,128)S(1)}, u32[]{:S(2)}, u32[]{:S(2)}) collective-permute-start(f32[384,256]{1,0:T(8,128)S(1)} %bitcast.53), channel_id=1, source_target_pairs={{0,1},{1,0},{2,3},{3,2},{4,5},{5,4},{6,7},{7,6},{8,9},{9,8},{10,11... | collective-permute-start | bytes 1179656 | tf_op jit(solution)/shard_map/ppermute | solution.py:30
  185.9 0.0 copy-start.6
  185.9 0.0 copy-done
  185.9 0.8 bitcast_subtract_fusion
  186.8 0.0 copy-done.6
  186.8 0.5 collective-permute-done.6
  187.2 0.1 broadcast_select_fusion
  187.3 0.0 copy-start.4
  187.3 0.9 copy-done.4
  188.3 0.0 copy-start.2
  188.3 0.3 fusion.1
  188.6 0.4 copy-done.2
  189.0 0.0 copy-start.3
  189.0 0.0 copy-start.5
  189.0 0.4 convolution_bitcast_fusion
  189.4 0.3 copy-done.3
  189.7 0.3 copy-done.5
  190.0 1.1 fusion.3
  (18 shorter events, 0.3 us)
Async XLA Ops:
  0.6 185.3 %copy-start = (f32[256,256]{1,0:T(8,128)S(1)}, f32[256,256]{1,0:T(8,128)}, u32[]{:S(2)}) copy-start(f32[256,256]{1,0:T(8,128)} %param.13) | copy-start | bytes 786436
  0.7 0.7 copy-start.9
  0.7 1.3 copy-start.8
  0.7 1.3 copy-start.7
  3.3 6.6 %collective-permute-start = (f32[16,256]{1,0:T(8,128)S(1)}, f32[16,256]{1,0:T(8,128)S(1)}, u32[]{:S(2)}, u32[]{:S(2)}) collective-permute-start(f32[16,256]{1,0:T(8,128)S(1)} %get-tuple-element.13), channel_id=1, source_target_pairs={{0,0},{1,32},{2,64},{3,96},{4,128},{5,160},{6,192},{7,224},{8,256}... | collective-permute-start | bytes 49160 | tf_op jit(solution)/shard_map/ppermute | solution.py:59
  8.0 12.7 %collective-permute-start.1 = (f32[16,256]{1,0:T(8,128)S(1)}, f32[16,256]{1,0:T(8,128)S(1)}, u32[]{:S(2)}, u32[]{:S(2)}) collective-permute-start(f32[16,256]{1,0:T(8,128)S(1)} %get-tuple-element.14), channel_id=1, source_target_pairs={{0,1},{1,33},{2,65},{3,97},{4,129},{5,161},{6,193},{7,225},{8,257}... | collective-permute-start | bytes 49160 | tf_op jit(solution)/shard_map/ppermute | solution.py:60
  21.8 22.9 %copy-start.1 = (f32[512,512]{1,0:T(8,128)S(1)}, f32[512,512]{1,0:T(8,128)}, u32[]{:S(2)}) copy-start(f32[512,512]{1,0:T(8,128)} %param.7) | copy-start | bytes 3145732
  21.8 48.8 %all-to-all-start = ((f32[32,2,16,256]{3,2,1,0:T(8,128)}), f32[32,2,16,256]{3,2,1,0:T(8,128)S(1)}, u32[]{:S(2)}, u32[]{:S(2)}) async-start(f32[32,2,16,256]{3,2,1,0:T(8,128)} %broadcast_in_dim.8), calls=%async_computation | async-start | bytes 2097152 | tf_op jit(solution)/shard_map/all_to_all | solution.py:34
  44.7 27.0 %collective-permute-start.2 = (f32[512,512]{1,0:T(8,128)S(1)}, f32[512,512]{1,0:T(8,128)S(1)}, u32[]{:S(2)}, u32[]{:S(2)}) collective-permute-start(f32[512,512]{1,0:T(8,128)S(1)} %copy-done.1), channel_id=1, source_target_pairs={{0,1},{1,0},{2,3},{3,2},{4,5},{5,4},{6,7},{7,6},{8,9},{9,8},{10,11... | collective-permute-start | bytes 3145736 | tf_op jit(solution)/shard_map/ppermute | solution.py:30
  73.8 19.9 %all-to-all-start.1 = ((f32[8,64,256]{2,1,0:T(8,128)}), f32[8,64,256]{2,1,0:T(8,128)S(1)}, u32[]{:S(2)}, u32[]{:S(2)}) async-start(f32[8,64,256]{2,1,0:T(8,128)} %bitcast.7), calls=%async_computation.1 | async-start | bytes 1048576 | tf_op jit(solution)/shard_map/all_to_all | solution.py:34
  82.2 16.4 %collective-permute-start.5 = (f32[2,16,256]{2,1,0:T(8,128)S(1)}, f32[2,16,256]{2,1,0:T(8,128)S(1)}, u32[]{:S(2)}, u32[]{:S(2)}) collective-permute-start(f32[2,16,256]{2,1,0:T(8,128)S(1)} %pad_maximum_fusion.7), channel_id=1, source_target_pairs={{0,1},{1,0},{2,3},{3,2},{4,5},{5,4},{6,7},{7,6},{8,9},{9,8},{10,11... | collective-permute-start | bytes 98312 | tf_op jit(solution)/shard_map/ppermute | solution.py:30
  93.8 8.6 %collective-permute-start.3 = (f32[32,256]{1,0:T(8,128)S(1)}, f32[32,256]{1,0:T(8,128)S(1)}, u32[]{:S(2)}, u32[]{:S(2)}) collective-permute-start(f32[32,256]{1,0:T(8,128)S(1)} %dynamic-slice_bitcast_fusion), channel_id=1, source_target_pairs={{0,2},{2,0},{1,3},{3,1},{4,6},{6,4},{5,7},{7,5},{8,10},{10,8},{9,1... | collective-permute-start | bytes 98312 | tf_op jit(solution)/shard_map/ppermute | solution.py:30
  102.4 10.8 %collective-permute-start.4 = (f32[32,256]{1,0:T(8,128)S(1)}, f32[32,256]{1,0:T(8,128)S(1)}, u32[]{:S(2)}, u32[]{:S(2)}) collective-permute-start(f32[32,256]{1,0:T(8,128)S(1)} %fusion.13), channel_id=1, source_target_pairs={{0,1},{1,0},{2,3},{3,2},{4,5},{5,4},{6,7},{7,6},{8,9},{9,8},{10,11... | collective-permute-start | bytes 98312 | tf_op jit(solution)/shard_map/ppermute | solution.py:30
  178.8 8.4 %collective-permute-start.6 = (f32[384,256]{1,0:T(8,128)S(1)}, f32[384,256]{1,0:T(8,128)S(1)}, u32[]{:S(2)}, u32[]{:S(2)}) collective-permute-start(f32[384,256]{1,0:T(8,128)S(1)} %bitcast.53), channel_id=1, source_target_pairs={{0,1},{1,0},{2,3},{3,2},{4,5},{5,4},{6,7},{7,6},{8,9},{9,8},{10,11... | collective-permute-start | bytes 1179656 | tf_op jit(solution)/shard_map/ppermute | solution.py:30
  185.9 0.8 copy-start.6
  187.3 1.0 copy-start.4
  188.3 0.7 copy-start.2
  189.0 0.7 copy-start.3
  189.0 1.0 copy-start.5

commit v3 on v2

--- a/solution.py
+++ b/solution.py
@@ -61,28 +61,40 @@
     panel = gather(jnp.stack([own, other]), PROW)
     own, other = panel[:, 0].reshape(-1, width), panel[:, 1].reshape(-1, width)
 
+    live = jnp.concatenate([live_one, live_two], axis=1)
+    came = swap(live, "zh")
+    group = jnp.stack([jnp.where(zh == 0, live, came), jnp.where(zh == 0, came, live)])
+    place = lax.axis_index("x")
+    rows = lax.dynamic_update_index_in_dim(jnp.zeros((nx,) + group.shape, jnp.float32), group, place, 0)
+    for step in range(1, nx):
+        came = lax.ppermute(group, "x", [(i, i ^ step) for i in range(nx)])
+        rows = lax.dynamic_update_index_in_dim(rows, came, place ^ step, 0)
+    came = swap(rows, "core")
+    rows = jnp.stack([jnp.where(first, rows, came), jnp.where(first, came, rows)], axis=2)
+    rows = rows.reshape(-1, 2 * width)
+    rows_two = rows[:, width:]
+    rows_own = jnp.where(first, rows[:, :width], rows_two)
+
     total = mm(inverse_blocks, own) + mm(swap(inverse_blocks, "core"), other)
-    total = exchange(total.reshape(nx, 4 * span, width), "x")
-    total = jnp.sum(total, axis=0).reshape(2, 2 * span, width)
+    came = swap(total[:, half:], "core")
+    grams = jnp.concatenate(
+        [
+            inner(rows_own, total),
+            inner(jnp.where(first, total[:, :half], came), rows_two),
+        ]
+    )
+
+    parts = jnp.concatenate([total.reshape(nx, -1, width), grams.reshape(nx, -1, width)], axis=1)
+    parts = jnp.sum(exchange(parts, "x"), axis=0)
+    total, grams = parts[: 4 * span].reshape(2, 2 * span, width), parts[4 * span :]
+
     column = -(swap(pick(total, 1 - zh), "zh") + pick(total, zh))
     sibling = swap(column, "core")
-    live = jnp.stack([live_one, live_two])
-    came = swap(live, "core")
-    lower, upper = jnp.where(first, live, came), jnp.where(first, came, live)
-    pair = jnp.concatenate([lower, upper], axis=1)
-
     col_one = jnp.where(first, column, sibling)
     col_two = jnp.where(first, sibling, column)
     column_one = pick(col_one.reshape(2, span, width), core)
     column_two = pick(col_two.reshape(2, span, width), core) - mm(column_one, link_block)
 
-    grams = jnp.concatenate(
-        [
-            inner(pick(pair, core), column),
-            inner(lax.dynamic_slice_in_dim(col_one, core * half, half, axis=1), pair[1]),
-        ]
-    )
-    grams = jnp.sum(exchange(grams.reshape(nx, -1, width), "x"), axis=0)
     grams = jnp.sum(gather(grams, "y"), axis=0)
     grams = jnp.sum(gather(grams, ("zh", "zl")), axis=0)
     grams = gather(grams, "x").reshape(-1, width)
@@ -90,9 +102,9 @@
     lower, upper = jnp.where(first, grams, came), jnp.where(first, came, grams)
     crossed = jnp.concatenate([lower[width:], upper[width:]])
 
-    corner_one = diag_one - lower[:width]
-    link_two = -(crossed + mm(corner_one, link_block))
-    folded = upper[:width] - inner(crossed, link_block)
+    corner_one = diag_one + lower[:width]
+    link_two = crossed - mm(corner_one, link_block)
+    folded = inner(crossed, link_block) - upper[:width]
     corner_two = diag_two - folded - inner(link_block, link_two)
     return (column_one, corner_one, column_two, link_two, corner_two)
 

time: 192 us -> 189 us (0.984)
  waiting for transfers between devices: 43.8 us -> 11.5 us
  starting transfers between devices: 68.9 us -> 94.4 us
  matrix products: 5.25 us -> 7.99 us
    ppermute x0 -> x7, starting transfers between devices: none -> 28.8 us  [local(): came = lax.ppermute(group, 'x', [(i, i ^ step) for i in range(nx)])]
    all_to_all x2, waiting for transfers between devices: 28.2 us -> 0.01 us  [exchange(): return lax.all_to_all(a, axes, 0, 0, tiled=True)]
    all_to_all x2, starting transfers between devices: 31.2 us -> 16.4 us  [exchange(): return lax.all_to_all(a, axes, 0, 0, tiled=True)]
    ppermute x1, waiting for transfers between devices: 10.7 us -> 0.01 us  [local(): other = lax.ppermute(jnp.where(even, live_two, live_one), ALL, to_other)]
    ppermute x1, starting transfers between devices: 4.71 us -> 15.5 us  [local(): own = lax.ppermute(jnp.where(even, live_one, live_two), ALL, to_own)]
    ppermute x0 -> x7, waiting for transfers between devices: none -> 4.61 us  [local(): came = lax.ppermute(group, 'x', [(i, i ^ step) for i in range(nx)])]
    dot_general x8, matrix products: 5.25 us -> 7.99 us  [mm(): lax.dot_general(a, b, (dims, ((), ())), precision=lax.Precision.HIGH, pre...]
    ppermute x1, starting transfers between devices: 1.92 us -> 4.15 us  [local(): other = lax.ppermute(jnp.where(even, live_two, live_one), ALL, to_other)]
  transfers between devices with their start and end apart: 9 -> 18, of which waited for: 6 -> 6; matrix products, arithmetic and copies ran while one was open for 1% -> 3% of each run, Pallas kernels for 0% -> 0%
where the time goes in v3:
time: 189 us; the launch traced here: 188 us
  starting transfers between devices  94.4 us (50%)
  blocking collectives  64.9 us (34%)
  waiting for transfers between devices  11.5 us (6%)
  matrix products  7.99 us (4%)
  local copies, waits for them, and re-layouts  5.65 us (3%)
  other arithmetic  1.97 us (1%)
    all_to_all x3, blocking collectives, exchange(): return lax.all_to_all(a, axes, 0, 0, tiled=True)  64.9 us
    ppermute x7, starting transfers between devices, swap(): return lax.ppermute(a, axis, SWAP)  29.5 us
    ppermute x7, starting transfers between devices, local(): came = lax.ppermute(group, 'x', [(i, i ^ step) for i in range(nx)])  28.8 us
    all_to_all x2, starting transfers between devices, exchange(): return lax.all_to_all(a, axes, 0, 0, tiled=True)  16.4 us
    ppermute x1, starting transfers between devices, local(): own = lax.ppermute(jnp.where(even, live_one, live_two), ALL, to_own)  15.5 us
    dot_general x8, matrix products, mm(): lax.dot_general(a, b, (dims, ((), ())), precision=lax.Precision.HIGH, pre...  7.99 us
    ppermute x7, waiting for transfers between devices, swap(): return lax.ppermute(a, axis, SWAP)  6.88 us
    ppermute x7, waiting for transfers between devices, local(): came = lax.ppermute(group, 'x', [(i, i ^ step) for i in range(nx)])  4.61 us
  transfers between devices with their start and end apart: 18, of which 6 were waited for; matrix products, arithmetic and copies ran while one was open for 3% of the time, Pallas kernels for 0%

profile of v3, /device:TPU:1, one launch (start us, length us, event | category | flops | bytes accessed | tf_op | source)
XLA Modules:
  0.0 187.7 jit_solution(17367851739038239246)
XLA Ops:
  0.6 0.0 copy-start
  0.7 0.7 copy-done.8
  1.4 0.1 fusion.9
  1.5 0.5 fusion.12
  2.0 1.3 broadcast_select_fusion.5
  3.3 4.1 %collective-permute-start.1 = (f32[16,256]{1,0:T(8,128)S(1)}, f32[16,256]{1,0:T(8,128)S(1)}, u32[]{:S(2)}, u32[]{:S(2)}) collective-permute-start(f32[16,256]{1,0:T(8,128)S(1)} %broadcast_select_fusion.4), channel_id=1, source_target_pairs={{0,1},{1,33},{2,65},{3,97},{4,129},{5,161},{6,193},{7,225},{8,257}... | collective-permute-start | bytes 49160 | tf_op jit(solution)/shard_map/ppermute | solution.py:60
  7.5 15.5 %collective-permute-start = (f32[16,256]{1,0:T(8,128)S(1)}, f32[16,256]{1,0:T(8,128)S(1)}, u32[]{:S(2)}, u32[]{:S(2)}) collective-permute-start(f32[16,256]{1,0:T(8,128)S(1)} %get-tuple-element.5), channel_id=1, source_target_pairs={{0,0},{1,32},{2,64},{3,96},{4,128},{5,160},{6,192},{7,224},{8,256}... | collective-permute-start | bytes 49160 | tf_op jit(solution)/shard_map/ppermute | solution.py:59
  22.9 8.2 %collective-permute-start.3 = (f32[16,512]{1,0:T(8,128)S(1)}, f32[16,512]{1,0:T(8,128)S(1)}, u32[]{:S(2)}, u32[]{:S(2)}) collective-permute-start(f32[16,512]{1,0:T(8,128)S(1)} %pad_maximum_fusion.7), channel_id=1, source_target_pairs={{0,2},{2,0},{1,3},{3,1},{4,6},{6,4},{5,7},{7,5},{8,10},{10,8},{9,1... | collective-permute-start | bytes 98312 | tf_op jit(solution)/shard_map/ppermute | solution.py:30
  31.3 1.1 broadcast_in_dim.52
  32.4 13.0 %all-to-all-start = ((f32[32,2,16,256]{3,2,1,0:T(8,128)}), f32[32,2,16,256]{3,2,1,0:T(8,128)S(1)}, u32[]{:S(2)}, u32[]{:S(2)}) async-start(f32[32,2,16,256]{3,2,1,0:T(8,128)} %broadcast_in_dim.52), calls=%async_computation | async-start | bytes 2097152 | tf_op jit(solution)/shard_map/all_to_all | solution.py:34
  45.4 0.0 collective-permute-done.3
  45.4 4.5 %collective-permute-start.4 = (f32[2,16,512]{2,1,0:T(8,128)S(1)}, f32[2,16,512]{2,1,0:T(8,128)S(1)}, u32[]{:S(2)}, u32[]{:S(2)}) collective-permute-start(f32[2,16,512]{2,1,0:T(8,128)S(1)} %pad_maximum_fusion.5), channel_id=1, source_target_pairs={{0,4},{4,0},{8,12},{12,8},{16,20},{20,16},{24,28},{28,24},{1,5},{5... | collective-permute-start | bytes 196616 | tf_op jit(solution)/shard_map/ppermute | solution.py:70
  50.0 5.8 %collective-permute-start.5 = (f32[2,16,512]{2,1,0:T(8,128)S(1)}, f32[2,16,512]{2,1,0:T(8,128)S(1)}, u32[]{:S(2)}, u32[]{:S(2)}) collective-permute-start(f32[2,16,512]{2,1,0:T(8,128)S(1)} %pad_maximum_fusion.5), channel_id=1, source_target_pairs={{0,8},{4,12},{8,0},{12,4},{16,24},{20,28},{24,16},{28,20},{1,9},{5... | collective-permute-start | bytes 196616 | tf_op jit(solution)/shard_map/ppermute | solution.py:70
  55.8 1.9 %collective-permute-start.6 = (f32[2,16,512]{2,1,0:T(8,128)S(1)}, f32[2,16,512]{2,1,0:T(8,128)S(1)}, u32[]{:S(2)}, u32[]{:S(2)}) collective-permute-start(f32[2,16,512]{2,1,0:T(8,128)S(1)} %pad_maximum_fusion.5), channel_id=1, source_target_pairs={{0,12},{4,8},{8,4},{12,0},{16,28},{20,24},{24,20},{28,16},{1,13},{... | collective-permute-start | bytes 196616 | tf_op jit(solution)/shard_map/ppermute | solution.py:70
  57.7 5.5 %collective-permute-start.7 = (f32[2,16,512]{2,1,0:T(8,128)S(1)}, f32[2,16,512]{2,1,0:T(8,128)S(1)}, u32[]{:S(2)}, u32[]{:S(2)}) collective-permute-start(f32[2,16,512]{2,1,0:T(8,128)S(1)} %pad_maximum_fusion.5), channel_id=1, source_target_pairs={{0,16},{4,20},{8,24},{12,28},{16,0},{20,4},{24,8},{28,12},{1,17},{... | collective-permute-start | bytes 196616 | tf_op jit(solution)/shard_map/ppermute | solution.py:70
  63.2 2.8 %collective-permute-start.8 = (f32[2,16,512]{2,1,0:T(8,128)S(1)}, f32[2,16,512]{2,1,0:T(8,128)S(1)}, u32[]{:S(2)}, u32[]{:S(2)}) collective-permute-start(f32[2,16,512]{2,1,0:T(8,128)S(1)} %pad_maximum_fusion.5), channel_id=1, source_target_pairs={{0,20},{4,16},{8,28},{12,24},{16,4},{20,0},{24,12},{28,8},{1,21},{... | collective-permute-start | bytes 196616 | tf_op jit(solution)/shard_map/ppermute | solution.py:70
  66.0 0.1 broadcast_in_dim.53
  66.1 0.0 collective-permute-done.4
  66.1 6.4 %collective-permute-start.9 = (f32[2,16,512]{2,1,0:T(8,128)S(1)}, f32[2,16,512]{2,1,0:T(8,128)S(1)}, u32[]{:S(2)}, u32[]{:S(2)}) collective-permute-start(f32[2,16,512]{2,1,0:T(8,128)S(1)} %pad_maximum_fusion.5), channel_id=1, source_target_pairs={{0,24},{4,28},{8,16},{12,20},{16,8},{20,12},{24,0},{28,4},{1,25},{... | collective-permute-start | bytes 196616 | tf_op jit(solution)/shard_map/ppermute | solution.py:70
  72.5 0.0 collective-permute-done.5
  72.5 1.9 %collective-permute-start.10 = (f32[2,16,512]{2,1,0:T(8,128)S(1)}, f32[2,16,512]{2,1,0:T(8,128)S(1)}, u32[]{:S(2)}, u32[]{:S(2)}) collective-permute-start(f32[2,16,512]{2,1,0:T(8,128)S(1)} %pad_maximum_fusion.5), channel_id=1, source_target_pairs={{0,28},{4,24},{8,20},{12,16},{16,12},{20,8},{24,4},{28,0},{1,29},{... | collective-permute-start | bytes 196616 | tf_op jit(solution)/shard_map/ppermute | solution.py:70
  74.4 0.0 collective-permute-done.6
  74.5 0.0 collective-permute-done.7
  74.5 0.0 collective-permute-done.8
  74.5 0.6 collective-permute-done.9
  75.1 4.0 %collective-permute-done.10 = f32[2,16,512]{2,1,0:T(8,128)S(1)} collective-permute-done((f32[2,16,512]{2,1,0:T(8,128)S(1)}, f32[2,16,512]{2,1,0:T(8,128)S(1)}, u32[]{:S(2)}, u32[]{:S(2)}) %collective-permute-start.10) | collective-permute-done | bytes 65568 | tf_op jit(solution)/shard_map/ppermute | solution.py:70
  79.1 4.7 %collective-permute-start.11 = (f32[8,2,16,512]{3,2,1,0:T(8,128)S(1)}, f32[8,2,16,512]{3,2,1,0:T(8,128)S(1)}, u32[]{:S(2)}, u32[]{:S(2)}) collective-permute-start(f32[8,2,16,512]{3,2,1,0:T(8,128)S(1)} %bitcast_dynamic-update-slice_fusion), channel_id=1, source_target_pairs={{0,1},{1,0},{2,3},{3,2},{4,5},{5,4},{6,7},{7,6},{8,9},{9,8},{10,11... | collective-permute-start | bytes 1572872 | tf_op jit(solution)/shard_map/ppermute | solution.py:30
  83.9 1.9 %collective-permute-start.2 = (f32[512,512]{1,0:T(8,128)}, f32[512,512]{1,0:T(8,128)}, u32[]{:S(2)}, u32[]{:S(2)}) collective-permute-start(f32[512,512]{1,0:T(8,128)} %param.7), channel_id=1, source_target_pairs={{0,1},{1,0},{2,3},{3,2},{4,5},{5,4},{6,7},{7,6},{8,9},{9,8},{10,11... | collective-permute-start | bytes 3145736 | tf_op jit(solution)/shard_map/ppermute | solution.py:30
  85.8 0.1 select_bitcast_fusion.1
  86.0 0.0 all-to-all-done
  86.0 0.1 fusion.11
  86.1 2.3 %fusion.13 = f32[256,512]{1,0:T(8,128)S(1)} fusion(f32[512,256]{1,0:T(8,128)S(1)} %bitcast.73, f32[512,512]{1,0:T(8,128)} %param.7), kind=kOutput, calls=%fused_computation.52 | convolution fusion | flops 402653184 | bytes 2097152 | tf_op jit(solution)/shard_map/dot_general | solution.py:16
  88.3 0.4 collective-permute-done.2
  88.8 2.3 %convolution_add_fusion = f32[256,512]{1,0:T(8,128)S(1)} fusion(f32[256,512]{1,0:T(8,128)S(1)} %fusion.13, f32[512,256]{1,0:T(8,128)S(1)} %bitcast.72, f32[512,512]{1,0:T(8,128)} %collective-permute-done.2), kind=kOutput, calls=%fused_computation | convolution fusion | flops 402784256 | bytes 2621440 | tf_op jit(solution)/shard_map/dot_general | solution.py:16
  91.1 2.0 %collective-permute-start.12 = (f32[512,128]{0,1:T(8,128)S(1)}, f32[512,128]{0,1:T(8,128)S(1)}, u32[]{:S(2)}, u32[]{:S(2)}) collective-permute-start(f32[512,128]{0,1:T(8,128)S(1)} %slice.61), channel_id=1, source_target_pairs={{0,1},{1,0},{2,3},{3,2},{4,5},{5,4},{6,7},{7,6},{8,9},{9,8},{10,11... | collective-permute-start | bytes 786440 | tf_op jit(solution)/shard_map/ppermute | solution.py:30
  93.1 0.1 pad_maximum_fusion
  93.2 0.2 copy.17
  93.4 0.6 fusion.2
  94.0 0.5 collective-permute-done.12
  94.5 0.3 fusion.3
  94.8 0.1 pad_maximum_fusion.1
  94.9 29.3 %all_to_all.25 = f32[8,112,256]{2,1,0:T(8,128)S(1)} all-to-all(f32[8,112,256]{2,1,0:T(8,128)S(1)} %pad_maximum_fusion.1), channel_id=1, replica_groups=mesh['zl'=4,'y'=8,'x'=8,'zh'=2,'core'=2] {'x'}, dimensions={0} | all-to-all | bytes 1835008 | tf_op jit(solution)/shard_map/all_to_all | solution.py:34
  124.2 0.1 reduce_sum.27
  124.3 20.0 %all_to_all.26 = f32[8,48,256]{2,1,0:T(8,128)S(1)} all-to-all(f32[8,48,256]{2,1,0:T(8,128)S(1)} %broadcast_in_dim.62), channel_id=1, replica_groups=mesh['zl'=4,'y'=8,'x'=8,'zh'=2,'core'=2] {'y'}, dimensions={0} | all-to-all | bytes 786432 | tf_op jit(solution)/shard_map/all_to_all | solution.py:34
  144.4 15.6 %all_to_all.27 = f32[8,48,256]{2,1,0:T(8,128)S(1)} all-to-all(f32[8,48,256]{2,1,0:T(8,128)S(1)} %broadcast_in_dim.63), channel_id=1, replica_groups=mesh['zl'=4,'y'=8,'x'=8,'zh'=2,'core'=2] {'zh','zl'}, dimensions={0} | all-to-all | bytes 786432 | tf_op jit(solution)/shard_map/all_to_all | solution.py:34
  160.0 0.8 broadcast_in_dim.64
  160.8 3.5 %all-to-all-start.4 = ((f32[8,48,256]{2,1,0:T(8,128)}), f32[8,48,256]{2,1,0:T(8,128)S(1)}, u32[]{:S(2)}, u32[]{:S(2)}) async-start(f32[8,48,256]{2,1,0:T(8,128)} %broadcast_in_dim.64), calls=%async_computation.4 | async-start | bytes 786432 | tf_op jit(solution)/shard_map/all_to_all | solution.py:34
  164.3 3.4 %collective-permute-start.13 = (f32[32,256]{1,0:T(8,128)S(1)}, f32[32,256]{1,0:T(8,128)S(1)}, u32[]{:S(2)}, u32[]{:S(2)}) collective-permute-start(f32[32,256]{1,0:T(8,128)S(1)} %dynamic-slice_bitcast_fusion), channel_id=1, source_target_pairs={{0,2},{2,0},{1,3},{3,1},{4,6},{6,4},{5,7},{7,5},{8,10},{10,8},{9,1... | collective-permute-start | bytes 98312 | tf_op jit(solution)/shard_map/ppermute | solution.py:30
  167.7 5.2 %collective-permute-done.13 = f32[32,256]{1,0:T(8,128)S(1)} collective-permute-done((f32[32,256]{1,0:T(8,128)S(1)}, f32[32,256]{1,0:T(8,128)S(1)}, u32[]{:S(2)}, u32[]{:S(2)}) %collective-permute-start.13) | collective-permute-done | bytes 32800 | tf_op jit(solution)/shard_map/ppermute | solution.py:30
  172.9 7.3 %collective-permute-start.14 = (f32[32,256]{1,0:T(8,128)S(1)}, f32[32,256]{1,0:T(8,128)S(1)}, u32[]{:S(2)}, u32[]{:S(2)}) collective-permute-start(f32[32,256]{1,0:T(8,128)S(1)} %fusion.8), channel_id=1, source_target_pairs={{0,1},{1,0},{2,3},{3,2},{4,5},{5,4},{6,7},{7,6},{8,9},{9,8},{10,11... | collective-permute-start | bytes 98312 | tf_op jit(solution)/shard_map/ppermute | solution.py:30
  180.2 1.9 %collective-permute-start.15 = (f32[384,256]{1,0:T(8,128)S(1)}, f32[384,256]{1,0:T(8,128)S(1)}, u32[]{:S(2)}, u32[]{:S(2)}) collective-permute-start(f32[384,256]{1,0:T(8,128)S(1)} %bitcast.75), channel_id=1, source_target_pairs={{0,1},{1,0},{2,3},{3,2},{4,5},{5,4},{6,7},{7,6},{8,9},{9,8},{10,11... | collective-permute-start | bytes 1179656 | tf_op jit(solution)/shard_map/ppermute | solution.py:30
  182.2 0.0 copy-start.5
  182.2 0.8 bitcast_subtract_fusion
  183.0 0.8 collective-permute-done.15
  183.8 0.1 broadcast_select_fusion
  183.9 0.0 copy-start.3
  183.9 0.9 copy-done.3
  184.8 0.0 copy-start.1
  184.9 0.3 convolution_subtract_fusion.1
  185.2 0.4 copy-done.1
  185.6 0.4 convolution_bitcast_fusion
  186.0 0.3 copy-done.2
  186.3 0.3 copy-done.4
  186.6 1.1 fusion.1
  (42 shorter events, 0.4 us)
Async XLA Ops:
  0.6 181.5 %copy-start = (f32[256,256]{1,0:T(8,128)S(1)}, f32[256,256]{1,0:T(8,128)}, u32[]{:S(2)}) copy-start(f32[256,256]{1,0:T(8,128)} %param.13) | copy-start | bytes 786436
  0.7 0.7 copy-start.8
  0.7 1.3 copy-start.7
  0.7 1.3 copy-start.6
  3.3 27.9 %collective-permute-start.1 = (f32[16,256]{1,0:T(8,128)S(1)}, f32[16,256]{1,0:T(8,128)S(1)}, u32[]{:S(2)}, u32[]{:S(2)}) collective-permute-start(f32[16,256]{1,0:T(8,128)S(1)} %broadcast_select_fusion.4), channel_id=1, source_target_pairs={{0,1},{1,33},{2,65},{3,97},{4,129},{5,161},{6,193},{7,225},{8,257}... | collective-permute-start | bytes 49160 | tf_op jit(solution)/shard_map/ppermute | solution.py:60
  7.5 23.8 %collective-permute-start = (f32[16,256]{1,0:T(8,128)S(1)}, f32[16,256]{1,0:T(8,128)S(1)}, u32[]{:S(2)}, u32[]{:S(2)}) collective-permute-start(f32[16,256]{1,0:T(8,128)S(1)} %get-tuple-element.5), channel_id=1, source_target_pairs={{0,0},{1,32},{2,64},{3,96},{4,128},{5,160},{6,192},{7,224},{8,256}... | collective-permute-start | bytes 49160 | tf_op jit(solution)/shard_map/ppermute | solution.py:59
  22.9 22.5 %collective-permute-start.3 = (f32[16,512]{1,0:T(8,128)S(1)}, f32[16,512]{1,0:T(8,128)S(1)}, u32[]{:S(2)}, u32[]{:S(2)}) collective-permute-start(f32[16,512]{1,0:T(8,128)S(1)} %pad_maximum_fusion.7), channel_id=1, source_target_pairs={{0,2},{2,0},{1,3},{3,1},{4,6},{6,4},{5,7},{7,5},{8,10},{10,8},{9,1... | collective-permute-start | bytes 98312 | tf_op jit(solution)/shard_map/ppermute | solution.py:30
  32.4 53.6 %all-to-all-start = ((f32[32,2,16,256]{3,2,1,0:T(8,128)}), f32[32,2,16,256]{3,2,1,0:T(8,128)S(1)}, u32[]{:S(2)}, u32[]{:S(2)}) async-start(f32[32,2,16,256]{3,2,1,0:T(8,128)} %broadcast_in_dim.52), calls=%async_computation | async-start | bytes 2097152 | tf_op jit(solution)/shard_map/all_to_all | solution.py:34
  45.4 20.6 %collective-permute-start.4 = (f32[2,16,512]{2,1,0:T(8,128)S(1)}, f32[2,16,512]{2,1,0:T(8,128)S(1)}, u32[]{:S(2)}, u32[]{:S(2)}) collective-permute-start(f32[2,16,512]{2,1,0:T(8,128)S(1)} %pad_maximum_fusion.5), channel_id=1, source_target_pairs={{0,4},{4,0},{8,12},{12,8},{16,20},{20,16},{24,28},{28,24},{1,5},{5... | collective-permute-start | bytes 196616 | tf_op jit(solution)/shard_map/ppermute | solution.py:70
  50.0 22.5 %collective-permute-start.5 = (f32[2,16,512]{2,1,0:T(8,128)S(1)}, f32[2,16,512]{2,1,0:T(8,128)S(1)}, u32[]{:S(2)}, u32[]{:S(2)}) collective-permute-start(f32[2,16,512]{2,1,0:T(8,128)S(1)} %pad_maximum_fusion.5), channel_id=1, source_target_pairs={{0,8},{4,12},{8,0},{12,4},{16,24},{20,28},{24,16},{28,20},{1,9},{5... | collective-permute-start | bytes 196616 | tf_op jit(solution)/shard_map/ppermute | solution.py:70
  55.8 18.7 %collective-permute-start.6 = (f32[2,16,512]{2,1,0:T(8,128)S(1)}, f32[2,16,512]{2,1,0:T(8,128)S(1)}, u32[]{:S(2)}, u32[]{:S(2)}) collective-permute-start(f32[2,16,512]{2,1,0:T(8,128)S(1)} %pad_maximum_fusion.5), channel_id=1, source_target_pairs={{0,12},{4,8},{8,4},{12,0},{16,28},{20,24},{24,20},{28,16},{1,13},{... | collective-permute-start | bytes 196616 | tf_op jit(solution)/shard_map/ppermute | solution.py:70
  57.7 16.8 %collective-permute-start.7 = (f32[2,16,512]{2,1,0:T(8,128)S(1)}, f32[2,16,512]{2,1,0:T(8,128)S(1)}, u32[]{:S(2)}, u32[]{:S(2)}) collective-permute-start(f32[2,16,512]{2,1,0:T(8,128)S(1)} %pad_maximum_fusion.5), channel_id=1, source_target_pairs={{0,16},{4,20},{8,24},{12,28},{16,0},{20,4},{24,8},{28,12},{1,17},{... | collective-permute-start | bytes 196616 | tf_op jit(solution)/shard_map/ppermute | solution.py:70
  63.2 11.3 %collective-permute-start.8 = (f32[2,16,512]{2,1,0:T(8,128)S(1)}, f32[2,16,512]{2,1,0:T(8,128)S(1)}, u32[]{:S(2)}, u32[]{:S(2)}) collective-permute-start(f32[2,16,512]{2,1,0:T(8,128)S(1)} %pad_maximum_fusion.5), channel_id=1, source_target_pairs={{0,20},{4,16},{8,28},{12,24},{16,4},{20,0},{24,12},{28,8},{1,21},{... | collective-permute-start | bytes 196616 | tf_op jit(solution)/shard_map/ppermute | solution.py:70
  66.1 9.0 %collective-permute-start.9 = (f32[2,16,512]{2,1,0:T(8,128)S(1)}, f32[2,16,512]{2,1,0:T(8,128)S(1)}, u32[]{:S(2)}, u32[]{:S(2)}) collective-permute-start(f32[2,16,512]{2,1,0:T(8,128)S(1)} %pad_maximum_fusion.5), channel_id=1, source_target_pairs={{0,24},{4,28},{8,16},{12,20},{16,8},{20,12},{24,0},{28,4},{1,25},{... | collective-permute-start | bytes 196616 | tf_op jit(solution)/shard_map/ppermute | solution.py:70
  72.5 6.7 %collective-permute-start.10 = (f32[2,16,512]{2,1,0:T(8,128)S(1)}, f32[2,16,512]{2,1,0:T(8,128)S(1)}, u32[]{:S(2)}, u32[]{:S(2)}) collective-permute-start(f32[2,16,512]{2,1,0:T(8,128)S(1)} %pad_maximum_fusion.5), channel_id=1, source_target_pairs={{0,28},{4,24},{8,20},{12,16},{16,12},{20,8},{24,4},{28,0},{1,29},{... | collective-permute-start | bytes 196616 | tf_op jit(solution)/shard_map/ppermute | solution.py:70
  79.1 6.7 %collective-permute-start.11 = (f32[8,2,16,512]{3,2,1,0:T(8,128)S(1)}, f32[8,2,16,512]{3,2,1,0:T(8,128)S(1)}, u32[]{:S(2)}, u32[]{:S(2)}) collective-permute-start(f32[8,2,16,512]{3,2,1,0:T(8,128)S(1)} %bitcast_dynamic-update-slice_fusion), channel_id=1, source_target_pairs={{0,1},{1,0},{2,3},{3,2},{4,5},{5,4},{6,7},{7,6},{8,9},{9,8},{10,11... | collective-permute-start | bytes 1572872 | tf_op jit(solution)/shard_map/ppermute | solution.py:30
  83.9 4.9 %collective-permute-start.2 = (f32[512,512]{1,0:T(8,128)}, f32[512,512]{1,0:T(8,128)}, u32[]{:S(2)}, u32[]{:S(2)}) collective-permute-start(f32[512,512]{1,0:T(8,128)} %param.7), channel_id=1, source_target_pairs={{0,1},{1,0},{2,3},{3,2},{4,5},{5,4},{6,7},{7,6},{8,9},{9,8},{10,11... | collective-permute-start | bytes 3145736 | tf_op jit(solution)/shard_map/ppermute | solution.py:30
  91.1 3.4 %collective-permute-start.12 = (f32[512,128]{0,1:T(8,128)S(1)}, f32[512,128]{0,1:T(8,128)S(1)}, u32[]{:S(2)}, u32[]{:S(2)}) collective-permute-start(f32[512,128]{0,1:T(8,128)S(1)} %slice.61), channel_id=1, source_target_pairs={{0,1},{1,0},{2,3},{3,2},{4,5},{5,4},{6,7},{7,6},{8,9},{9,8},{10,11... | collective-permute-start | bytes 786440 | tf_op jit(solution)/shard_map/ppermute | solution.py:30
  160.8 19.4 %all-to-all-start.4 = ((f32[8,48,256]{2,1,0:T(8,128)}), f32[8,48,256]{2,1,0:T(8,128)S(1)}, u32[]{:S(2)}, u32[]{:S(2)}) async-start(f32[8,48,256]{2,1,0:T(8,128)} %broadcast_in_dim.64), calls=%async_computation.4 | async-start | bytes 786432 | tf_op jit(solution)/shard_map/all_to_all | solution.py:34
  164.3 8.6 %collective-permute-start.13 = (f32[32,256]{1,0:T(8,128)S(1)}, f32[32,256]{1,0:T(8,128)S(1)}, u32[]{:S(2)}, u32[]{:S(2)}) collective-permute-start(f32[32,256]{1,0:T(8,128)S(1)} %dynamic-slice_bitcast_fusion), channel_id=1, source_target_pairs={{0,2},{2,0},{1,3},{3,1},{4,6},{6,4},{5,7},{7,5},{8,10},{10,8},{9,1... | collective-permute-start | bytes 98312 | tf_op jit(solution)/shard_map/ppermute | solution.py:30
  172.9 9.2 %collective-permute-start.14 = (f32[32,256]{1,0:T(8,128)S(1)}, f32[32,256]{1,0:T(8,128)S(1)}, u32[]{:S(2)}, u32[]{:S(2)}) collective-permute-start(f32[32,256]{1,0:T(8,128)S(1)} %fusion.8), channel_id=1, source_target_pairs={{0,1},{1,0},{2,3},{3,2},{4,5},{5,4},{6,7},{7,6},{8,9},{9,8},{10,11... | collective-permute-start | bytes 98312 | tf_op jit(solution)/shard_map/ppermute | solution.py:30
  180.2 3.6 %collective-permute-start.15 = (f32[384,256]{1,0:T(8,128)S(1)}, f32[384,256]{1,0:T(8,128)S(1)}, u32[]{:S(2)}, u32[]{:S(2)}) collective-permute-start(f32[384,256]{1,0:T(8,128)S(1)} %bitcast.75), channel_id=1, source_target_pairs={{0,1},{1,0},{2,3},{3,2},{4,5},{5,4},{6,7},{7,6},{8,9},{9,8},{10,11... | collective-permute-start | bytes 1179656 | tf_op jit(solution)/shard_map/ppermute | solution.py:30
  182.2 0.8 copy-start.5
  183.9 1.0 copy-start.3
  184.8 0.7 copy-start.1
  185.6 0.7 copy-start.2
  185.6 1.0 copy-start.4

commit v4 on v3

--- a/solution.py
+++ b/solution.py
@@ -42,6 +42,14 @@
     return lax.dynamic_index_in_dim(a, index, 0, keepdims=False)
 
 
+def both(mine, came, ahead, axis):
+    return jnp.stack([jnp.where(ahead, mine, came), jnp.where(ahead, came, mine)], axis=axis)
+
+
+def after(a, b):
+    return a + 0.0 * b[:1]
+
+
 def local(inverse_blocks, panel_one, panel_two, tile_mask, diag_one, diag_two, link_block):
     span, width = panel_one.shape
     half = width // 2
@@ -61,21 +69,23 @@
     panel = gather(jnp.stack([own, other]), PROW)
     own, other = panel[:, 0].reshape(-1, width), panel[:, 1].reshape(-1, width)
 
+    blocks = swap(inverse_blocks, "core")
     live = jnp.concatenate([live_one, live_two], axis=1)
     came = swap(live, "zh")
     group = jnp.stack([jnp.where(zh == 0, live, came), jnp.where(zh == 0, came, live)])
+    group = after(group, blocks)
     place = lax.axis_index("x")
-    rows = lax.dynamic_update_index_in_dim(jnp.zeros((nx,) + group.shape, jnp.float32), group, place, 0)
-    for step in range(1, nx):
-        came = lax.ppermute(group, "x", [(i, i ^ step) for i in range(nx)])
-        rows = lax.dynamic_update_index_in_dim(rows, came, place ^ step, 0)
-    came = swap(rows, "core")
-    rows = jnp.stack([jnp.where(first, rows, came), jnp.where(first, came, rows)], axis=2)
-    rows = rows.reshape(-1, 2 * width)
+    rows = jnp.zeros((nx // 2,) + group.shape, jnp.float32)
+    rows = lax.dynamic_update_index_in_dim(rows, group, place // 2, 0)
+    for step in range(1, nx // 2):
+        came = lax.ppermute(group, "x", [(i, i ^ (2 * step)) for i in range(nx)])
+        rows = lax.dynamic_update_index_in_dim(rows, came, (place // 2) ^ step, 0)
+    rows = both(rows, lax.ppermute(rows, "x", [(i, i ^ 1) for i in range(nx)]), place % 2 == 0, 1)
+    rows = both(rows, swap(rows, "core"), first, 3).reshape(-1, 2 * width)
     rows_two = rows[:, width:]
     rows_own = jnp.where(first, rows[:, :width], rows_two)
 
-    total = mm(inverse_blocks, own) + mm(swap(inverse_blocks, "core"), other)
+    total = mm(inverse_blocks, own) + mm(blocks, other)
     came = swap(total[:, half:], "core")
     grams = jnp.concatenate(
         [
@@ -95,8 +105,8 @@
     column_one = pick(col_one.reshape(2, span, width), core)
     column_two = pick(col_two.reshape(2, span, width), core) - mm(column_one, link_block)
 
-    grams = jnp.sum(gather(grams, "y"), axis=0)
-    grams = jnp.sum(gather(grams, ("zh", "zl")), axis=0)
+    grams = after(jnp.sum(gather(grams, "y"), axis=0), column)
+    grams = after(jnp.sum(gather(grams, ("zh", "zl")), axis=0), sibling)
     grams = gather(grams, "x").reshape(-1, width)
     came = swap(grams, "core")
     lower, upper = jnp.where(first, grams, came), jnp.where(first, came, grams)

time: 189 us -> 183 us (0.968)
  blocking collectives: 64.9 us -> 27.6 us
  waiting for transfers between devices: 11.5 us -> 37.8 us
  starting transfers between devices: 94.4 us -> 98.8 us
  local copies, waits for them, and re-layouts: 5.65 us -> 8.58 us
  matrix products: 7.99 us -> 5.54 us
    all_to_all x3 -> x1, blocking collectives: 64.9 us -> 27.6 us  [exchange(): return lax.all_to_all(a, axes, 0, 0, tiled=True)]
    all_to_all x2 -> x4, waiting for transfers between devices: 0.01 us -> 18.6 us  [exchange(): return lax.all_to_all(a, axes, 0, 0, tiled=True)]
    ppermute x7, starting transfers between devices: 29.5 us -> 46.6 us  [swap(): return lax.ppermute(a, axis, SWAP)]
    ppermute x1, starting transfers between devices: 15.5 us -> 3.54 us  [local(): own = lax.ppermute(jnp.where(even, live_one, live_two), ALL, to_own)]
    all_to_all x2 -> x4, starting transfers between devices: 16.4 us -> 27.9 us  [exchange(): return lax.all_to_all(a, axes, 0, 0, tiled=True)]
    ppermute x7 -> x4, starting transfers between devices: 28.8 us -> 18.8 us  [the longest x3 12.9 us: local(): came = lax.ppermute(group, 'x', [(i, i ^ 2 * step) for i in range(nx)])]
    ppermute x7 -> x4, waiting for transfers between devices: 4.61 us -> 11.3 us  [the longest x1 5.75 us: local(): lax.ppermute(rows, 'x', [(i, i ^ 1) for i in range(nx)])]
    dot_general x8, matrix products: 7.99 us -> 5.54 us  [mm(): lax.dot_general(a, b, (dims, ((), ())), precision=lax.Precision.HIGH, pre...]
  transfers between devices with their start and end apart: 18 -> 17, of which waited for: 6 -> 11; matrix products, arithmetic and copies ran while one was open for 3% -> 3% of each run, Pallas kernels for 0% -> 0%
where the time goes in v4:
time: 183 us; the launch traced here: 182 us
  starting transfers between devices  98.8 us (54%)
  waiting for transfers between devices  37.8 us (21%)
  blocking collectives  27.6 us (15%)
  local copies, waits for them, and re-layouts  8.58 us (5%)
  matrix products  5.54 us (3%)
  other arithmetic  2.1 us (1%)
    ppermute x7, starting transfers between devices, swap(): return lax.ppermute(a, axis, SWAP)  46.6 us
    all_to_all x4, starting transfers between devices, exchange(): return lax.all_to_all(a, axes, 0, 0, tiled=True)  27.9 us
    all_to_all x1, blocking collectives, exchange(): return lax.all_to_all(a, axes, 0, 0, tiled=True)  27.6 us
    all_to_all x4, waiting for transfers between devices, exchange(): return lax.all_to_all(a, axes, 0, 0, tiled=True)  18.6 us
    ppermute x3, starting transfers between devices, local(): came = lax.ppermute(group, 'x', [(i, i ^ 2 * step) for i in range(nx)])  12.9 us
    ppermute x7, waiting for transfers between devices, swap(): return lax.ppermute(a, axis, SWAP)  7.92 us
    ppermute x1, starting transfers between devices, local(): lax.ppermute(rows, 'x', [(i, i ^ 1) for i in range(nx)])  5.93 us
    ppermute x1, waiting for transfers between devices, local(): lax.ppermute(rows, 'x', [(i, i ^ 1) for i in range(nx)])  5.75 us
  transfers between devices with their start and end apart: 17, of which 11 were waited for; matrix products, arithmetic and copies ran while one was open for 3% of the time, Pallas kernels for 0%

profile of v4, /device:TPU:1, one launch (start us, length us, event | category | flops | bytes accessed | tf_op | source)
XLA Modules:
  0.0 181.7 jit_solution(4083288812722835917)
XLA Ops:
  0.6 0.0 copy-start
  0.6 16.2 %collective-permute-start.2 = (f32[512,512]{1,0:T(8,128)}, f32[512,512]{1,0:T(8,128)S(1)}, u32[]{:S(2)}, u32[]{:S(2)}) collective-permute-start(f32[512,512]{1,0:T(8,128)} %param.7), channel_id=1, source_target_pairs={{0,1},{1,0},{2,3},{3,2},{4,5},{5,4},{6,7},{7,6},{8,9},{9,8},{10,11... | collective-permute-start | bytes 3145736 | tf_op jit(solution)/shard_map/ppermute | solution.py:30
  16.9 0.7 copy-done.11
  17.6 0.1 fusion.14
  17.6 0.5 fusion.17
  18.2 0.2 copy-done.9
  18.4 0.0 copy-done.10
  18.4 1.3 broadcast_select_fusion.7
  19.7 1.9 %collective-permute-start.1 = (f32[16,256]{1,0:T(8,128)S(1)}, f32[16,256]{1,0:T(8,128)S(1)}, u32[]{:S(2)}, u32[]{:S(2)}) collective-permute-start(f32[16,256]{1,0:T(8,128)S(1)} %broadcast_select_fusion.6), channel_id=1, source_target_pairs={{0,1},{1,33},{2,65},{3,97},{4,129},{5,161},{6,193},{7,225},{8,257}... | collective-permute-start | bytes 49160 | tf_op jit(solution)/shard_map/ppermute | solution.py:68
  21.6 3.5 %collective-permute-start = (f32[16,256]{1,0:T(8,128)S(1)}, f32[16,256]{1,0:T(8,128)S(1)}, u32[]{:S(2)}, u32[]{:S(2)}) collective-permute-start(f32[16,256]{1,0:T(8,128)S(1)} %get-tuple-element.5), channel_id=1, source_target_pairs={{0,0},{1,32},{2,64},{3,96},{4,128},{5,160},{6,192},{7,224},{8,256}... | collective-permute-start | bytes 49160 | tf_op jit(solution)/shard_map/ppermute | solution.py:67
  25.2 8.2 %collective-permute-start.3 = (f32[16,512]{1,0:T(8,128)S(1)}, f32[16,512]{1,0:T(8,128)S(1)}, u32[]{:S(2)}, u32[]{:S(2)}) collective-permute-start(f32[16,512]{1,0:T(8,128)S(1)} %pad_maximum_fusion.7), channel_id=1, source_target_pairs={{0,2},{2,0},{1,3},{3,1},{4,6},{6,4},{5,7},{7,5},{8,10},{10,8},{9,1... | collective-permute-start | bytes 98312 | tf_op jit(solution)/shard_map/ppermute | solution.py:30
  33.5 1.1 broadcast_in_dim.39
  34.6 13.0 %all-to-all-start = ((f32[32,2,16,256]{3,2,1,0:T(8,128)}), f32[32,2,16,256]{3,2,1,0:T(8,128)S(1)}, u32[]{:S(2)}, u32[]{:S(2)}) async-start(f32[32,2,16,256]{3,2,1,0:T(8,128)} %broadcast_in_dim.39), calls=%async_computation | async-start | bytes 2097152 | tf_op jit(solution)/shard_map/all_to_all | solution.py:34
  47.7 5.8 %collective-permute-start.4 = (f32[2,16,512]{2,1,0:T(8,128)S(1)}, f32[2,16,512]{2,1,0:T(8,128)S(1)}, u32[]{:S(2)}, u32[]{:S(2)}) collective-permute-start(f32[2,16,512]{2,1,0:T(8,128)S(1)} %maximum_add_fusion.1), channel_id=1, source_target_pairs={{0,8},{4,12},{8,0},{12,4},{16,24},{20,28},{24,16},{28,20},{1,9},{5... | collective-permute-start | bytes 196616 | tf_op jit(solution)/shard_map/ppermute | solution.py:81
  53.5 4.9 %collective-permute-start.5 = (f32[2,16,512]{2,1,0:T(8,128)S(1)}, f32[2,16,512]{2,1,0:T(8,128)S(1)}, u32[]{:S(2)}, u32[]{:S(2)}) collective-permute-start(f32[2,16,512]{2,1,0:T(8,128)S(1)} %maximum_add_fusion.1), channel_id=1, source_target_pairs={{0,16},{4,20},{8,24},{12,28},{16,0},{20,4},{24,8},{28,12},{1,17},{... | collective-permute-start | bytes 196616 | tf_op jit(solution)/shard_map/ppermute | solution.py:81
  58.3 2.2 %collective-permute-start.6 = (f32[2,16,512]{2,1,0:T(8,128)S(1)}, f32[2,16,512]{2,1,0:T(8,128)S(1)}, u32[]{:S(2)}, u32[]{:S(2)}) collective-permute-start(f32[2,16,512]{2,1,0:T(8,128)S(1)} %maximum_add_fusion.1), channel_id=1, source_target_pairs={{0,24},{4,28},{8,16},{12,20},{16,8},{20,12},{24,0},{28,4},{1,25},{... | collective-permute-start | bytes 196616 | tf_op jit(solution)/shard_map/ppermute | solution.py:81
  60.7 1.7 collective-permute-done.5
  62.4 3.9 %collective-permute-done.6 = f32[2,16,512]{2,1,0:T(8,128)S(1)} collective-permute-done((f32[2,16,512]{2,1,0:T(8,128)S(1)}, f32[2,16,512]{2,1,0:T(8,128)S(1)}, u32[]{:S(2)}, u32[]{:S(2)}) %collective-permute-start.6) | collective-permute-done | bytes 65568 | tf_op jit(solution)/shard_map/ppermute | solution.py:81
  66.3 5.9 %collective-permute-start.7 = (f32[4,2,16,512]{3,2,1,0:T(8,128)S(1)}, f32[4,2,16,512]{3,2,1,0:T(8,128)S(1)}, u32[]{:S(2)}, u32[]{:S(2)}) collective-permute-start(f32[4,2,16,512]{3,2,1,0:T(8,128)S(1)} %bitcast_dynamic-update-slice_fusion), channel_id=1, source_target_pairs={{0,4},{4,0},{8,12},{12,8},{16,20},{20,16},{24,28},{28,24},{1,5},{5... | collective-permute-start | bytes 786440 | tf_op jit(solution)/shard_map/ppermute | solution.py:83
  72.2 5.8 %collective-permute-done.7 = f32[4,2,16,512]{3,2,1,0:T(8,128)S(1)} collective-permute-done((f32[4,2,16,512]{3,2,1,0:T(8,128)S(1)}, f32[4,2,16,512]{3,2,1,0:T(8,128)S(1)}, u32[]{:S(2)}, u32[]{:S(2)}) %collective-permute-start.7) | collective-permute-done | bytes 262176 | tf_op jit(solution)/shard_map/ppermute | solution.py:83
  78.1 3.4 %collective-permute-start.8 = (f32[4,2,2,16,512]{4,3,2,1,0:T(8,128)S(1)}, f32[4,2,2,16,512]{4,3,2,1,0:T(8,128)S(1)}, u32[]{:S(2)}, u32[]{:S(2)}) collective-permute-start(f32[4,2,2,16,512]{4,3,2,1,0:T(8,128)S(1)} %pad_maximum_fusion.2), channel_id=1, source_target_pairs={{0,1},{1,0},{2,3},{3,2},{4,5},{5,4},{6,7},{7,6},{8,9},{9,8},{10,11... | collective-permute-start | bytes 1572872 | tf_op jit(solution)/shard_map/ppermute | solution.py:30
  81.5 1.5 collective-permute-done.8
  83.0 0.1 select_bitcast_fusion.1
  83.1 0.0 copy-start.3
  83.1 0.1 fusion.16
  83.2 1.1 copy-done.3
  84.4 1.0 fusion.18
  85.4 0.2 copy-done.2
  85.6 1.0 convolution_add_fusion
  86.7 2.3 %collective-permute-start.9 = (f32[512,128]{0,1:T(8,128)S(1)}, f32[512,128]{0,1:T(8,128)S(1)}, u32[]{:S(2)}, u32[]{:S(2)}) collective-permute-start(f32[512,128]{0,1:T(8,128)S(1)} %slice.74), channel_id=1, source_target_pairs={{0,1},{1,0},{2,3},{3,2},{4,5},{5,4},{6,7},{7,6},{8,9},{9,8},{10,11... | collective-permute-start | bytes 786440 | tf_op jit(solution)/shard_map/ppermute | solution.py:30
  89.0 0.1 pad_maximum_fusion
  89.1 0.2 copy.18
  89.3 0.6 fusion.2
  89.9 0.2 collective-permute-done.9
  90.1 0.3 fusion.3
  90.4 0.1 pad_maximum_fusion.1
  90.5 27.6 %all_to_all.25 = f32[8,112,256]{2,1,0:T(8,128)S(1)} all-to-all(f32[8,112,256]{2,1,0:T(8,128)S(1)} %pad_maximum_fusion.1), channel_id=1, replica_groups=mesh['zl'=4,'y'=8,'x'=8,'zh'=2,'core'=2] {'x'}, dimensions={0} | all-to-all | bytes 1835008 | tf_op jit(solution)/shard_map/all_to_all | solution.py:34
  118.1 0.1 reduce_sum.27
  118.2 0.8 broadcast_in_dim.44
  119.0 6.3 %all-to-all-start.2 = ((f32[8,48,256]{2,1,0:T(8,128)}), f32[8,48,256]{2,1,0:T(8,128)S(1)}, u32[]{:S(2)}, u32[]{:S(2)}) async-start(f32[8,48,256]{2,1,0:T(8,128)} %broadcast_in_dim.44), calls=%async_computation.2 | async-start | bytes 786432 | tf_op jit(solution)/shard_map/all_to_all | solution.py:34
  125.3 3.8 %collective-permute-start.10 = (f32[32,256]{1,0:T(8,128)S(1)}, f32[32,256]{1,0:T(8,128)S(1)}, u32[]{:S(2)}, u32[]{:S(2)}) collective-permute-start(f32[32,256]{1,0:T(8,128)S(1)} %dynamic-slice_bitcast_fusion), channel_id=1, source_target_pairs={{0,2},{2,0},{1,3},{3,1},{4,6},{6,4},{5,7},{7,5},{8,10},{10,8},{9,1... | collective-permute-start | bytes 98312 | tf_op jit(solution)/shard_map/ppermute | solution.py:30
  129.1 4.9 %collective-permute-done.10 = f32[32,256]{1,0:T(8,128)S(1)} collective-permute-done((f32[32,256]{1,0:T(8,128)S(1)}, f32[32,256]{1,0:T(8,128)S(1)}, u32[]{:S(2)}, u32[]{:S(2)}) %collective-permute-start.10) | collective-permute-done | bytes 32800 | tf_op jit(solution)/shard_map/ppermute | solution.py:30
  134.0 3.5 %all-to-all-done.2 = f32[8,48,256]{2,1,0:T(8,128)S(1)} async-done(((f32[8,48,256]{2,1,0:T(8,128)}), f32[8,48,256]{2,1,0:T(8,128)S(1)}, u32[]{:S(2)}, u32[]{:S(2)}) %all-to-all-start.2) | async-done | bytes 393248 | tf_op jit(solution)/shard_map/all_to_all | solution.py:34
  137.6 0.8 broadcast_in_dim.45
  138.4 4.3 %all-to-all-start.3 = ((f32[8,48,256]{2,1,0:T(8,128)}), f32[8,48,256]{2,1,0:T(8,128)S(1)}, u32[]{:S(2)}, u32[]{:S(2)}) async-start(f32[8,48,256]{2,1,0:T(8,128)} %broadcast_in_dim.45), calls=%async_computation.3 | async-start | bytes 786432 | tf_op jit(solution)/shard_map/all_to_all | solution.py:34
  142.7 5.6 %collective-permute-start.11 = (f32[32,256]{1,0:T(8,128)S(1)}, f32[32,256]{1,0:T(8,128)S(1)}, u32[]{:S(2)}, u32[]{:S(2)}) collective-permute-start(f32[32,256]{1,0:T(8,128)S(1)} %fusion.9), channel_id=1, source_target_pairs={{0,1},{1,0},{2,3},{3,2},{4,5},{5,4},{6,7},{7,6},{8,9},{9,8},{10,11... | collective-permute-start | bytes 98312 | tf_op jit(solution)/shard_map/ppermute | solution.py:30
  148.2 0.8 collective-permute-done.11
  149.1 4.2 %all-to-all-done.3 = f32[8,48,256]{2,1,0:T(8,128)S(1)} async-done(((f32[8,48,256]{2,1,0:T(8,128)}), f32[8,48,256]{2,1,0:T(8,128)S(1)}, u32[]{:S(2)}, u32[]{:S(2)}) %all-to-all-start.3) | async-done | bytes 393248 | tf_op jit(solution)/shard_map/all_to_all | solution.py:34
  153.4 0.8 broadcast_in_dim.46
  154.2 4.3 %all-to-all-start.4 = ((f32[8,48,256]{2,1,0:T(8,128)}), f32[8,48,256]{2,1,0:T(8,128)S(1)}, u32[]{:S(2)}, u32[]{:S(2)}) async-start(f32[8,48,256]{2,1,0:T(8,128)} %broadcast_in_dim.46), calls=%async_computation.4 | async-start | bytes 786432 | tf_op jit(solution)/shard_map/all_to_all | solution.py:34
  158.5 10.8 %all-to-all-done.4 = f32[8,48,256]{2,1,0:T(8,128)S(1)} async-done(((f32[8,48,256]{2,1,0:T(8,128)}), f32[8,48,256]{2,1,0:T(8,128)S(1)}, u32[]{:S(2)}, u32[]{:S(2)}) %all-to-all-start.4) | async-done | bytes 393248 | tf_op jit(solution)/shard_map/all_to_all | solution.py:34
  169.3 7.2 %collective-permute-start.12 = (f32[384,256]{1,0:T(8,128)S(1)}, f32[384,256]{1,0:T(8,128)S(1)}, u32[]{:S(2)}, u32[]{:S(2)}) collective-permute-start(f32[384,256]{1,0:T(8,128)S(1)} %bitcast.78), channel_id=1, source_target_pairs={{0,1},{1,0},{2,3},{3,2},{4,5},{5,4},{6,7},{7,6},{8,9},{9,8},{10,11... | collective-permute-start | bytes 1179656 | tf_op jit(solution)/shard_map/ppermute | solution.py:30
  176.5 0.0 copy-start.8
  176.5 0.8 bitcast_subtract_fusion
  177.4 0.5 collective-permute-done.12
  177.8 0.1 broadcast_select_fusion
  177.9 0.9 copy-done.6
  178.9 0.0 copy-start.4
  178.9 0.3 convolution_subtract_fusion.1
  179.2 0.4 copy-done.4
  179.6 0.4 convolution_bitcast_fusion
  180.0 0.3 copy-done.5
  180.3 0.3 copy-done.7
  180.6 1.1 fusion.1
  (47 shorter events, 0.5 us)
Async XLA Ops:
  0.6 175.9 %copy-start = (f32[256,256]{1,0:T(8,128)S(1)}, f32[256,256]{1,0:T(8,128)}, u32[]{:S(2)}) copy-start(f32[256,256]{1,0:T(8,128)} %param.13) | copy-start | bytes 786436
  0.6 47.0 %collective-permute-start.2 = (f32[512,512]{1,0:T(8,128)}, f32[512,512]{1,0:T(8,128)S(1)}, u32[]{:S(2)}, u32[]{:S(2)}) collective-permute-start(f32[512,512]{1,0:T(8,128)} %param.7), channel_id=1, source_target_pairs={{0,1},{1,0},{2,3},{3,2},{4,5},{5,4},{6,7},{7,6},{8,9},{9,8},{10,11... | collective-permute-start | bytes 3145736 | tf_op jit(solution)/shard_map/ppermute | solution.py:30
  16.9 0.7 copy-start.11
  17.6 0.7 copy-start.9
  17.6 0.7 copy-start.10
  19.7 13.8 %collective-permute-start.1 = (f32[16,256]{1,0:T(8,128)S(1)}, f32[16,256]{1,0:T(8,128)S(1)}, u32[]{:S(2)}, u32[]{:S(2)}) collective-permute-start(f32[16,256]{1,0:T(8,128)S(1)} %broadcast_select_fusion.6), channel_id=1, source_target_pairs={{0,1},{1,33},{2,65},{3,97},{4,129},{5,161},{6,193},{7,225},{8,257}... | collective-permute-start | bytes 49160 | tf_op jit(solution)/shard_map/ppermute | solution.py:68
  21.6 11.8 %collective-permute-start = (f32[16,256]{1,0:T(8,128)S(1)}, f32[16,256]{1,0:T(8,128)S(1)}, u32[]{:S(2)}, u32[]{:S(2)}) collective-permute-start(f32[16,256]{1,0:T(8,128)S(1)} %get-tuple-element.5), channel_id=1, source_target_pairs={{0,0},{1,32},{2,64},{3,96},{4,128},{5,160},{6,192},{7,224},{8,256}... | collective-permute-start | bytes 49160 | tf_op jit(solution)/shard_map/ppermute | solution.py:67
  25.2 22.4 %collective-permute-start.3 = (f32[16,512]{1,0:T(8,128)S(1)}, f32[16,512]{1,0:T(8,128)S(1)}, u32[]{:S(2)}, u32[]{:S(2)}) collective-permute-start(f32[16,512]{1,0:T(8,128)S(1)} %pad_maximum_fusion.7), channel_id=1, source_target_pairs={{0,2},{2,0},{1,3},{3,1},{4,6},{6,4},{5,7},{7,5},{8,10},{10,8},{9,1... | collective-permute-start | bytes 98312 | tf_op jit(solution)/shard_map/ppermute | solution.py:30
  34.6 48.5 %all-to-all-start = ((f32[32,2,16,256]{3,2,1,0:T(8,128)}), f32[32,2,16,256]{3,2,1,0:T(8,128)S(1)}, u32[]{:S(2)}, u32[]{:S(2)}) async-start(f32[32,2,16,256]{3,2,1,0:T(8,128)} %broadcast_in_dim.39), calls=%async_computation | async-start | bytes 2097152 | tf_op jit(solution)/shard_map/all_to_all | solution.py:34
  47.6 24.6 %copy-start.1 = (f32[512,512]{1,0:T(8,128)}, f32[512,512]{1,0:T(8,128)S(1)}, u32[]{:S(2)}) copy-start(f32[512,512]{1,0:T(8,128)S(1)} %collective-permute-done.2) | copy-start | bytes 3145732
  47.7 13.0 %collective-permute-start.4 = (f32[2,16,512]{2,1,0:T(8,128)S(1)}, f32[2,16,512]{2,1,0:T(8,128)S(1)}, u32[]{:S(2)}, u32[]{:S(2)}) collective-permute-start(f32[2,16,512]{2,1,0:T(8,128)S(1)} %maximum_add_fusion.1), channel_id=1, source_target_pairs={{0,8},{4,12},{8,0},{12,4},{16,24},{20,28},{24,16},{28,20},{1,9},{5... | collective-permute-start | bytes 196616 | tf_op jit(solution)/shard_map/ppermute | solution.py:81
  53.5 8.9 %collective-permute-start.5 = (f32[2,16,512]{2,1,0:T(8,128)S(1)}, f32[2,16,512]{2,1,0:T(8,128)S(1)}, u32[]{:S(2)}, u32[]{:S(2)}) collective-permute-start(f32[2,16,512]{2,1,0:T(8,128)S(1)} %maximum_add_fusion.1), channel_id=1, source_target_pairs={{0,16},{4,20},{8,24},{12,28},{16,0},{20,4},{24,8},{28,12},{1,17},{... | collective-permute-start | bytes 196616 | tf_op jit(solution)/shard_map/ppermute | solution.py:81
  58.3 7.9 %collective-permute-start.6 = (f32[2,16,512]{2,1,0:T(8,128)S(1)}, f32[2,16,512]{2,1,0:T(8,128)S(1)}, u32[]{:S(2)}, u32[]{:S(2)}) collective-permute-start(f32[2,16,512]{2,1,0:T(8,128)S(1)} %maximum_add_fusion.1), channel_id=1, source_target_pairs={{0,24},{4,28},{8,16},{12,20},{16,8},{20,12},{24,0},{28,4},{1,25},{... | collective-permute-start | bytes 196616 | tf_op jit(solution)/shard_map/ppermute | solution.py:81
  66.3 11.7 %collective-permute-start.7 = (f32[4,2,16,512]{3,2,1,0:T(8,128)S(1)}, f32[4,2,16,512]{3,2,1,0:T(8,128)S(1)}, u32[]{:S(2)}, u32[]{:S(2)}) collective-permute-start(f32[4,2,16,512]{3,2,1,0:T(8,128)S(1)} %bitcast_dynamic-update-slice_fusion), channel_id=1, source_target_pairs={{0,4},{4,0},{8,12},{12,8},{16,20},{20,16},{24,28},{28,24},{1,5},{5... | collective-permute-start | bytes 786440 | tf_op jit(solution)/shard_map/ppermute | solution.py:83
  78.1 4.9 %collective-permute-start.8 = (f32[4,2,2,16,512]{4,3,2,1,0:T(8,128)S(1)}, f32[4,2,2,16,512]{4,3,2,1,0:T(8,128)S(1)}, u32[]{:S(2)}, u32[]{:S(2)}) collective-permute-start(f32[4,2,2,16,512]{4,3,2,1,0:T(8,128)S(1)} %pad_maximum_fusion.2), channel_id=1, source_target_pairs={{0,1},{1,0},{2,3},{3,2},{4,5},{5,4},{6,7},{7,6},{8,9},{9,8},{10,11... | collective-permute-start | bytes 1572872 | tf_op jit(solution)/shard_map/ppermute | solution.py:30
  83.1 1.2 copy-start.3
  84.4 1.2 copy-start.2
  86.7 3.4 %collective-permute-start.9 = (f32[512,128]{0,1:T(8,128)S(1)}, f32[512,128]{0,1:T(8,128)S(1)}, u32[]{:S(2)}, u32[]{:S(2)}) collective-permute-start(f32[512,128]{0,1:T(8,128)S(1)} %slice.74), channel_id=1, source_target_pairs={{0,1},{1,0},{2,3},{3,2},{4,5},{5,4},{6,7},{7,6},{8,9},{9,8},{10,11... | collective-permute-start | bytes 786440 | tf_op jit(solution)/shard_map/ppermute | solution.py:30
  119.0 18.5 %all-to-all-start.2 = ((f32[8,48,256]{2,1,0:T(8,128)}), f32[8,48,256]{2,1,0:T(8,128)S(1)}, u32[]{:S(2)}, u32[]{:S(2)}) async-start(f32[8,48,256]{2,1,0:T(8,128)} %broadcast_in_dim.44), calls=%async_computation.2 | async-start | bytes 786432 | tf_op jit(solution)/shard_map/all_to_all | solution.py:34
  125.3 8.7 %collective-permute-start.10 = (f32[32,256]{1,0:T(8,128)S(1)}, f32[32,256]{1,0:T(8,128)S(1)}, u32[]{:S(2)}, u32[]{:S(2)}) collective-permute-start(f32[32,256]{1,0:T(8,128)S(1)} %dynamic-slice_bitcast_fusion), channel_id=1, source_target_pairs={{0,2},{2,0},{1,3},{3,1},{4,6},{6,4},{5,7},{7,5},{8,10},{10,8},{9,1... | collective-permute-start | bytes 98312 | tf_op jit(solution)/shard_map/ppermute | solution.py:30
  138.4 14.9 %all-to-all-start.3 = ((f32[8,48,256]{2,1,0:T(8,128)}), f32[8,48,256]{2,1,0:T(8,128)S(1)}, u32[]{:S(2)}, u32[]{:S(2)}) async-start(f32[8,48,256]{2,1,0:T(8,128)} %broadcast_in_dim.45), calls=%async_computation.3 | async-start | bytes 786432 | tf_op jit(solution)/shard_map/all_to_all | solution.py:34
  142.7 6.4 %collective-permute-start.11 = (f32[32,256]{1,0:T(8,128)S(1)}, f32[32,256]{1,0:T(8,128)S(1)}, u32[]{:S(2)}, u32[]{:S(2)}) collective-permute-start(f32[32,256]{1,0:T(8,128)S(1)} %fusion.9), channel_id=1, source_target_pairs={{0,1},{1,0},{2,3},{3,2},{4,5},{5,4},{6,7},{7,6},{8,9},{9,8},{10,11... | collective-permute-start | bytes 98312 | tf_op jit(solution)/shard_map/ppermute | solution.py:30
  154.2 15.1 %all-to-all-start.4 = ((f32[8,48,256]{2,1,0:T(8,128)}), f32[8,48,256]{2,1,0:T(8,128)S(1)}, u32[]{:S(2)}, u32[]{:S(2)}) async-start(f32[8,48,256]{2,1,0:T(8,128)} %broadcast_in_dim.46), calls=%async_computation.4 | async-start | bytes 786432 | tf_op jit(solution)/shard_map/all_to_all | solution.py:34
  169.3 8.5 %collective-permute-start.12 = (f32[384,256]{1,0:T(8,128)S(1)}, f32[384,256]{1,0:T(8,128)S(1)}, u32[]{:S(2)}, u32[]{:S(2)}) collective-permute-start(f32[384,256]{1,0:T(8,128)S(1)} %bitcast.78), channel_id=1, source_target_pairs={{0,1},{1,0},{2,3},{3,2},{4,5},{5,4},{6,7},{7,6},{8,9},{9,8},{10,11... | collective-permute-start | bytes 1179656 | tf_op jit(solution)/shard_map/ppermute | solution.py:30
  176.5 0.8 copy-start.8
  177.9 1.0 copy-start.6
  178.9 0.7 copy-start.4
  179.6 0.7 copy-start.5
  179.6 1.0 copy-start.7

commit v5 on v4

--- a/solution.py
+++ b/solution.py
@@ -53,27 +53,32 @@
 def local(inverse_blocks, panel_one, panel_two, tile_mask, diag_one, diag_two, link_block):
     span, width = panel_one.shape
     half = width // 2
-    ny, nx, n = lax.axis_size("y"), lax.axis_size("x"), lax.axis_size(PROW)
+    nzl, ny, nx = lax.axis_size("zl"), lax.axis_size("y"), lax.axis_size("x")
+    n = nzl * ny
     core, zh = lax.axis_index("core"), lax.axis_index("zh")
     first = core == 0
-    row = lax.axis_index(PROW)
-    begin = (row * n + lax.axis_index(PCOL)) * span
-    spread = lax.dynamic_slice_in_dim(tile_mask, begin // width, 1, axis=1).astype(jnp.float32)
-    live_one, live_two = panel_one * spread[0], panel_two * spread[1]
+    row, col = lax.axis_index(PROW), lax.axis_index(PCOL)
+
+    def mask(panel, group, place):
+        tile = (group * n + place) * span // width
+        return lax.dynamic_slice(tile_mask, (panel, tile), (1, 1)).astype(jnp.float32)
 
     even = row % 2 == 0
-    to_own = [(c * n + j, j * n + c) for c in range(n) for j in range(n)]
-    to_other = [(c * n + j, j * n + (c ^ 1)) for c in range(n) for j in range(n)]
-    own = lax.ppermute(jnp.where(even, live_one, live_two), ALL, to_own)
-    other = lax.ppermute(jnp.where(even, live_two, live_one), ALL, to_other)
-    panel = gather(jnp.stack([own, other]), PROW)
+    target = [((j % nzl) * ny + j // nzl) * n for j in range(n)]
+    to_own = [(c * n + j, target[j] + c) for c in range(n) for j in range(n)]
+    to_other = [(c * n + j, target[j] + (c ^ 1)) for c in range(n) for j in range(n)]
+    own = lax.ppermute(jnp.where(even, panel_one, panel_two), ALL, to_own)
+    other = lax.ppermute(jnp.where(even, panel_two, panel_one), ALL, to_other)
+    came_from = lax.axis_index(("y", "zl"))
+    panel = jnp.stack([own * mask(core, col, came_from), other * mask(core, col ^ 1, came_from)])
+    panel = gather(gather(panel, "zl"), "y").reshape(n, 2, span, width)
     own, other = panel[:, 0].reshape(-1, width), panel[:, 1].reshape(-1, width)
 
-    blocks = swap(inverse_blocks, "core")
-    live = jnp.concatenate([live_one, live_two], axis=1)
+    live = jnp.concatenate([panel_one, panel_two], axis=1)
     came = swap(live, "zh")
     group = jnp.stack([jnp.where(zh == 0, live, came), jnp.where(zh == 0, came, live)])
-    group = after(group, blocks)
+    near = lax.optimization_barrier(after(inverse_blocks, group[0]))
+    blocks = swap(near, "core")
     place = lax.axis_index("x")
     rows = jnp.zeros((nx // 2,) + group.shape, jnp.float32)
     rows = lax.dynamic_update_index_in_dim(rows, group, place // 2, 0)
@@ -81,11 +86,15 @@
         came = lax.ppermute(group, "x", [(i, i ^ (2 * step)) for i in range(nx)])
         rows = lax.dynamic_update_index_in_dim(rows, came, (place // 2) ^ step, 0)
     rows = both(rows, lax.ppermute(rows, "x", [(i, i ^ 1) for i in range(nx)]), place % 2 == 0, 1)
-    rows = both(rows, swap(rows, "core"), first, 3).reshape(-1, 2 * width)
+    tiles = n * span // width
+    kept = lax.dynamic_slice(tile_mask, (0, row * tiles), (2, tiles)).astype(jnp.float32)
+    kept = jnp.repeat(kept.T, width, axis=1)[:, None, :]
+    rows = both(rows, swap(rows, "core"), first, 3).reshape(tiles, -1, 2 * width) * kept
+    rows = rows.reshape(-1, 2 * width)
     rows_two = rows[:, width:]
     rows_own = jnp.where(first, rows[:, :width], rows_two)
 
-    total = mm(inverse_blocks, own) + mm(blocks, other)
+    total = mm(near, own) + mm(blocks, other)
     came = swap(total[:, half:], "core")
     grams = jnp.concatenate(
         [
@@ -104,6 +113,9 @@
     col_two = jnp.where(first, sibling, column)
     column_one = pick(col_one.reshape(2, span, width), core)
     column_two = pick(col_two.reshape(2, span, width), core) - mm(column_one, link_block)
+
+    diag_one = lax.optimization_barrier(after(diag_one, column))
+    diag_two = lax.optimization_barrier(after(diag_two, column))
 
     grams = after(jnp.sum(gather(grams, "y"), axis=0), column)
     grams = after(jnp.sum(gather(grams, ("zh", "zl")), axis=0), sibling)

time: 183 us -> 189 us (1.033)
  waiting for transfers between devices: 37.8 us -> 40.5 us
    all_to_all x4 -> x5, waiting for transfers between devices: 18.6 us -> 30.7 us  [exchange(): return lax.all_to_all(a, axes, 0, 0, tiled=True)]
    ppermute x7, starting transfers between devices: 46.6 us -> 37.9 us  [swap(): return lax.ppermute(a, axis, SWAP)]
    ppermute x3, starting transfers between devices: 12.9 us -> 20.1 us  [local(): came = lax.ppermute(group, 'x', [(i, i ^ 2 * step) for i in range(nx)])]
    ppermute x3, waiting for transfers between devices: 5.56 us -> 0.01 us  [local(): came = lax.ppermute(group, 'x', [(i, i ^ 2 * step) for i in range(nx)])]
    ppermute x7, waiting for transfers between devices: 7.92 us -> 4.39 us  [swap(): return lax.ppermute(a, axis, SWAP)]
    ppermute x1, starting transfers between devices: 5.93 us -> 2.48 us  [local(): lax.ppermute(rows, 'x', [(i, i ^ 1) for i in range(nx)])]
    ppermute x2, starting transfers between devices: 5.46 us -> 8.23 us  [the longest x1 5.73 us: local(): other = lax.ppermute(jnp.where(even, panel_two, panel_one), ALL, to_other)]
    all_to_all x4 -> x5, starting transfers between devices: 27.9 us -> 29.5 us  [exchange(): return lax.all_to_all(a, axes, 0, 0, tiled=True)]
  transfers between devices with their start and end apart: 17 -> 18, of which waited for: 11 -> 9; matrix products, arithmetic and copies ran while one was open for 3% -> 4% of each run, Pallas kernels for 0% -> 0%
where the time goes in v5:
time: 189 us; the launch traced here: 187 us
  starting transfers between devices  98.2 us (52%)
  waiting for transfers between devices  40.5 us (21%)
  blocking collectives  29.2 us (15%)
  local copies, waits for them, and re-layouts  7.93 us (4%)
  matrix products  5.98 us (3%)
  other arithmetic  2.95 us (2%)
  between operations  2.64 us (1%)
    ppermute x7, starting transfers between devices, swap(): return lax.ppermute(a, axis, SWAP)  37.9 us
    all_to_all x5, waiting for transfers between devices, exchange(): return lax.all_to_all(a, axes, 0, 0, tiled=True)  30.7 us
    all_to_all x5, starting transfers between devices, exchange(): return lax.all_to_all(a, axes, 0, 0, tiled=True)  29.5 us
    all_to_all x1, blocking collectives, exchange(): return lax.all_to_all(a, axes, 0, 0, tiled=True)  29.2 us
    ppermute x3, starting transfers between devices, local(): came = lax.ppermute(group, 'x', [(i, i ^ 2 * step) for i in range(nx)])  20.1 us
    dot_general x8, matrix products, mm(): lax.dot_general(a, b, (dims, ((), ())), precision=lax.Precision.HIGH, pre...  5.98 us
    ppermute x1, starting transfers between devices, local(): other = lax.ppermute(jnp.where(even, panel_two, panel_one), ALL, to_other)  5.73 us
    ppermute x1, waiting for transfers between devices, local(): lax.ppermute(rows, 'x', [(i, i ^ 1) for i in range(nx)])  5.37 us
  transfers between devices with their start and end apart: 18, of which 9 were waited for; matrix products, arithmetic and copies ran while one was open for 4% of the time, Pallas kernels for 0%

profile of v5, /device:TPU:1, one launch (start us, length us, event | category | flops | bytes accessed | tf_op | source)
XLA Modules:
  0.0 187.4 jit_solution(628543251299971689)
XLA Ops:
  0.6 0.0 copy-start
  0.7 0.7 copy-done.7
  1.4 0.7 copy-done.9
  2.1 5.7 %collective-permute-start.2 = (f32[16,256]{1,0:T(8,128)S(1)}, f32[16,256]{1,0:T(8,128)S(1)}, u32[]{:S(2)}, u32[]{:S(2)}) collective-permute-start(f32[16,256]{1,0:T(8,128)S(1)} %get-tuple-element.18), channel_id=1, source_target_pairs={{0,1},{1,257},{2,513},{3,769},{4,33},{5,289},{6,545},{7,801},{8,65... | collective-permute-start | bytes 49160 | tf_op jit(solution)/shard_map/ppermute | solution.py:71
  7.9 2.5 %collective-permute-start.1 = (f32[16,256]{1,0:T(8,128)S(1)}, f32[16,256]{1,0:T(8,128)S(1)}, u32[]{:S(2)}, u32[]{:S(2)}) collective-permute-start(f32[16,256]{1,0:T(8,128)S(1)} %get-tuple-element.17), channel_id=1, source_target_pairs={{0,0},{1,256},{2,512},{3,768},{4,32},{5,288},{6,544},{7,800},{8,64... | collective-permute-start | bytes 49160 | tf_op jit(solution)/shard_map/ppermute | solution.py:70
  10.4 10.7 %collective-permute-start = (f32[16,512]{1,0:T(8,128)S(1)}, f32[16,512]{1,0:T(8,128)S(1)}, u32[]{:S(2)}, u32[]{:S(2)}) collective-permute-start(f32[16,512]{1,0:T(8,128)S(1)} %get-tuple-element.19), channel_id=1, source_target_pairs={{0,2},{2,0},{1,3},{3,1},{4,6},{6,4},{5,7},{7,5},{8,10},{10,8},{9,1... | collective-permute-start | bytes 98312 | tf_op jit(solution)/shard_map/ppermute | solution.py:30
  21.2 0.0 copy-start.10
  21.2 0.7 copy-done.10
  21.9 0.6 fusion.13
  23.8 0.0 collective-permute-done.2
  23.8 0.7 broadcast_in_dim.49
  24.5 7.6 %all-to-all-start = ((f32[4,2,16,256]{3,2,1,0:T(8,128)}), f32[4,2,16,256]{3,2,1,0:T(8,128)S(1)}, u32[]{:S(2)}, u32[]{:S(2)}) async-start(f32[4,2,16,256]{3,2,1,0:T(8,128)} %broadcast_in_dim.49), calls=%async_computation | async-start | bytes 262144 | tf_op jit(solution)/shard_map/all_to_all | solution.py:34
  32.1 12.9 %collective-permute-start.4 = (f32[2,16,512]{2,1,0:T(8,128)S(1)}, f32[2,16,512]{2,1,0:T(8,128)S(1)}, u32[]{:S(2)}, u32[]{:S(2)}) collective-permute-start(f32[2,16,512]{2,1,0:T(8,128)S(1)} %pad_maximum_fusion.6), channel_id=1, source_target_pairs={{0,8},{4,12},{8,0},{12,4},{16,24},{20,28},{24,16},{28,20},{1,9},{5... | collective-permute-start | bytes 196616 | tf_op jit(solution)/shard_map/ppermute | solution.py:86
  45.1 3.4 %collective-permute-start.5 = (f32[2,16,512]{2,1,0:T(8,128)S(1)}, f32[2,16,512]{2,1,0:T(8,128)S(1)}, u32[]{:S(2)}, u32[]{:S(2)}) collective-permute-start(f32[2,16,512]{2,1,0:T(8,128)S(1)} %pad_maximum_fusion.6), channel_id=1, source_target_pairs={{0,16},{4,20},{8,24},{12,28},{16,0},{20,4},{24,8},{28,12},{1,17},{... | collective-permute-start | bytes 196616 | tf_op jit(solution)/shard_map/ppermute | solution.py:86
  48.5 3.7 %collective-permute-start.6 = (f32[2,16,512]{2,1,0:T(8,128)S(1)}, f32[2,16,512]{2,1,0:T(8,128)S(1)}, u32[]{:S(2)}, u32[]{:S(2)}) collective-permute-start(f32[2,16,512]{2,1,0:T(8,128)S(1)} %pad_maximum_fusion.6), channel_id=1, source_target_pairs={{0,24},{4,28},{8,16},{12,20},{16,8},{20,12},{24,0},{28,4},{1,25},{... | collective-permute-start | bytes 196616 | tf_op jit(solution)/shard_map/ppermute | solution.py:86
  52.3 1.1 broadcast_in_dim.50
  53.4 7.2 %all-to-all-start.1 = ((f32[8,4,2,16,256]{4,3,2,1,0:T(8,128)}), f32[8,4,2,16,256]{4,3,2,1,0:T(8,128)S(1)}, u32[]{:S(2)}, u32[]{:S(2)}) async-start(f32[8,4,2,16,256]{4,3,2,1,0:T(8,128)} %broadcast_in_dim.50), calls=%async_computation.1 | async-start | bytes 2097152 | tf_op jit(solution)/shard_map/all_to_all | solution.py:34
  60.6 2.5 %collective-permute-start.7 = (f32[4,2,16,512]{3,2,1,0:T(8,128)S(1)}, f32[4,2,16,512]{3,2,1,0:T(8,128)S(1)}, u32[]{:S(2)}, u32[]{:S(2)}) collective-permute-start(f32[4,2,16,512]{3,2,1,0:T(8,128)S(1)} %bitcast_dynamic-update-slice_fusion), channel_id=1, source_target_pairs={{0,4},{4,0},{8,12},{12,8},{16,20},{20,16},{24,28},{28,24},{1,5},{5... | collective-permute-start | bytes 786440 | tf_op jit(solution)/shard_map/ppermute | solution.py:88
  63.1 0.0 copy-start.2
  63.2 5.4 %collective-permute-done.7 = f32[4,2,16,512]{3,2,1,0:T(8,128)S(1)} collective-permute-done((f32[4,2,16,512]{3,2,1,0:T(8,128)S(1)}, f32[4,2,16,512]{3,2,1,0:T(8,128)S(1)}, u32[]{:S(2)}, u32[]{:S(2)}) %collective-permute-start.7) | collective-permute-done | bytes 262176 | tf_op jit(solution)/shard_map/ppermute | solution.py:88
  68.6 4.6 %collective-permute-start.8 = (f32[4,2,2,16,512]{4,3,2,1,0:T(8,128)S(1)}, f32[4,2,2,16,512]{4,3,2,1,0:T(8,128)}, u32[]{:S(2)}, u32[]{:S(2)}) collective-permute-start(f32[4,2,2,16,512]{4,3,2,1,0:T(8,128)S(1)} %pad_maximum_fusion.2), channel_id=1, source_target_pairs={{0,1},{1,0},{2,3},{3,2},{4,5},{5,4},{6,7},{7,6},{8,9},{9,8},{10,11... | collective-permute-start | bytes 1572872 | tf_op jit(solution)/shard_map/ppermute | solution.py:30
  73.3 0.1 broadcast_add_fusion
  73.4 1.9 %collective-permute-start.3 = (f32[512,512]{1,0:T(8,128)S(1)}, f32[512,512]{1,0:T(8,128)}, u32[]{:S(2)}, u32[]{:S(2)}) collective-permute-start(f32[512,512]{1,0:T(8,128)S(1)} %broadcast_add_fusion), channel_id=1, source_target_pairs={{0,1},{1,0},{2,3},{3,2},{4,5},{5,4},{6,7},{7,6},{8,9},{9,8},{10,11... | collective-permute-start | bytes 3145736 | tf_op jit(solution)/shard_map/ppermute | solution.py:30
  75.3 0.1 fusion.10
  75.4 0.1 copy.20
  75.5 0.1 broadcast_bitcast_fusion
  75.6 2.0 %select_bitcast_fusion.1 = (f32[4,2,2,1,16,512]{5,4,3,2,1,0:T(8,128)S(1)}, f32[4,2,2,1,16,512]{5,4,3,2,1,0:T(8,128)}) fusion(f32[4,2,2,16,512]{4,3,2,1,0:T(8,128)} %collective-permute-done.8, pred[]{:T(512)S(6)} %eq.16, f32[4,1,2,16,512]{4,3,2,1,0:T(8,128)S(1)} %get-tuple-element.12, f32[4,1,2,16,512]{4,3,2,1,0:T(8,128)S(1)} %get-tuple-element.11), kind=kLoop, calls=%fused_computation.13 | loop fusion | flops 393216 | bytes 2097153 | tf_op jit(solution)/shard_map/stack | solution.py:46
  77.6 12.2 %all-to-all-done.1 = f32[8,4,2,16,256]{4,3,2,1,0:T(8,128)S(1)} async-done(((f32[8,4,2,16,256]{4,3,2,1,0:T(8,128)}), f32[8,4,2,16,256]{4,3,2,1,0:T(8,128)S(1)}, u32[]{:S(2)}, u32[]{:S(2)}) %all-to-all-start.1) | async-done | bytes 1048608 | tf_op jit(solution)/shard_map/all_to_all | solution.py:34
  89.8 0.1 fusion.12
  89.9 0.6 fusion.14
  90.5 1.8 convolution_add_fusion
  92.3 2.5 %collective-permute-start.9 = (f32[512,128]{1,0:T(8,128)S(1)}, f32[512,128]{1,0:T(8,128)S(1)}, u32[]{:S(2)}, u32[]{:S(2)}) collective-permute-start(f32[512,128]{1,0:T(8,128)S(1)} %slice.68), channel_id=1, source_target_pairs={{0,1},{1,0},{2,3},{3,2},{4,5},{5,4},{6,7},{7,6},{8,9},{9,8},{10,11... | collective-permute-start | bytes 786440 | tf_op jit(solution)/shard_map/ppermute | solution.py:30
  94.9 0.1 pad_maximum_fusion
  95.0 0.2 bitcast_multiply_fusion
  95.1 0.6 fusion.2
  95.7 0.3 collective-permute-done.9
  96.0 0.4 fusion.3
  96.4 0.1 pad_maximum_fusion.1
  96.5 29.2 %all_to_all.30 = f32[8,112,256]{2,1,0:T(8,128)S(1)} all-to-all(f32[8,112,256]{2,1,0:T(8,128)S(1)} %pad_maximum_fusion.1), channel_id=1, replica_groups=mesh['zl'=4,'y'=8,'x'=8,'zh'=2,'core'=2] {'x'}, dimensions={0} | all-to-all | bytes 1835008 | tf_op jit(solution)/shard_map/all_to_all | solution.py:34
  125.7 0.1 reduce_sum.27
  125.8 0.8 broadcast_in_dim.57
  126.6 3.5 %all-to-all-start.3 = ((f32[8,48,256]{2,1,0:T(8,128)}), f32[8,48,256]{2,1,0:T(8,128)S(1)}, u32[]{:S(2)}, u32[]{:S(2)}) async-start(f32[8,48,256]{2,1,0:T(8,128)} %broadcast_in_dim.57), calls=%async_computation.3 | async-start | bytes 786432 | tf_op jit(solution)/shard_map/all_to_all | solution.py:34
  130.0 5.7 %collective-permute-start.10 = (f32[32,256]{1,0:T(8,128)S(1)}, f32[32,256]{1,0:T(8,128)S(1)}, u32[]{:S(2)}, u32[]{:S(2)}) collective-permute-start(f32[32,256]{1,0:T(8,128)S(1)} %dynamic-slice_bitcast_fusion), channel_id=1, source_target_pairs={{0,2},{2,0},{1,3},{3,1},{4,6},{6,4},{5,7},{7,5},{8,10},{10,8},{9,1... | collective-permute-start | bytes 98312 | tf_op jit(solution)/shard_map/ppermute | solution.py:30
  135.8 2.8 %collective-permute-done.10 = f32[32,256]{1,0:T(8,128)S(1)} collective-permute-done((f32[32,256]{1,0:T(8,128)S(1)}, f32[32,256]{1,0:T(8,128)S(1)}, u32[]{:S(2)}, u32[]{:S(2)}) %collective-permute-start.10) | collective-permute-done | bytes 32800 | tf_op jit(solution)/shard_map/ppermute | solution.py:30
  138.6 3.6 %all-to-all-done.3 = f32[8,48,256]{2,1,0:T(8,128)S(1)} async-done(((f32[8,48,256]{2,1,0:T(8,128)}), f32[8,48,256]{2,1,0:T(8,128)S(1)}, u32[]{:S(2)}, u32[]{:S(2)}) %all-to-all-start.3) | async-done | bytes 393248 | tf_op jit(solution)/shard_map/all_to_all | solution.py:34
  142.3 0.8 broadcast_in_dim.58
  143.1 5.5 %all-to-all-start.4 = ((f32[8,48,256]{2,1,0:T(8,128)}), f32[8,48,256]{2,1,0:T(8,128)S(1)}, u32[]{:S(2)}, u32[]{:S(2)}) async-start(f32[8,48,256]{2,1,0:T(8,128)} %broadcast_in_dim.58), calls=%async_computation.4 | async-start | bytes 786432 | tf_op jit(solution)/shard_map/all_to_all | solution.py:34
  148.6 5.5 %collective-permute-start.11 = (f32[32,256]{1,0:T(8,128)S(1)}, f32[32,256]{1,0:T(8,128)S(1)}, u32[]{:S(2)}, u32[]{:S(2)}) collective-permute-start(f32[32,256]{1,0:T(8,128)S(1)} %fusion.8), channel_id=1, source_target_pairs={{0,1},{1,0},{2,3},{3,2},{4,5},{5,4},{6,7},{7,6},{8,9},{9,8},{10,11... | collective-permute-start | bytes 98312 | tf_op jit(solution)/shard_map/ppermute | solution.py:30
  154.1 0.8 collective-permute-done.11
  154.9 4.3 %all-to-all-done.4 = f32[8,48,256]{2,1,0:T(8,128)S(1)} async-done(((f32[8,48,256]{2,1,0:T(8,128)}), f32[8,48,256]{2,1,0:T(8,128)S(1)}, u32[]{:S(2)}, u32[]{:S(2)}) %all-to-all-start.4) | async-done | bytes 393248 | tf_op jit(solution)/shard_map/all_to_all | solution.py:34
  159.3 0.8 broadcast_in_dim.59
  160.1 5.8 %all-to-all-start.5 = ((f32[8,48,256]{2,1,0:T(8,128)}), f32[8,48,256]{2,1,0:T(8,128)S(1)}, u32[]{:S(2)}, u32[]{:S(2)}) async-start(f32[8,48,256]{2,1,0:T(8,128)} %broadcast_in_dim.59), calls=%async_computation.5 | async-start | bytes 786432 | tf_op jit(solution)/shard_map/all_to_all | solution.py:34
  165.9 10.6 %all-to-all-done.5 = f32[8,48,256]{2,1,0:T(8,128)S(1)} async-done(((f32[8,48,256]{2,1,0:T(8,128)}), f32[8,48,256]{2,1,0:T(8,128)S(1)}, u32[]{:S(2)}, u32[]{:S(2)}) %all-to-all-start.5) | async-done | bytes 393248 | tf_op jit(solution)/shard_map/all_to_all | solution.py:34
  176.5 6.9 %collective-permute-start.12 = (f32[384,256]{1,0:T(8,128)S(1)}, f32[384,256]{1,0:T(8,128)S(1)}, u32[]{:S(2)}, u32[]{:S(2)}) collective-permute-start(f32[384,256]{1,0:T(8,128)S(1)} %bitcast.81), channel_id=1, source_target_pairs={{0,1},{1,0},{2,3},{3,2},{4,5},{5,4},{6,7},{7,6},{8,9},{9,8},{10,11... | collective-permute-start | bytes 1179656 | tf_op jit(solution)/shard_map/ppermute | solution.py:30
  183.5 0.0 copy-start.8
  183.5 0.8 bitcast_subtract_fusion
  184.3 0.5 collective-permute-done.12
  184.8 0.1 broadcast_select_fusion
  184.9 0.0 copy-start.3
  184.9 0.3 convolution_subtract_fusion.1
  185.2 0.4 copy-done.3
  185.6 0.4 convolution_bitcast_fusion
  186.0 0.3 copy-done.4
  186.3 1.1 fusion.1
  (54 shorter events, 0.5 us)
Async XLA Ops:
  0.6 182.9 %copy-start = (f32[256,256]{1,0:T(8,128)S(1)}, f32[256,256]{1,0:T(8,128)}, u32[]{:S(2)}) copy-start(f32[256,256]{1,0:T(8,128)} %param.13) | copy-start | bytes 786436
  0.7 0.8 copy-start.7
  1.4 0.7 copy-start.9
  2.1 21.6 %collective-permute-start.2 = (f32[16,256]{1,0:T(8,128)S(1)}, f32[16,256]{1,0:T(8,128)S(1)}, u32[]{:S(2)}, u32[]{:S(2)}) collective-permute-start(f32[16,256]{1,0:T(8,128)S(1)} %get-tuple-element.18), channel_id=1, source_target_pairs={{0,1},{1,257},{2,513},{3,769},{4,33},{5,289},{6,545},{7,801},{8,65... | collective-permute-start | bytes 49160 | tf_op jit(solution)/shard_map/ppermute | solution.py:71
  7.9 15.9 %collective-permute-start.1 = (f32[16,256]{1,0:T(8,128)S(1)}, f32[16,256]{1,0:T(8,128)S(1)}, u32[]{:S(2)}, u32[]{:S(2)}) collective-permute-start(f32[16,256]{1,0:T(8,128)S(1)} %get-tuple-element.17), channel_id=1, source_target_pairs={{0,0},{1,256},{2,512},{3,768},{4,32},{5,288},{6,544},{7,800},{8,64... | collective-permute-start | bytes 49160 | tf_op jit(solution)/shard_map/ppermute | solution.py:70
  10.4 21.7 %collective-permute-start = (f32[16,512]{1,0:T(8,128)S(1)}, f32[16,512]{1,0:T(8,128)S(1)}, u32[]{:S(2)}, u32[]{:S(2)}) collective-permute-start(f32[16,512]{1,0:T(8,128)S(1)} %get-tuple-element.19), channel_id=1, source_target_pairs={{0,2},{2,0},{1,3},{3,1},{4,6},{6,4},{5,7},{7,5},{8,10},{10,8},{9,1... | collective-permute-start | bytes 98312 | tf_op jit(solution)/shard_map/ppermute | solution.py:30
  21.2 0.7 copy-start.10
  24.5 27.8 %all-to-all-start = ((f32[4,2,16,256]{3,2,1,0:T(8,128)}), f32[4,2,16,256]{3,2,1,0:T(8,128)S(1)}, u32[]{:S(2)}, u32[]{:S(2)}) async-start(f32[4,2,16,256]{3,2,1,0:T(8,128)} %broadcast_in_dim.49), calls=%async_computation | async-start | bytes 262144 | tf_op jit(solution)/shard_map/all_to_all | solution.py:34
  32.1 20.1 %collective-permute-start.4 = (f32[2,16,512]{2,1,0:T(8,128)S(1)}, f32[2,16,512]{2,1,0:T(8,128)S(1)}, u32[]{:S(2)}, u32[]{:S(2)}) collective-permute-start(f32[2,16,512]{2,1,0:T(8,128)S(1)} %pad_maximum_fusion.6), channel_id=1, source_target_pairs={{0,8},{4,12},{8,0},{12,4},{16,24},{20,28},{24,16},{28,20},{1,9},{5... | collective-permute-start | bytes 196616 | tf_op jit(solution)/shard_map/ppermute | solution.py:86
  45.1 15.5 %collective-permute-start.5 = (f32[2,16,512]{2,1,0:T(8,128)S(1)}, f32[2,16,512]{2,1,0:T(8,128)S(1)}, u32[]{:S(2)}, u32[]{:S(2)}) collective-permute-start(f32[2,16,512]{2,1,0:T(8,128)S(1)} %pad_maximum_fusion.6), channel_id=1, source_target_pairs={{0,16},{4,20},{8,24},{12,28},{16,0},{20,4},{24,8},{28,12},{1,17},{... | collective-permute-start | bytes 196616 | tf_op jit(solution)/shard_map/ppermute | solution.py:86
  48.5 12.1 %collective-permute-start.6 = (f32[2,16,512]{2,1,0:T(8,128)S(1)}, f32[2,16,512]{2,1,0:T(8,128)S(1)}, u32[]{:S(2)}, u32[]{:S(2)}) collective-permute-start(f32[2,16,512]{2,1,0:T(8,128)S(1)} %pad_maximum_fusion.6), channel_id=1, source_target_pairs={{0,24},{4,28},{8,16},{12,20},{16,8},{20,12},{24,0},{28,4},{1,25},{... | collective-permute-start | bytes 196616 | tf_op jit(solution)/shard_map/ppermute | solution.py:86
  53.4 36.4 %all-to-all-start.1 = ((f32[8,4,2,16,256]{4,3,2,1,0:T(8,128)}), f32[8,4,2,16,256]{4,3,2,1,0:T(8,128)S(1)}, u32[]{:S(2)}, u32[]{:S(2)}) async-start(f32[8,4,2,16,256]{4,3,2,1,0:T(8,128)} %broadcast_in_dim.50), calls=%async_computation.1 | async-start | bytes 2097152 | tf_op jit(solution)/shard_map/all_to_all | solution.py:34
  60.6 7.9 %collective-permute-start.7 = (f32[4,2,16,512]{3,2,1,0:T(8,128)S(1)}, f32[4,2,16,512]{3,2,1,0:T(8,128)S(1)}, u32[]{:S(2)}, u32[]{:S(2)}) collective-permute-start(f32[4,2,16,512]{3,2,1,0:T(8,128)S(1)} %bitcast_dynamic-update-slice_fusion), channel_id=1, source_target_pairs={{0,4},{4,0},{8,12},{12,8},{16,20},{20,16},{24,28},{28,24},{1,5},{5... | collective-permute-start | bytes 786440 | tf_op jit(solution)/shard_map/ppermute | solution.py:88
  63.1 10.1 %copy-start.2 = (f32[512,512]{1,0:T(8,128)S(1)}, f32[512,512]{1,0:T(8,128)}, u32[]{:S(2)}) copy-start(f32[512,512]{1,0:T(8,128)} %param.7) | copy-start | bytes 3145732
  68.6 7.0 %collective-permute-start.8 = (f32[4,2,2,16,512]{4,3,2,1,0:T(8,128)S(1)}, f32[4,2,2,16,512]{4,3,2,1,0:T(8,128)}, u32[]{:S(2)}, u32[]{:S(2)}) collective-permute-start(f32[4,2,2,16,512]{4,3,2,1,0:T(8,128)S(1)} %pad_maximum_fusion.2), channel_id=1, source_target_pairs={{0,1},{1,0},{2,3},{3,2},{4,5},{5,4},{6,7},{7,6},{8,9},{9,8},{10,11... | collective-permute-start | bytes 1572872 | tf_op jit(solution)/shard_map/ppermute | solution.py:30
  73.4 17.0 %collective-permute-start.3 = (f32[512,512]{1,0:T(8,128)S(1)}, f32[512,512]{1,0:T(8,128)}, u32[]{:S(2)}, u32[]{:S(2)}) collective-permute-start(f32[512,512]{1,0:T(8,128)S(1)} %broadcast_add_fusion), channel_id=1, source_target_pairs={{0,1},{1,0},{2,3},{3,2},{4,5},{5,4},{6,7},{7,6},{8,9},{9,8},{10,11... | collective-permute-start | bytes 3145736 | tf_op jit(solution)/shard_map/ppermute | solution.py:30
  92.3 2.6 %copy-start.1 = (f32[4,2,2,1,16,512]{5,4,3,2,1,0:T(8,128)S(1)}, f32[4,2,2,1,16,512]{5,4,3,2,1,0:T(8,128)}, u32[]{:S(2)}) copy-start(f32[4,2,2,1,16,512]{5,4,3,2,1,0:T(8,128)} %get-tuple-element.8) | copy-start | bytes 1572868
  92.3 3.7 %collective-permute-start.9 = (f32[512,128]{1,0:T(8,128)S(1)}, f32[512,128]{1,0:T(8,128)S(1)}, u32[]{:S(2)}, u32[]{:S(2)}) collective-permute-start(f32[512,128]{1,0:T(8,128)S(1)} %slice.68), channel_id=1, source_target_pairs={{0,1},{1,0},{2,3},{3,2},{4,5},{5,4},{6,7},{7,6},{8,9},{9,8},{10,11... | collective-permute-start | bytes 786440 | tf_op jit(solution)/shard_map/ppermute | solution.py:30
  126.6 15.7 %all-to-all-start.3 = ((f32[8,48,256]{2,1,0:T(8,128)}), f32[8,48,256]{2,1,0:T(8,128)S(1)}, u32[]{:S(2)}, u32[]{:S(2)}) async-start(f32[8,48,256]{2,1,0:T(8,128)} %broadcast_in_dim.57), calls=%async_computation.3 | async-start | bytes 786432 | tf_op jit(solution)/shard_map/all_to_all | solution.py:34
  130.0 8.6 %collective-permute-start.10 = (f32[32,256]{1,0:T(8,128)S(1)}, f32[32,256]{1,0:T(8,128)S(1)}, u32[]{:S(2)}, u32[]{:S(2)}) collective-permute-start(f32[32,256]{1,0:T(8,128)S(1)} %dynamic-slice_bitcast_fusion), channel_id=1, source_target_pairs={{0,2},{2,0},{1,3},{3,1},{4,6},{6,4},{5,7},{7,5},{8,10},{10,8},{9,1... | collective-permute-start | bytes 98312 | tf_op jit(solution)/shard_map/ppermute | solution.py:30
  143.1 16.2 %all-to-all-start.4 = ((f32[8,48,256]{2,1,0:T(8,128)}), f32[8,48,256]{2,1,0:T(8,128)S(1)}, u32[]{:S(2)}, u32[]{:S(2)}) async-start(f32[8,48,256]{2,1,0:T(8,128)} %broadcast_in_dim.58), calls=%async_computation.4 | async-start | bytes 786432 | tf_op jit(solution)/shard_map/all_to_all | solution.py:34
  148.6 6.3 %collective-permute-start.11 = (f32[32,256]{1,0:T(8,128)S(1)}, f32[32,256]{1,0:T(8,128)S(1)}, u32[]{:S(2)}, u32[]{:S(2)}) collective-permute-start(f32[32,256]{1,0:T(8,128)S(1)} %fusion.8), channel_id=1, source_target_pairs={{0,1},{1,0},{2,3},{3,2},{4,5},{5,4},{6,7},{7,6},{8,9},{9,8},{10,11... | collective-permute-start | bytes 98312 | tf_op jit(solution)/shard_map/ppermute | solution.py:30
  160.1 5.8 %copy-start.5 = (f32[256,256]{1,0:T(8,128)S(1)}, f32[256,256]{1,0:T(8,128)}, u32[]{:S(2)}) copy-start(f32[256,256]{1,0:T(8,128)} %param.12) | copy-start | bytes 786436
  160.1 5.8 %copy-start.6 = (f32[256,256]{1,0:T(8,128)S(1)}, f32[256,256]{1,0:T(8,128)}, u32[]{:S(2)}) copy-start(f32[256,256]{1,0:T(8,128)} %param.11) | copy-start | bytes 786436
  160.1 16.5 %all-to-all-start.5 = ((f32[8,48,256]{2,1,0:T(8,128)}), f32[8,48,256]{2,1,0:T(8,128)S(1)}, u32[]{:S(2)}, u32[]{:S(2)}) async-start(f32[8,48,256]{2,1,0:T(8,128)} %broadcast_in_dim.59), calls=%async_computation.5 | async-start | bytes 786432 | tf_op jit(solution)/shard_map/all_to_all | solution.py:34
  176.5 8.3 %collective-permute-start.12 = (f32[384,256]{1,0:T(8,128)S(1)}, f32[384,256]{1,0:T(8,128)S(1)}, u32[]{:S(2)}, u32[]{:S(2)}) collective-permute-start(f32[384,256]{1,0:T(8,128)S(1)} %bitcast.81), channel_id=1, source_target_pairs={{0,1},{1,0},{2,3},{3,2},{4,5},{5,4},{6,7},{7,6},{8,9},{9,8},{10,11... | collective-permute-start | bytes 1179656 | tf_op jit(solution)/shard_map/ppermute | solution.py:30
  183.5 0.8 copy-start.8
  184.9 0.7 copy-start.3
  185.6 0.7 copy-start.4

commit v6 on v5

--- a/solution.py
+++ b/solution.py
@@ -53,8 +53,7 @@
 def local(inverse_blocks, panel_one, panel_two, tile_mask, diag_one, diag_two, link_block):
     span, width = panel_one.shape
     half = width // 2
-    nzl, ny, nx = lax.axis_size("zl"), lax.axis_size("y"), lax.axis_size("x")
-    n = nzl * ny
+    ny, nx, n = lax.axis_size("y"), lax.axis_size("x"), lax.axis_size(PROW)
     core, zh = lax.axis_index("core"), lax.axis_index("zh")
     first = core == 0
     row, col = lax.axis_index(PROW), lax.axis_index(PCOL)
@@ -64,14 +63,12 @@
         return lax.dynamic_slice(tile_mask, (panel, tile), (1, 1)).astype(jnp.float32)
 
     even = row % 2 == 0
-    target = [((j % nzl) * ny + j // nzl) * n for j in range(n)]
-    to_own = [(c * n + j, target[j] + c) for c in range(n) for j in range(n)]
-    to_other = [(c * n + j, target[j] + (c ^ 1)) for c in range(n) for j in range(n)]
+    to_own = [(c * n + j, j * n + c) for c in range(n) for j in range(n)]
+    to_other = [(c * n + j, j * n + (c ^ 1)) for c in range(n) for j in range(n)]
     own = lax.ppermute(jnp.where(even, panel_one, panel_two), ALL, to_own)
     other = lax.ppermute(jnp.where(even, panel_two, panel_one), ALL, to_other)
-    came_from = lax.axis_index(("y", "zl"))
-    panel = jnp.stack([own * mask(core, col, came_from), other * mask(core, col ^ 1, came_from)])
-    panel = gather(gather(panel, "zl"), "y").reshape(n, 2, span, width)
+    panel = jnp.stack([own * mask(core, col, row), other * mask(core, col ^ 1, row)])
+    panel = gather(panel, PROW)
     own, other = panel[:, 0].reshape(-1, width), panel[:, 1].reshape(-1, width)
 
     live = jnp.concatenate([panel_one, panel_two], axis=1)
@@ -80,16 +77,16 @@
     near = lax.optimization_barrier(after(inverse_blocks, group[0]))
     blocks = swap(near, "core")
     place = lax.axis_index("x")
-    rows = jnp.zeros((nx // 2,) + group.shape, jnp.float32)
-    rows = lax.dynamic_update_index_in_dim(rows, group, place // 2, 0)
-    for step in range(1, nx // 2):
-        came = lax.ppermute(group, "x", [(i, i ^ (2 * step)) for i in range(nx)])
-        rows = lax.dynamic_update_index_in_dim(rows, came, (place // 2) ^ step, 0)
-    rows = both(rows, lax.ppermute(rows, "x", [(i, i ^ 1) for i in range(nx)]), place % 2 == 0, 1)
+    rows = group
+    for axis, step in enumerate((4, 2, 1)):
+        if step == 1:
+            rows = after(rows, blocks)
+        came = lax.ppermute(rows, "x", [(i, i ^ step) for i in range(nx)])
+        rows = both(rows, came, place & step == 0, axis)
     tiles = n * span // width
     kept = lax.dynamic_slice(tile_mask, (0, row * tiles), (2, tiles)).astype(jnp.float32)
     kept = jnp.repeat(kept.T, width, axis=1)[:, None, :]
-    rows = both(rows, swap(rows, "core"), first, 3).reshape(tiles, -1, 2 * width) * kept
+    rows = both(rows, swap(rows, "core"), first, 4).reshape(tiles, -1, 2 * width) * kept
     rows = rows.reshape(-1, 2 * width)
     rows_two = rows[:, width:]
     rows_own = jnp.where(first, rows[:, :width], rows_two)
@@ -103,9 +100,9 @@
         ]
     )
 
-    parts = jnp.concatenate([total.reshape(nx, -1, width), grams.reshape(nx, -1, width)], axis=1)
-    parts = jnp.sum(exchange(parts, "x"), axis=0)
-    total, grams = parts[: 4 * span].reshape(2, 2 * span, width), parts[4 * span :]
+    grams = jnp.sum(exchange(grams.reshape(ny, -1, width), "y"), axis=0)
+    total = jnp.sum(exchange(total.reshape(nx, -1, width), "x"), axis=0)
+    total = total.reshape(2, 2 * span, width)
 
     column = -(swap(pick(total, 1 - zh), "zh") + pick(total, zh))
     sibling = swap(column, "core")
@@ -117,9 +114,9 @@
     diag_one = lax.optimization_barrier(after(diag_one, column))
     diag_two = lax.optimization_barrier(after(diag_two, column))
 
-    grams = after(jnp.sum(gather(grams, "y"), axis=0), column)
+    grams = after(jnp.sum(gather(grams, "x"), axis=0), column)
     grams = after(jnp.sum(gather(grams, ("zh", "zl")), axis=0), sibling)
-    grams = gather(grams, "x").reshape(-1, width)
+    grams = gather(grams, "y").reshape(-1, width)
     came = swap(grams, "core")
     lower, upper = jnp.where(first, grams, came), jnp.where(first, came, grams)
     crossed = jnp.concatenate([lower[width:], upper[width:]])

time: 189 us -> 212 us (1.12)
  waiting for transfers between devices: 40.5 us -> 77.6 us
  blocking collectives: 29.2 us -> 18 us
  starting transfers between devices: 98.2 us -> 91 us
  matrix products: 5.98 us -> 8.77 us
    all_to_all x5, waiting for transfers between devices: 30.7 us -> 59.9 us  [exchange(): return lax.all_to_all(a, axes, 0, 0, tiled=True)]
    all_to_all x1, blocking collectives: 29.2 us -> 18 us  [exchange(): return lax.all_to_all(a, axes, 0, 0, tiled=True)]
    ppermute x4 -> x3, starting transfers between devices: 22.5 us -> 17.5 us  [local(): came = lax.ppermute(rows, 'x', [(i, i ^ step) for i in range(nx)])]
    ppermute x7, waiting for transfers between devices: 4.39 us -> 9.33 us  [swap(): return lax.ppermute(a, axis, SWAP)]
    ppermute x7, starting transfers between devices: 37.9 us -> 34.3 us  [swap(): return lax.ppermute(a, axis, SWAP)]
    all_to_all x5, starting transfers between devices: 29.5 us -> 32.8 us  [exchange(): return lax.all_to_all(a, axes, 0, 0, tiled=True)]
    ppermute x4 -> x3, waiting for transfers between devices: 5.37 us -> 8.38 us  [local(): came = lax.ppermute(rows, 'x', [(i, i ^ step) for i in range(nx)])]
    dot_general x8, matrix products: 5.98 us -> 8.77 us  [mm(): lax.dot_general(a, b, (dims, ((), ())), precision=lax.Precision.HIGH, pre...]
  transfers between devices with their start and end apart: 18 -> 17, of which waited for: 9 -> 11; matrix products, arithmetic and copies ran while one was open for 4% -> 4% of each run, Pallas kernels for 0% -> 0%
where the time goes in v6:
time: 212 us; the launch traced here: 211 us
  starting transfers between devices  91 us (43%)
  waiting for transfers between devices  77.6 us (37%)
  blocking collectives  18 us (8%)
  matrix products  8.77 us (4%)
  local copies, waits for them, and re-layouts  8.23 us (4%)
  other arithmetic  4.91 us (2%)
  between operations  2.56 us (1%)
    all_to_all x5, waiting for transfers between devices, exchange(): return lax.all_to_all(a, axes, 0, 0, tiled=True)  59.9 us
    ppermute x7, starting transfers between devices, swap(): return lax.ppermute(a, axis, SWAP)  34.3 us
    all_to_all x5, starting transfers between devices, exchange(): return lax.all_to_all(a, axes, 0, 0, tiled=True)  32.8 us
    all_to_all x1, blocking collectives, exchange(): return lax.all_to_all(a, axes, 0, 0, tiled=True)  18 us
    ppermute x3, starting transfers between devices, local(): came = lax.ppermute(rows, 'x', [(i, i ^ step) for i in range(nx)])  17.5 us
    ppermute x7, waiting for transfers between devices, swap(): return lax.ppermute(a, axis, SWAP)  9.33 us
    dot_general x8, matrix products, mm(): lax.dot_general(a, b, (dims, ((), ())), precision=lax.Precision.HIGH, pre...  8.77 us
    ppermute x3, waiting for transfers between devices, local(): came = lax.ppermute(rows, 'x', [(i, i ^ step) for i in range(nx)])  8.38 us
  transfers between devices with their start and end apart: 17, of which 11 were waited for; matrix products, arithmetic and copies ran while one was open for 4% of the time, Pallas kernels for 0%

profile of v6, /device:TPU:1, one launch (start us, length us, event | category | flops | bytes accessed | tf_op | source)
XLA Modules:
  0.0 211.1 jit_solution(15368838206734857197)
XLA Ops:
  0.6 0.0 copy-start
  0.7 0.7 copy-done.6
  1.4 0.7 copy-done.8
  2.1 15.1 %collective-permute-start = (f32[16,512]{1,0:T(8,128)S(1)}, f32[16,512]{1,0:T(8,128)S(1)}, u32[]{:S(2)}, u32[]{:S(2)}) collective-permute-start(f32[16,512]{1,0:T(8,128)S(1)} %get-tuple-element.23), channel_id=1, source_target_pairs={{0,2},{2,0},{1,3},{3,1},{4,6},{6,4},{5,7},{7,5},{8,10},{10,8},{9,1... | collective-permute-start | bytes 98312 | tf_op jit(solution)/shard_map/ppermute | solution.py:30
  17.2 3.3 %collective-permute-start.2 = (f32[16,256]{1,0:T(8,128)S(1)}, f32[16,256]{1,0:T(8,128)S(1)}, u32[]{:S(2)}, u32[]{:S(2)}) collective-permute-start(f32[16,256]{1,0:T(8,128)S(1)} %get-tuple-element.22), channel_id=1, source_target_pairs={{0,1},{1,33},{2,65},{3,97},{4,129},{5,161},{6,193},{7,225},{8,257}... | collective-permute-start | bytes 49160 | tf_op jit(solution)/shard_map/ppermute | solution.py:69
  20.6 3.1 %collective-permute-start.1 = (f32[16,256]{1,0:T(8,128)S(1)}, f32[16,256]{1,0:T(8,128)S(1)}, u32[]{:S(2)}, u32[]{:S(2)}) collective-permute-start(f32[16,256]{1,0:T(8,128)S(1)} %get-tuple-element.21), channel_id=1, source_target_pairs={{0,0},{1,32},{2,64},{3,96},{4,128},{5,160},{6,192},{7,224},{8,256}... | collective-permute-start | bytes 49160 | tf_op jit(solution)/shard_map/ppermute | solution.py:68
  23.7 0.0 copy-start.9
  23.7 0.7 copy-done.9
  24.4 0.6 fusion.13
  26.3 0.0 collective-permute-done
  26.3 1.4 broadcast_add_fusion
  27.7 1.9 collective-permute-start.3
  29.7 13.7 %collective-permute-start.6 = (f32[2,16,512]{2,1,0:T(8,128)S(1)}, f32[2,16,512]{2,1,0:T(8,128)S(1)}, u32[]{:S(2)}, u32[]{:S(2)}) collective-permute-start(f32[2,16,512]{2,1,0:T(8,128)S(1)} %pad_maximum_fusion.6), channel_id=1, source_target_pairs={{0,16},{4,20},{8,24},{12,28},{16,0},{20,4},{24,8},{28,12},{1,17},{... | collective-permute-start | bytes 196616 | tf_op jit(solution)/shard_map/ppermute | solution.py:84
  43.4 2.0 collective-permute-done.6
  45.4 1.9 collective-permute-start.7
  47.4 1.1 broadcast_in_dim.10
  48.5 18.8 %all-to-all-start = ((f32[32,2,16,256]{3,2,1,0:T(8,128)}), f32[32,2,16,256]{3,2,1,0:T(8,128)S(1)}, u32[]{:S(2)}, u32[]{:S(2)}) async-start(f32[32,2,16,256]{3,2,1,0:T(8,128)} %broadcast_in_dim.10), calls=%async_computation | async-start | bytes 2097152 | tf_op jit(solution)/shard_map/all_to_all | solution.py:34
  67.3 0.7 slice_multiply_fusion
  68.1 1.9 collective-permute-start.8
  70.0 6.4 %collective-permute-done.8 = f32[2,2,2,16,512]{4,3,2,1,0:T(8,128)S(1)} collective-permute-done((f32[2,2,2,16,512]{4,3,2,1,0:T(8,128)S(1)}, f32[2,2,2,16,512]{4,3,2,1,0:T(8,128)S(1)}, u32[]{:S(2)}, u32[]{:S(2)}) %collective-permute-start.8) | collective-permute-done | bytes 262176 | tf_op jit(solution)/shard_map/ppermute | solution.py:84
  76.4 0.1 select_bitcast_fusion.3
  76.5 4.2 %collective-permute-start.9 = (f32[2,2,2,2,16,512]{5,4,3,2,1,0:T(8,128)S(1)}, f32[2,2,2,2,16,512]{5,4,3,2,1,0:T(8,128)}, u32[]{:S(2)}, u32[]{:S(2)}) collective-permute-start(f32[2,2,2,2,16,512]{5,4,3,2,1,0:T(8,128)S(1)} %pad_maximum_fusion.1), channel_id=1, source_target_pairs={{0,1},{1,0},{2,3},{3,2},{4,5},{5,4},{6,7},{7,6},{8,9},{9,8},{10,11... | collective-permute-start | bytes 1572872 | tf_op jit(solution)/shard_map/ppermute | solution.py:30
  80.7 0.1 fusion.10
  80.8 0.1 copy.22
  80.9 0.1 broadcast_bitcast_fusion
  81.0 1.4 collective-permute-done.9
  82.4 2.0 select_bitcast_fusion.1
  84.4 8.8 %all-to-all-done = f32[32,2,16,256]{3,2,1,0:T(8,128)S(1)} async-done(((f32[32,2,16,256]{3,2,1,0:T(8,128)}), f32[32,2,16,256]{3,2,1,0:T(8,128)S(1)}, u32[]{:S(2)}, u32[]{:S(2)}) %all-to-all-start) | async-done | bytes 1048608 | tf_op jit(solution)/shard_map/all_to_all | solution.py:34
  93.2 0.1 fusion.12
  93.3 0.6 fusion.14
  93.9 2.6 %convolution_add_fusion = f32[512,256]{1,0:T(8,128)} fusion(f32[512,256]{1,0:T(8,128)S(1)} %fusion.14, f32[512,512]{1,0:T(8,128)} %collective-permute-done.3, f32[512,256]{1,0:T(8,128)S(1)} %bitcast.78), kind=kOutput, calls=%fused_computation | convolution fusion | flops 402784256 | bytes 2621440 | tf_op jit(solution)/shard_map/dot_general | solution.py:16
  96.5 1.0 slice.66
  97.5 6.3 %collective-permute-start.10 = (f32[512,128]{1,0:T(8,128)S(1)}, f32[512,128]{1,0:T(8,128)S(1)}, u32[]{:S(2)}, u32[]{:S(2)}) collective-permute-start(f32[512,128]{1,0:T(8,128)S(1)} %slice.66), channel_id=1, source_target_pairs={{0,1},{1,0},{2,3},{3,2},{4,5},{5,4},{6,7},{7,6},{8,9},{9,8},{10,11... | collective-permute-start | bytes 786440 | tf_op jit(solution)/shard_map/ppermute | solution.py:30
  103.9 0.1 pad_maximum_fusion
  104.0 0.2 bitcast_multiply_fusion
  104.1 1.6 fusion.2
  105.8 1.3 fusion.3
  107.2 18.0 %all_to_all.30 = f32[8,48,256]{2,1,0:T(8,128)S(1)} all-to-all(f32[8,48,256]{2,1,0:T(8,128)S(1)} %bitcast.80), channel_id=1, replica_groups=mesh['zl'=4,'y'=8,'x'=8,'zh'=2,'core'=2] {'y'}, dimensions={0} | all-to-all | bytes 786432 | tf_op jit(solution)/shard_map/all_to_all | solution.py:34
  125.2 3.5 %all-to-all-start.1 = ((f32[8,64,256]{2,1,0:T(8,128)}), f32[8,64,256]{2,1,0:T(8,128)S(1)}, u32[]{:S(2)}, u32[]{:S(2)}) async-start(f32[8,64,256]{2,1,0:T(8,128)} %bitcast.7), calls=%async_computation.1 | async-start | bytes 1048576 | tf_op jit(solution)/shard_map/all_to_all | solution.py:34
  128.8 17.8 %all-to-all-done.1 = f32[8,64,256]{2,1,0:T(8,128)S(1)} async-done(((f32[8,64,256]{2,1,0:T(8,128)}), f32[8,64,256]{2,1,0:T(8,128)S(1)}, u32[]{:S(2)}, u32[]{:S(2)}) %all-to-all-start.1) | async-done | bytes 524320 | tf_op jit(solution)/shard_map/all_to_all | solution.py:34
  146.6 0.8 broadcast_in_dim.12
  147.4 3.5 %all-to-all-start.3 = ((f32[8,48,256]{2,1,0:T(8,128)}), f32[8,48,256]{2,1,0:T(8,128)S(1)}, u32[]{:S(2)}, u32[]{:S(2)}) async-start(f32[8,48,256]{2,1,0:T(8,128)} %broadcast_in_dim.12), calls=%async_computation.3 | async-start | bytes 786432 | tf_op jit(solution)/shard_map/all_to_all | solution.py:34
  150.9 1.9 collective-permute-start.4
  152.9 6.6 %collective-permute-done.4 = f32[32,256]{1,0:T(8,128)S(1)} collective-permute-done((f32[32,256]{1,0:T(8,128)S(1)}, f32[32,256]{1,0:T(8,128)S(1)}, u32[]{:S(2)}, u32[]{:S(2)}) %collective-permute-start.4) | collective-permute-done | bytes 32800 | tf_op jit(solution)/shard_map/ppermute | solution.py:30
  159.5 6.4 %all-to-all-done.3 = f32[8,48,256]{2,1,0:T(8,128)S(1)} async-done(((f32[8,48,256]{2,1,0:T(8,128)}), f32[8,48,256]{2,1,0:T(8,128)S(1)}, u32[]{:S(2)}, u32[]{:S(2)}) %all-to-all-start.3) | async-done | bytes 393248 | tf_op jit(solution)/shard_map/all_to_all | solution.py:34
  166.0 0.8 broadcast_in_dim.13
  166.8 3.5 %all-to-all-start.4 = ((f32[8,48,256]{2,1,0:T(8,128)}), f32[8,48,256]{2,1,0:T(8,128)S(1)}, u32[]{:S(2)}, u32[]{:S(2)}) async-start(f32[8,48,256]{2,1,0:T(8,128)} %broadcast_in_dim.13), calls=%async_computation.4 | async-start | bytes 786432 | tf_op jit(solution)/shard_map/all_to_all | solution.py:34
  170.2 2.4 %collective-permute-start.5 = (f32[32,256]{1,0:T(8,128)S(1)}, f32[32,256]{1,0:T(8,128)S(1)}, u32[]{:S(2)}, u32[]{:S(2)}) collective-permute-start(f32[32,256]{1,0:T(8,128)S(1)} %fusion.8), channel_id=1, source_target_pairs={{0,1},{1,0},{2,3},{3,2},{4,5},{5,4},{6,7},{7,6},{8,9},{9,8},{10,11... | collective-permute-start | bytes 98312 | tf_op jit(solution)/shard_map/ppermute | solution.py:30
  172.6 0.8 collective-permute-done.5
  173.5 11.8 %all-to-all-done.4 = f32[8,48,256]{2,1,0:T(8,128)S(1)} async-done(((f32[8,48,256]{2,1,0:T(8,128)}), f32[8,48,256]{2,1,0:T(8,128)S(1)}, u32[]{:S(2)}, u32[]{:S(2)}) %all-to-all-start.4) | async-done | bytes 393248 | tf_op jit(solution)/shard_map/all_to_all | solution.py:34
  185.3 0.8 broadcast_in_dim.14
  186.1 3.6 %all-to-all-start.5 = ((f32[8,48,256]{2,1,0:T(8,128)}), f32[8,48,256]{2,1,0:T(8,128)S(1)}, u32[]{:S(2)}, u32[]{:S(2)}) async-start(f32[8,48,256]{2,1,0:T(8,128)} %broadcast_in_dim.14), calls=%async_computation.5 | async-start | bytes 786432 | tf_op jit(solution)/shard_map/all_to_all | solution.py:34
  189.8 15.0 %all-to-all-done.5 = f32[8,48,256]{2,1,0:T(8,128)S(1)} async-done(((f32[8,48,256]{2,1,0:T(8,128)}), f32[8,48,256]{2,1,0:T(8,128)S(1)}, u32[]{:S(2)}, u32[]{:S(2)}) %all-to-all-start.5) | async-done | bytes 393248 | tf_op jit(solution)/shard_map/all_to_all | solution.py:34
  204.8 2.4 %collective-permute-start.11 = (f32[384,256]{1,0:T(8,128)S(1)}, f32[384,256]{1,0:T(8,128)S(1)}, u32[]{:S(2)}, u32[]{:S(2)}) collective-permute-start(f32[384,256]{1,0:T(8,128)S(1)} %bitcast.81), channel_id=1, source_target_pairs={{0,1},{1,0},{2,3},{3,2},{4,5},{5,4},{6,7},{7,6},{8,9},{9,8},{10,11... | collective-permute-start | bytes 1179656 | tf_op jit(solution)/shard_map/ppermute | solution.py:30
  207.2 0.0 copy-start.7
  207.2 0.8 bitcast_subtract_fusion
  208.0 0.5 collective-permute-done.11
  208.5 0.1 broadcast_select_fusion
  208.6 0.0 copy-start.2
  208.7 0.3 convolution_subtract_fusion.1
  208.9 0.4 copy-done.2
  209.3 0.4 convolution_bitcast_fusion
  209.7 0.3 copy-done.3
  210.0 1.1 fusion.1
  (47 shorter events, 0.5 us)
Async XLA Ops:
  0.6 206.6 %copy-start = (f32[256,256]{1,0:T(8,128)S(1)}, f32[256,256]{1,0:T(8,128)}, u32[]{:S(2)}) copy-start(f32[256,256]{1,0:T(8,128)} %param.13) | copy-start | bytes 786436
  0.7 0.8 copy-start.6
  1.4 0.7 copy-start.8
  2.1 24.2 %collective-permute-start = (f32[16,512]{1,0:T(8,128)S(1)}, f32[16,512]{1,0:T(8,128)S(1)}, u32[]{:S(2)}, u32[]{:S(2)}) collective-permute-start(f32[16,512]{1,0:T(8,128)S(1)} %get-tuple-element.23), channel_id=1, source_target_pairs={{0,2},{2,0},{1,3},{3,1},{4,6},{6,4},{5,7},{7,5},{8,10},{10,8},{9,1... | collective-permute-start | bytes 98312 | tf_op jit(solution)/shard_map/ppermute | solution.py:30
  17.2 26.1 %collective-permute-start.2 = (f32[16,256]{1,0:T(8,128)S(1)}, f32[16,256]{1,0:T(8,128)S(1)}, u32[]{:S(2)}, u32[]{:S(2)}) collective-permute-start(f32[16,256]{1,0:T(8,128)S(1)} %get-tuple-element.22), channel_id=1, source_target_pairs={{0,1},{1,33},{2,65},{3,97},{4,129},{5,161},{6,193},{7,225},{8,257}... | collective-permute-start | bytes 49160 | tf_op jit(solution)/shard_map/ppermute | solution.py:69
  20.6 26.8 %collective-permute-start.1 = (f32[16,256]{1,0:T(8,128)S(1)}, f32[16,256]{1,0:T(8,128)S(1)}, u32[]{:S(2)}, u32[]{:S(2)}) collective-permute-start(f32[16,256]{1,0:T(8,128)S(1)} %get-tuple-element.21), channel_id=1, source_target_pairs={{0,0},{1,32},{2,64},{3,96},{4,128},{5,160},{6,192},{7,224},{8,256}... | collective-permute-start | bytes 49160 | tf_op jit(solution)/shard_map/ppermute | solution.py:68
  23.7 0.7 copy-start.9
  27.7 39.6 %collective-permute-start.3 = (f32[512,512]{1,0:T(8,128)S(1)}, f32[512,512]{1,0:T(8,128)}, u32[]{:S(2)}, u32[]{:S(2)}) collective-permute-start(f32[512,512]{1,0:T(8,128)S(1)} %broadcast_add_fusion), channel_id=1, source_target_pairs={{0,1},{1,0},{2,3},{3,2},{4,5},{5,4},{6,7},{7,6},{8,9},{9,8},{10,11... | collective-permute-start | bytes 3145736 | tf_op jit(solution)/shard_map/ppermute | solution.py:30
  29.7 15.7 %collective-permute-start.6 = (f32[2,16,512]{2,1,0:T(8,128)S(1)}, f32[2,16,512]{2,1,0:T(8,128)S(1)}, u32[]{:S(2)}, u32[]{:S(2)}) collective-permute-start(f32[2,16,512]{2,1,0:T(8,128)S(1)} %pad_maximum_fusion.6), channel_id=1, source_target_pairs={{0,16},{4,20},{8,24},{12,28},{16,0},{20,4},{24,8},{28,12},{1,17},{... | collective-permute-start | bytes 196616 | tf_op jit(solution)/shard_map/ppermute | solution.py:84
  45.4 21.9 %collective-permute-start.7 = (f32[2,2,16,512]{3,2,1,0:T(8,128)S(1)}, f32[2,2,16,512]{3,2,1,0:T(8,128)S(1)}, u32[]{:S(2)}, u32[]{:S(2)}) collective-permute-start(f32[2,2,16,512]{3,2,1,0:T(8,128)S(1)} %pad_maximum_fusion.5), channel_id=1, source_target_pairs={{0,8},{4,12},{8,0},{12,4},{16,24},{20,28},{24,16},{28,20},{1,9},{5... | collective-permute-start | bytes 393224 | tf_op jit(solution)/shard_map/ppermute | solution.py:84
  48.5 44.7 %all-to-all-start = ((f32[32,2,16,256]{3,2,1,0:T(8,128)}), f32[32,2,16,256]{3,2,1,0:T(8,128)S(1)}, u32[]{:S(2)}, u32[]{:S(2)}) async-start(f32[32,2,16,256]{3,2,1,0:T(8,128)} %broadcast_in_dim.10), calls=%async_computation | async-start | bytes 2097152 | tf_op jit(solution)/shard_map/all_to_all | solution.py:34
  68.1 8.3 %collective-permute-start.8 = (f32[2,2,2,16,512]{4,3,2,1,0:T(8,128)S(1)}, f32[2,2,2,16,512]{4,3,2,1,0:T(8,128)S(1)}, u32[]{:S(2)}, u32[]{:S(2)}) collective-permute-start(f32[2,2,2,16,512]{4,3,2,1,0:T(8,128)S(1)} %maximum_add_fusion), channel_id=1, source_target_pairs={{0,4},{4,0},{8,12},{12,8},{16,20},{20,16},{24,28},{28,24},{1,5},{5... | collective-permute-start | bytes 786440 | tf_op jit(solution)/shard_map/ppermute | solution.py:84
  76.5 5.9 %collective-permute-start.9 = (f32[2,2,2,2,16,512]{5,4,3,2,1,0:T(8,128)S(1)}, f32[2,2,2,2,16,512]{5,4,3,2,1,0:T(8,128)}, u32[]{:S(2)}, u32[]{:S(2)}) collective-permute-start(f32[2,2,2,2,16,512]{5,4,3,2,1,0:T(8,128)S(1)} %pad_maximum_fusion.1), channel_id=1, source_target_pairs={{0,1},{1,0},{2,3},{3,2},{4,5},{5,4},{6,7},{7,6},{8,9},{9,8},{10,11... | collective-permute-start | bytes 1572872 | tf_op jit(solution)/shard_map/ppermute | solution.py:30
  96.5 7.4 %copy-start.1 = (f32[2,2,2,2,1,16,512]{6,5,4,3,2,1,0:T(8,128)S(1)}, f32[2,2,2,2,1,16,512]{6,5,4,3,2,1,0:T(8,128)}, u32[]{:S(2)}) copy-start(f32[2,2,2,2,1,16,512]{6,5,4,3,2,1,0:T(8,128)} %get-tuple-element.6) | copy-start | bytes 1572868
  97.5 8.3 %collective-permute-start.10 = (f32[512,128]{1,0:T(8,128)S(1)}, f32[512,128]{1,0:T(8,128)S(1)}, u32[]{:S(2)}, u32[]{:S(2)}) collective-permute-start(f32[512,128]{1,0:T(8,128)S(1)} %slice.66), channel_id=1, source_target_pairs={{0,1},{1,0},{2,3},{3,2},{4,5},{5,4},{6,7},{7,6},{8,9},{9,8},{10,11... | collective-permute-start | bytes 786440 | tf_op jit(solution)/shard_map/ppermute | solution.py:30
  125.2 21.4 %all-to-all-start.1 = ((f32[8,64,256]{2,1,0:T(8,128)}), f32[8,64,256]{2,1,0:T(8,128)S(1)}, u32[]{:S(2)}, u32[]{:S(2)}) async-start(f32[8,64,256]{2,1,0:T(8,128)} %bitcast.7), calls=%async_computation.1 | async-start | bytes 1048576 | tf_op jit(solution)/shard_map/all_to_all | solution.py:34
  147.4 18.5 %all-to-all-start.3 = ((f32[8,48,256]{2,1,0:T(8,128)}), f32[8,48,256]{2,1,0:T(8,128)S(1)}, u32[]{:S(2)}, u32[]{:S(2)}) async-start(f32[8,48,256]{2,1,0:T(8,128)} %broadcast_in_dim.12), calls=%async_computation.3 | async-start | bytes 786432 | tf_op jit(solution)/shard_map/all_to_all | solution.py:34
  150.9 8.6 %collective-permute-start.4 = (f32[32,256]{1,0:T(8,128)S(1)}, f32[32,256]{1,0:T(8,128)S(1)}, u32[]{:S(2)}, u32[]{:S(2)}) collective-permute-start(f32[32,256]{1,0:T(8,128)S(1)} %dynamic-slice_bitcast_fusion), channel_id=1, source_target_pairs={{0,2},{2,0},{1,3},{3,1},{4,6},{6,4},{5,7},{7,5},{8,10},{10,8},{9,1... | collective-permute-start | bytes 98312 | tf_op jit(solution)/shard_map/ppermute | solution.py:30
  166.8 18.5 %all-to-all-start.4 = ((f32[8,48,256]{2,1,0:T(8,128)}), f32[8,48,256]{2,1,0:T(8,128)S(1)}, u32[]{:S(2)}, u32[]{:S(2)}) async-start(f32[8,48,256]{2,1,0:T(8,128)} %broadcast_in_dim.13), calls=%async_computation.4 | async-start | bytes 786432 | tf_op jit(solution)/shard_map/all_to_all | solution.py:34
  170.2 3.2 %collective-permute-start.5 = (f32[32,256]{1,0:T(8,128)S(1)}, f32[32,256]{1,0:T(8,128)S(1)}, u32[]{:S(2)}, u32[]{:S(2)}) collective-permute-start(f32[32,256]{1,0:T(8,128)S(1)} %fusion.8), channel_id=1, source_target_pairs={{0,1},{1,0},{2,3},{3,2},{4,5},{5,4},{6,7},{7,6},{8,9},{9,8},{10,11... | collective-permute-start | bytes 98312 | tf_op jit(solution)/shard_map/ppermute | solution.py:30
  186.1 3.6 %copy-start.4 = (f32[256,256]{1,0:T(8,128)S(1)}, f32[256,256]{1,0:T(8,128)}, u32[]{:S(2)}) copy-start(f32[256,256]{1,0:T(8,128)} %param.12) | copy-start | bytes 786436
  186.1 3.6 %copy-start.5 = (f32[256,256]{1,0:T(8,128)S(1)}, f32[256,256]{1,0:T(8,128)}, u32[]{:S(2)}) copy-start(f32[256,256]{1,0:T(8,128)} %param.11) | copy-start | bytes 786436
  186.1 18.7 %all-to-all-start.5 = ((f32[8,48,256]{2,1,0:T(8,128)}), f32[8,48,256]{2,1,0:T(8,128)S(1)}, u32[]{:S(2)}, u32[]{:S(2)}) async-start(f32[8,48,256]{2,1,0:T(8,128)} %broadcast_in_dim.14), calls=%async_computation.5 | async-start | bytes 786432 | tf_op jit(solution)/shard_map/all_to_all | solution.py:34
  204.8 3.7 %collective-permute-start.11 = (f32[384,256]{1,0:T(8,128)S(1)}, f32[384,256]{1,0:T(8,128)S(1)}, u32[]{:S(2)}, u32[]{:S(2)}) collective-permute-start(f32[384,256]{1,0:T(8,128)S(1)} %bitcast.81), channel_id=1, source_target_pairs={{0,1},{1,0},{2,3},{3,2},{4,5},{5,4},{6,7},{7,6},{8,9},{9,8},{10,11... | collective-permute-start | bytes 1179656 | tf_op jit(solution)/shard_map/ppermute | solution.py:30
  207.2 0.8 copy-start.7
  208.6 0.7 copy-start.2
  209.3 0.7 copy-start.3

commit v7 on v4

--- a/solution.py
+++ b/solution.py
@@ -56,22 +56,29 @@
     ny, nx, n = lax.axis_size("y"), lax.axis_size("x"), lax.axis_size(PROW)
     core, zh = lax.axis_index("core"), lax.axis_index("zh")
     first = core == 0
-    row = lax.axis_index(PROW)
-    begin = (row * n + lax.axis_index(PCOL)) * span
-    spread = lax.dynamic_slice_in_dim(tile_mask, begin // width, 1, axis=1).astype(jnp.float32)
-    live_one, live_two = panel_one * spread[0], panel_two * spread[1]
+    row, col = lax.axis_index(PROW), lax.axis_index(PCOL)
+
+    def mask(panel, group, place):
+        tile = (group * n + place) * span // width
+        return lax.dynamic_slice(tile_mask, (panel, tile), (1, 1)).astype(jnp.float32)
 
     even = row % 2 == 0
     to_own = [(c * n + j, j * n + c) for c in range(n) for j in range(n)]
     to_other = [(c * n + j, j * n + (c ^ 1)) for c in range(n) for j in range(n)]
-    own = lax.ppermute(jnp.where(even, live_one, live_two), ALL, to_own)
-    other = lax.ppermute(jnp.where(even, live_two, live_one), ALL, to_other)
-    panel = gather(jnp.stack([own, other]), PROW)
+    own = lax.ppermute(jnp.where(even, panel_one, panel_two), ALL, to_own)
+    other = lax.ppermute(jnp.where(even, panel_two, panel_one), ALL, to_other)
+    panel = jnp.stack([own * mask(core, col, row), other * mask(core, col ^ 1, row)])
+    panel = gather(panel, PROW)
     own, other = panel[:, 0].reshape(-1, width), panel[:, 1].reshape(-1, width)
 
     blocks = swap(inverse_blocks, "core")
-    live = jnp.concatenate([live_one, live_two], axis=1)
+    live = jnp.concatenate([panel_one, panel_two], axis=1)
     came = swap(live, "zh")
+
+    def kept(place):
+        return jnp.repeat(jnp.concatenate([mask(0, row, place), mask(1, row, place)], axis=1), width, axis=1)
+
+    live, came = live * kept(col), came * kept(col ^ 2)
     group = jnp.stack([jnp.where(zh == 0, live, came), jnp.where(zh == 0, came, live)])
     group = after(group, blocks)
     place = lax.axis_index("x")
@@ -80,12 +87,13 @@
     for step in range(1, nx // 2):
         came = lax.ppermute(group, "x", [(i, i ^ (2 * step)) for i in range(nx)])
         rows = lax.dynamic_update_index_in_dim(rows, came, (place // 2) ^ step, 0)
+    near = lax.optimization_barrier(after(inverse_blocks, rows[0, 0]))
     rows = both(rows, lax.ppermute(rows, "x", [(i, i ^ 1) for i in range(nx)]), place % 2 == 0, 1)
     rows = both(rows, swap(rows, "core"), first, 3).reshape(-1, 2 * width)
     rows_two = rows[:, width:]
     rows_own = jnp.where(first, rows[:, :width], rows_two)
 
-    total = mm(inverse_blocks, own) + mm(blocks, other)
+    total = mm(near, own) + mm(blocks, other)
     came = swap(total[:, half:], "core")
     grams = jnp.concatenate(
         [
@@ -104,6 +112,9 @@
     col_two = jnp.where(first, sibling, column)
     column_one = pick(col_one.reshape(2, span, width), core)
     column_two = pick(col_two.reshape(2, span, width), core) - mm(column_one, link_block)
+
+    diag_one = lax.optimization_barrier(after(diag_one, column))
+    diag_two = lax.optimization_barrier(after(diag_two, column))
 
     grams = after(jnp.sum(gather(grams, "y"), axis=0), column)
     grams = after(jnp.sum(gather(grams, ("zh", "zl")), axis=0), sibling)

time: 183 us -> 187 us (1.022)
  between operations: 1.26 us -> 5.23 us
  blocking collectives: 27.6 us -> 30 us
  starting transfers between devices: 98.8 us -> 96.5 us
  other arithmetic: 2.1 us -> 4.1 us
    all_to_all x4, starting transfers between devices: 27.9 us -> 36.1 us  [exchange(): return lax.all_to_all(a, axes, 0, 0, tiled=True)]
    ppermute x7, starting transfers between devices: 46.6 us -> 41 us  [swap(): return lax.ppermute(a, axis, SWAP)]
    ppermute x1, starting transfers between devices: 5.93 us -> 1.92 us  [local(): lax.ppermute(rows, 'x', [(i, i ^ 1) for i in range(nx)])]
    all_to_all x1, blocking collectives: 27.6 us -> 30 us  [exchange(): return lax.all_to_all(a, axes, 0, 0, tiled=True)]
    unnamed x24 -> x29, local copies, waits for them, and re-layouts: 4.19 us -> 3.64 us
  transfers between devices with their start and end apart: 17 -> 17, of which waited for: 11 -> 11; matrix products, arithmetic and copies ran while one was open for 3% -> 4% of each run, Pallas kernels for 0% -> 0%
where the time goes in v7:
time: 187 us; the launch traced here: 185 us
  starting transfers between devices  96.5 us (52%)
  waiting for transfers between devices  36.9 us (20%)
  blocking collectives  30 us (16%)
  local copies, waits for them, and re-layouts  7.93 us (4%)
  between operations  5.23 us (3%)
  matrix products  4.76 us (3%)
  other arithmetic  4.1 us (2%)
    ppermute x7, starting transfers between devices, swap(): return lax.ppermute(a, axis, SWAP)  41 us
    all_to_all x4, starting transfers between devices, exchange(): return lax.all_to_all(a, axes, 0, 0, tiled=True)  36.1 us
    all_to_all x1, blocking collectives, exchange(): return lax.all_to_all(a, axes, 0, 0, tiled=True)  30 us
    all_to_all x4, waiting for transfers between devices, exchange(): return lax.all_to_all(a, axes, 0, 0, tiled=True)  18.6 us
    ppermute x3, starting transfers between devices, local(): came = lax.ppermute(group, 'x', [(i, i ^ 2 * step) for i in range(nx)])  12.1 us
    ppermute x7, waiting for transfers between devices, swap(): return lax.ppermute(a, axis, SWAP)  7.07 us
    ppermute x1, waiting for transfers between devices, local(): lax.ppermute(rows, 'x', [(i, i ^ 1) for i in range(nx)])  6.31 us
    ppermute x3, waiting for transfers between devices, local(): came = lax.ppermute(group, 'x', [(i, i ^ 2 * step) for i in range(nx)])  4.93 us
  transfers between devices with their start and end apart: 17, of which 11 were waited for; matrix products, arithmetic and copies ran while one was open for 4% of the time, Pallas kernels for 0%

profile of v7, /device:TPU:1, one launch (start us, length us, event | category | flops | bytes accessed | tf_op | source)
XLA Modules:
  0.0 185.4 jit_solution(9587657163106252102)
XLA Ops:
  0.6 0.0 copy-start
  0.7 0.7 copy-done.8
  1.4 0.7 copy-done.10
  2.1 15.1 %collective-permute-start = (f32[16,512]{1,0:T(8,128)S(1)}, f32[16,512]{1,0:T(8,128)S(1)}, u32[]{:S(2)}, u32[]{:S(2)}) collective-permute-start(f32[16,512]{1,0:T(8,128)S(1)} %get-tuple-element.21), channel_id=1, source_target_pairs={{0,2},{2,0},{1,3},{3,1},{4,6},{6,4},{5,7},{7,5},{8,10},{10,8},{9,1... | collective-permute-start | bytes 98312 | tf_op jit(solution)/shard_map/ppermute | solution.py:30
  17.2 2.9 %collective-permute-start.1 = (f32[512,512]{1,0:T(8,128)}, f32[512,512]{1,0:T(8,128)S(1)}, u32[]{:S(2)}, u32[]{:S(2)}) collective-permute-start(f32[512,512]{1,0:T(8,128)} %param.7), channel_id=1, source_target_pairs={{0,1},{1,0},{2,3},{3,2},{4,5},{5,4},{6,7},{7,6},{8,9},{9,8},{10,11... | collective-permute-start | bytes 3145736 | tf_op jit(solution)/shard_map/ppermute | solution.py:30
  20.1 3.3 %collective-permute-start.6 = (f32[16,256]{1,0:T(8,128)S(1)}, f32[16,256]{1,0:T(8,128)S(1)}, u32[]{:S(2)}, u32[]{:S(2)}) collective-permute-start(f32[16,256]{1,0:T(8,128)S(1)} %get-tuple-element.20), channel_id=1, source_target_pairs={{0,1},{1,33},{2,65},{3,97},{4,129},{5,161},{6,193},{7,225},{8,257}... | collective-permute-start | bytes 49160 | tf_op jit(solution)/shard_map/ppermute | solution.py:69
  23.4 2.2 %collective-permute-start.5 = (f32[16,256]{1,0:T(8,128)S(1)}, f32[16,256]{1,0:T(8,128)S(1)}, u32[]{:S(2)}, u32[]{:S(2)}) collective-permute-start(f32[16,256]{1,0:T(8,128)S(1)} %get-tuple-element.19), channel_id=1, source_target_pairs={{0,0},{1,32},{2,64},{3,96},{4,128},{5,160},{6,192},{7,224},{8,256}... | collective-permute-start | bytes 49160 | tf_op jit(solution)/shard_map/ppermute | solution.py:68
  25.7 0.0 copy-start.11
  25.7 0.7 copy-done.11
  26.4 0.7 fusion.17
  28.4 0.1 maximum_bitcast_fusion
  28.4 0.1 broadcast_bitcast_fusion.1
  29.8 0.1 maximum_bitcast_fusion.1
  29.9 0.1 broadcast_bitcast_fusion
  31.3 0.0 collective-permute-done.6
  31.3 1.1 broadcast_in_dim.57
  32.4 20.9 %all-to-all-start = ((f32[32,2,16,256]{3,2,1,0:T(8,128)}), f32[32,2,16,256]{3,2,1,0:T(8,128)S(1)}, u32[]{:S(2)}, u32[]{:S(2)}) async-start(f32[32,2,16,256]{3,2,1,0:T(8,128)} %broadcast_in_dim.57), calls=%async_computation | async-start | bytes 2097152 | tf_op jit(solution)/shard_map/all_to_all | solution.py:34
  53.4 4.9 %collective-permute-start.2 = (f32[2,16,512]{2,1,0:T(8,128)S(1)}, f32[2,16,512]{2,1,0:T(8,128)S(1)}, u32[]{:S(2)}, u32[]{:S(2)}) collective-permute-start(f32[2,16,512]{2,1,0:T(8,128)S(1)} %maximum_add_fusion.1), channel_id=1, source_target_pairs={{0,8},{4,12},{8,0},{12,4},{16,24},{20,28},{24,16},{28,20},{1,9},{5... | collective-permute-start | bytes 196616 | tf_op jit(solution)/shard_map/ppermute | solution.py:88
  58.4 4.5 %collective-permute-start.3 = (f32[2,16,512]{2,1,0:T(8,128)S(1)}, f32[2,16,512]{2,1,0:T(8,128)S(1)}, u32[]{:S(2)}, u32[]{:S(2)}) collective-permute-start(f32[2,16,512]{2,1,0:T(8,128)S(1)} %maximum_add_fusion.1), channel_id=1, source_target_pairs={{0,16},{4,20},{8,24},{12,28},{16,0},{20,4},{24,8},{28,12},{1,17},{... | collective-permute-start | bytes 196616 | tf_op jit(solution)/shard_map/ppermute | solution.py:88
  62.9 2.6 %collective-permute-start.4 = (f32[2,16,512]{2,1,0:T(8,128)S(1)}, f32[2,16,512]{2,1,0:T(8,128)S(1)}, u32[]{:S(2)}, u32[]{:S(2)}) collective-permute-start(f32[2,16,512]{2,1,0:T(8,128)S(1)} %maximum_add_fusion.1), channel_id=1, source_target_pairs={{0,24},{4,28},{8,16},{12,20},{16,8},{20,12},{24,0},{28,4},{1,25},{... | collective-permute-start | bytes 196616 | tf_op jit(solution)/shard_map/ppermute | solution.py:88
  65.6 1.8 collective-permute-done.3
  67.4 3.2 %collective-permute-done.4 = f32[2,16,512]{2,1,0:T(8,128)S(1)} collective-permute-done((f32[2,16,512]{2,1,0:T(8,128)S(1)}, f32[2,16,512]{2,1,0:T(8,128)S(1)}, u32[]{:S(2)}, u32[]{:S(2)}) %collective-permute-start.4) | collective-permute-done | bytes 65568 | tf_op jit(solution)/shard_map/ppermute | solution.py:88
  70.6 1.9 %collective-permute-start.7 = (f32[4,2,16,512]{3,2,1,0:T(8,128)S(1)}, f32[4,2,16,512]{3,2,1,0:T(8,128)S(1)}, u32[]{:S(2)}, u32[]{:S(2)}) collective-permute-start(f32[4,2,16,512]{3,2,1,0:T(8,128)S(1)} %bitcast_dynamic-update-slice_fusion), channel_id=1, source_target_pairs={{0,4},{4,0},{8,12},{12,8},{16,20},{20,16},{24,28},{28,24},{1,5},{5... | collective-permute-start | bytes 786440 | tf_op jit(solution)/shard_map/ppermute | solution.py:91
  72.5 6.3 %collective-permute-done.7 = f32[4,2,16,512]{3,2,1,0:T(8,128)S(1)} collective-permute-done((f32[4,2,16,512]{3,2,1,0:T(8,128)S(1)}, f32[4,2,16,512]{3,2,1,0:T(8,128)S(1)}, u32[]{:S(2)}, u32[]{:S(2)}) %collective-permute-start.7) | collective-permute-done | bytes 262176 | tf_op jit(solution)/shard_map/ppermute | solution.py:91
  78.9 4.3 %collective-permute-start.8 = (f32[4,2,2,16,512]{4,3,2,1,0:T(8,128)S(1)}, f32[4,2,2,16,512]{4,3,2,1,0:T(8,128)}, u32[]{:S(2)}, u32[]{:S(2)}) collective-permute-start(f32[4,2,2,16,512]{4,3,2,1,0:T(8,128)S(1)} %pad_maximum_fusion.2), channel_id=1, source_target_pairs={{0,1},{1,0},{2,3},{3,2},{4,5},{5,4},{6,7},{7,6},{8,9},{9,8},{10,11... | collective-permute-start | bytes 1572872 | tf_op jit(solution)/shard_map/ppermute | solution.py:30
  83.2 1.4 broadcast_add_fusion
  84.6 0.3 collective-permute-done.8
  84.9 2.0 %select_bitcast_fusion.1 = (f32[4,2,2,1,16,512]{5,4,3,2,1,0:T(8,128)S(1)}, f32[4,2,2,1,16,512]{5,4,3,2,1,0:T(8,128)}) fusion(f32[4,2,2,16,512]{4,3,2,1,0:T(8,128)} %collective-permute-done.8, pred[]{:T(512)S(6)} %eq.16, f32[4,1,2,16,512]{4,3,2,1,0:T(8,128)S(1)} %get-tuple-element.12, f32[4,1,2,16,512]{4,3,2,1,0:T(8,128)S(1)} %get-tuple-element.11), kind=kLoop, calls=%fused_computation.13 | loop fusion | flops 393216 | bytes 2097153 | tf_op jit(solution)/shard_map/stack | solution.py:46
  86.8 0.1 fusion.16
  86.9 0.6 fusion.18
  87.5 0.6 copy-done.3
  88.1 0.6 fusion
  88.8 2.4 %collective-permute-start.9 = (f32[512,128]{1,0:T(8,128)S(1)}, f32[512,128]{1,0:T(8,128)S(1)}, u32[]{:S(2)}, u32[]{:S(2)}) collective-permute-start(f32[512,128]{1,0:T(8,128)S(1)} %slice.76), channel_id=1, source_target_pairs={{0,1},{1,0},{2,3},{3,2},{4,5},{5,4},{6,7},{7,6},{8,9},{9,8},{10,11... | collective-permute-start | bytes 786440 | tf_op jit(solution)/shard_map/ppermute | solution.py:30
  91.2 0.1 pad_maximum_fusion
  91.3 0.6 fusion.3
  91.9 0.4 collective-permute-done.9
  92.3 0.4 fusion.4
  92.8 0.1 pad_maximum_fusion.1
  92.9 30.0 %all_to_all.25 = f32[8,112,256]{2,1,0:T(8,128)S(1)} all-to-all(f32[8,112,256]{2,1,0:T(8,128)S(1)} %pad_maximum_fusion.1), channel_id=1, replica_groups=mesh['zl'=4,'y'=8,'x'=8,'zh'=2,'core'=2] {'x'}, dimensions={0} | all-to-all | bytes 1835008 | tf_op jit(solution)/shard_map/all_to_all | solution.py:34
  122.9 0.1 reduce_sum.27
  122.9 0.8 broadcast_in_dim.58
  123.7 6.4 %all-to-all-start.2 = ((f32[8,48,256]{2,1,0:T(8,128)}), f32[8,48,256]{2,1,0:T(8,128)S(1)}, u32[]{:S(2)}, u32[]{:S(2)}) async-start(f32[8,48,256]{2,1,0:T(8,128)} %broadcast_in_dim.58), calls=%async_computation.2 | async-start | bytes 786432 | tf_op jit(solution)/shard_map/all_to_all | solution.py:34
  130.1 3.5 %collective-permute-start.10 = (f32[32,256]{1,0:T(8,128)S(1)}, f32[32,256]{1,0:T(8,128)S(1)}, u32[]{:S(2)}, u32[]{:S(2)}) collective-permute-start(f32[32,256]{1,0:T(8,128)S(1)} %dynamic-slice_bitcast_fusion), channel_id=1, source_target_pairs={{0,2},{2,0},{1,3},{3,1},{4,6},{6,4},{5,7},{7,5},{8,10},{10,8},{9,1... | collective-permute-start | bytes 98312 | tf_op jit(solution)/shard_map/ppermute | solution.py:30
  133.7 5.1 %collective-permute-done.10 = f32[32,256]{1,0:T(8,128)S(1)} collective-permute-done((f32[32,256]{1,0:T(8,128)S(1)}, f32[32,256]{1,0:T(8,128)S(1)}, u32[]{:S(2)}, u32[]{:S(2)}) %collective-permute-start.10) | collective-permute-done | bytes 32800 | tf_op jit(solution)/shard_map/ppermute | solution.py:30
  138.8 3.6 %all-to-all-done.2 = f32[8,48,256]{2,1,0:T(8,128)S(1)} async-done(((f32[8,48,256]{2,1,0:T(8,128)}), f32[8,48,256]{2,1,0:T(8,128)S(1)}, u32[]{:S(2)}, u32[]{:S(2)}) %all-to-all-start.2) | async-done | bytes 393248 | tf_op jit(solution)/shard_map/all_to_all | solution.py:34
  142.4 0.8 broadcast_in_dim.59
  143.2 4.3 %all-to-all-start.3 = ((f32[8,48,256]{2,1,0:T(8,128)}), f32[8,48,256]{2,1,0:T(8,128)S(1)}, u32[]{:S(2)}, u32[]{:S(2)}) async-start(f32[8,48,256]{2,1,0:T(8,128)} %broadcast_in_dim.59), calls=%async_computation.3 | async-start | bytes 786432 | tf_op jit(solution)/shard_map/all_to_all | solution.py:34
  147.5 5.6 %collective-permute-start.11 = (f32[32,256]{1,0:T(8,128)S(1)}, f32[32,256]{1,0:T(8,128)S(1)}, u32[]{:S(2)}, u32[]{:S(2)}) collective-permute-start(f32[32,256]{1,0:T(8,128)S(1)} %fusion.10), channel_id=1, source_target_pairs={{0,1},{1,0},{2,3},{3,2},{4,5},{5,4},{6,7},{7,6},{8,9},{9,8},{10,11... | collective-permute-start | bytes 98312 | tf_op jit(solution)/shard_map/ppermute | solution.py:30
  153.1 0.8 collective-permute-done.11
  153.9 4.2 %all-to-all-done.3 = f32[8,48,256]{2,1,0:T(8,128)S(1)} async-done(((f32[8,48,256]{2,1,0:T(8,128)}), f32[8,48,256]{2,1,0:T(8,128)S(1)}, u32[]{:S(2)}, u32[]{:S(2)}) %all-to-all-start.3) | async-done | bytes 393248 | tf_op jit(solution)/shard_map/all_to_all | solution.py:34
  158.2 0.8 broadcast_in_dim.60
  159.0 4.5 %all-to-all-start.4 = ((f32[8,48,256]{2,1,0:T(8,128)}), f32[8,48,256]{2,1,0:T(8,128)S(1)}, u32[]{:S(2)}, u32[]{:S(2)}) async-start(f32[8,48,256]{2,1,0:T(8,128)} %broadcast_in_dim.60), calls=%async_computation.4 | async-start | bytes 786432 | tf_op jit(solution)/shard_map/all_to_all | solution.py:34
  163.5 10.7 %all-to-all-done.4 = f32[8,48,256]{2,1,0:T(8,128)S(1)} async-done(((f32[8,48,256]{2,1,0:T(8,128)}), f32[8,48,256]{2,1,0:T(8,128)S(1)}, u32[]{:S(2)}, u32[]{:S(2)}) %all-to-all-start.4) | async-done | bytes 393248 | tf_op jit(solution)/shard_map/all_to_all | solution.py:34
  174.2 7.2 %collective-permute-start.12 = (f32[384,256]{1,0:T(8,128)S(1)}, f32[384,256]{1,0:T(8,128)S(1)}, u32[]{:S(2)}, u32[]{:S(2)}) collective-permute-start(f32[384,256]{1,0:T(8,128)S(1)} %bitcast.91), channel_id=1, source_target_pairs={{0,1},{1,0},{2,3},{3,2},{4,5},{5,4},{6,7},{7,6},{8,9},{9,8},{10,11... | collective-permute-start | bytes 1179656 | tf_op jit(solution)/shard_map/ppermute | solution.py:30
  181.5 0.0 copy-start.9
  181.5 0.8 bitcast_subtract_fusion
  182.3 0.5 collective-permute-done.12
  182.8 0.1 broadcast_select_fusion
  182.9 0.0 copy-start.4
  182.9 0.3 convolution_subtract_fusion.1
  183.2 0.4 copy-done.4
  183.6 0.4 convolution_bitcast_fusion.1
  184.0 0.3 copy-done.5
  184.3 1.1 fusion.2
  (55 shorter events, 0.5 us)
Async XLA Ops:
  0.6 180.9 %copy-start = (f32[256,256]{1,0:T(8,128)S(1)}, f32[256,256]{1,0:T(8,128)}, u32[]{:S(2)}) copy-start(f32[256,256]{1,0:T(8,128)} %param.13) | copy-start | bytes 786436
  0.7 0.8 copy-start.8
  1.4 0.7 copy-start.10
  2.1 51.2 %collective-permute-start = (f32[16,512]{1,0:T(8,128)S(1)}, f32[16,512]{1,0:T(8,128)S(1)}, u32[]{:S(2)}, u32[]{:S(2)}) collective-permute-start(f32[16,512]{1,0:T(8,128)S(1)} %get-tuple-element.21), channel_id=1, source_target_pairs={{0,2},{2,0},{1,3},{3,1},{4,6},{6,4},{5,7},{7,5},{8,10},{10,8},{9,1... | collective-permute-start | bytes 98312 | tf_op jit(solution)/shard_map/ppermute | solution.py:30
  17.2 36.2 %collective-permute-start.1 = (f32[512,512]{1,0:T(8,128)}, f32[512,512]{1,0:T(8,128)S(1)}, u32[]{:S(2)}, u32[]{:S(2)}) collective-permute-start(f32[512,512]{1,0:T(8,128)} %param.7), channel_id=1, source_target_pairs={{0,1},{1,0},{2,3},{3,2},{4,5},{5,4},{6,7},{7,6},{8,9},{9,8},{10,11... | collective-permute-start | bytes 3145736 | tf_op jit(solution)/shard_map/ppermute | solution.py:30
  20.1 11.1 %collective-permute-start.6 = (f32[16,256]{1,0:T(8,128)S(1)}, f32[16,256]{1,0:T(8,128)S(1)}, u32[]{:S(2)}, u32[]{:S(2)}) collective-permute-start(f32[16,256]{1,0:T(8,128)S(1)} %get-tuple-element.20), channel_id=1, source_target_pairs={{0,1},{1,33},{2,65},{3,97},{4,129},{5,161},{6,193},{7,225},{8,257}... | collective-permute-start | bytes 49160 | tf_op jit(solution)/shard_map/ppermute | solution.py:69
  23.4 7.9 %collective-permute-start.5 = (f32[16,256]{1,0:T(8,128)S(1)}, f32[16,256]{1,0:T(8,128)S(1)}, u32[]{:S(2)}, u32[]{:S(2)}) collective-permute-start(f32[16,256]{1,0:T(8,128)S(1)} %get-tuple-element.19), channel_id=1, source_target_pairs={{0,0},{1,32},{2,64},{3,96},{4,128},{5,160},{6,192},{7,224},{8,256}... | collective-permute-start | bytes 49160 | tf_op jit(solution)/shard_map/ppermute | solution.py:68
  25.7 0.7 copy-start.11
  32.4 54.4 %all-to-all-start = ((f32[32,2,16,256]{3,2,1,0:T(8,128)}), f32[32,2,16,256]{3,2,1,0:T(8,128)S(1)}, u32[]{:S(2)}, u32[]{:S(2)}) async-start(f32[32,2,16,256]{3,2,1,0:T(8,128)} %broadcast_in_dim.57), calls=%async_computation | async-start | bytes 2097152 | tf_op jit(solution)/shard_map/all_to_all | solution.py:34
  53.4 12.1 %copy-start.2 = (f32[512,512]{1,0:T(8,128)}, f32[512,512]{1,0:T(8,128)S(1)}, u32[]{:S(2)}) copy-start(f32[512,512]{1,0:T(8,128)S(1)} %collective-permute-done.1) | copy-start | bytes 3145732
  53.4 12.1 %collective-permute-start.2 = (f32[2,16,512]{2,1,0:T(8,128)S(1)}, f32[2,16,512]{2,1,0:T(8,128)S(1)}, u32[]{:S(2)}, u32[]{:S(2)}) collective-permute-start(f32[2,16,512]{2,1,0:T(8,128)S(1)} %maximum_add_fusion.1), channel_id=1, source_target_pairs={{0,8},{4,12},{8,0},{12,4},{16,24},{20,28},{24,16},{28,20},{1,9},{5... | collective-permute-start | bytes 196616 | tf_op jit(solution)/shard_map/ppermute | solution.py:88
  58.4 9.0 %collective-permute-start.3 = (f32[2,16,512]{2,1,0:T(8,128)S(1)}, f32[2,16,512]{2,1,0:T(8,128)S(1)}, u32[]{:S(2)}, u32[]{:S(2)}) collective-permute-start(f32[2,16,512]{2,1,0:T(8,128)S(1)} %maximum_add_fusion.1), channel_id=1, source_target_pairs={{0,16},{4,20},{8,24},{12,28},{16,0},{20,4},{24,8},{28,12},{1,17},{... | collective-permute-start | bytes 196616 | tf_op jit(solution)/shard_map/ppermute | solution.py:88
  62.9 7.6 %collective-permute-start.4 = (f32[2,16,512]{2,1,0:T(8,128)S(1)}, f32[2,16,512]{2,1,0:T(8,128)S(1)}, u32[]{:S(2)}, u32[]{:S(2)}) collective-permute-start(f32[2,16,512]{2,1,0:T(8,128)S(1)} %maximum_add_fusion.1), channel_id=1, source_target_pairs={{0,24},{4,28},{8,16},{12,20},{16,8},{20,12},{24,0},{28,4},{1,25},{... | collective-permute-start | bytes 196616 | tf_op jit(solution)/shard_map/ppermute | solution.py:88
  70.6 8.3 %collective-permute-start.7 = (f32[4,2,16,512]{3,2,1,0:T(8,128)S(1)}, f32[4,2,16,512]{3,2,1,0:T(8,128)S(1)}, u32[]{:S(2)}, u32[]{:S(2)}) collective-permute-start(f32[4,2,16,512]{3,2,1,0:T(8,128)S(1)} %bitcast_dynamic-update-slice_fusion), channel_id=1, source_target_pairs={{0,4},{4,0},{8,12},{12,8},{16,20},{20,16},{24,28},{28,24},{1,5},{5... | collective-permute-start | bytes 786440 | tf_op jit(solution)/shard_map/ppermute | solution.py:91
  78.9 5.9 %collective-permute-start.8 = (f32[4,2,2,16,512]{4,3,2,1,0:T(8,128)S(1)}, f32[4,2,2,16,512]{4,3,2,1,0:T(8,128)}, u32[]{:S(2)}, u32[]{:S(2)}) collective-permute-start(f32[4,2,2,16,512]{4,3,2,1,0:T(8,128)S(1)} %pad_maximum_fusion.2), channel_id=1, source_target_pairs={{0,1},{1,0},{2,3},{3,2},{4,5},{5,4},{6,7},{7,6},{8,9},{9,8},{10,11... | collective-permute-start | bytes 1572872 | tf_op jit(solution)/shard_map/ppermute | solution.py:30
  86.9 1.2 copy-start.3
  88.7 2.5 %copy-start.1 = (f32[4,2,2,1,16,512]{5,4,3,2,1,0:T(8,128)S(1)}, f32[4,2,2,1,16,512]{5,4,3,2,1,0:T(8,128)}, u32[]{:S(2)}) copy-start(f32[4,2,2,1,16,512]{5,4,3,2,1,0:T(8,128)} %get-tuple-element.8) | copy-start | bytes 1572868
  88.8 3.6 %collective-permute-start.9 = (f32[512,128]{1,0:T(8,128)S(1)}, f32[512,128]{1,0:T(8,128)S(1)}, u32[]{:S(2)}, u32[]{:S(2)}) collective-permute-start(f32[512,128]{1,0:T(8,128)S(1)} %slice.76), channel_id=1, source_target_pairs={{0,1},{1,0},{2,3},{3,2},{4,5},{5,4},{6,7},{7,6},{8,9},{9,8},{10,11... | collective-permute-start | bytes 786440 | tf_op jit(solution)/shard_map/ppermute | solution.py:30
  123.7 18.6 %all-to-all-start.2 = ((f32[8,48,256]{2,1,0:T(8,128)}), f32[8,48,256]{2,1,0:T(8,128)S(1)}, u32[]{:S(2)}, u32[]{:S(2)}) async-start(f32[8,48,256]{2,1,0:T(8,128)} %broadcast_in_dim.58), calls=%async_computation.2 | async-start | bytes 786432 | tf_op jit(solution)/shard_map/all_to_all | solution.py:34
  130.1 8.6 %collective-permute-start.10 = (f32[32,256]{1,0:T(8,128)S(1)}, f32[32,256]{1,0:T(8,128)S(1)}, u32[]{:S(2)}, u32[]{:S(2)}) collective-permute-start(f32[32,256]{1,0:T(8,128)S(1)} %dynamic-slice_bitcast_fusion), channel_id=1, source_target_pairs={{0,2},{2,0},{1,3},{3,1},{4,6},{6,4},{5,7},{7,5},{8,10},{10,8},{9,1... | collective-permute-start | bytes 98312 | tf_op jit(solution)/shard_map/ppermute | solution.py:30
  143.2 15.0 %all-to-all-start.3 = ((f32[8,48,256]{2,1,0:T(8,128)}), f32[8,48,256]{2,1,0:T(8,128)S(1)}, u32[]{:S(2)}, u32[]{:S(2)}) async-start(f32[8,48,256]{2,1,0:T(8,128)} %broadcast_in_dim.59), calls=%async_computation.3 | async-start | bytes 786432 | tf_op jit(solution)/shard_map/all_to_all | solution.py:34
  147.5 6.4 %collective-permute-start.11 = (f32[32,256]{1,0:T(8,128)S(1)}, f32[32,256]{1,0:T(8,128)S(1)}, u32[]{:S(2)}, u32[]{:S(2)}) collective-permute-start(f32[32,256]{1,0:T(8,128)S(1)} %fusion.10), channel_id=1, source_target_pairs={{0,1},{1,0},{2,3},{3,2},{4,5},{5,4},{6,7},{7,6},{8,9},{9,8},{10,11... | collective-permute-start | bytes 98312 | tf_op jit(solution)/shard_map/ppermute | solution.py:30
  159.0 4.5 %copy-start.6 = (f32[256,256]{1,0:T(8,128)S(1)}, f32[256,256]{1,0:T(8,128)}, u32[]{:S(2)}) copy-start(f32[256,256]{1,0:T(8,128)} %param.12) | copy-start | bytes 786436
  159.0 4.5 %copy-start.7 = (f32[256,256]{1,0:T(8,128)S(1)}, f32[256,256]{1,0:T(8,128)}, u32[]{:S(2)}) copy-start(f32[256,256]{1,0:T(8,128)} %param.11) | copy-start | bytes 786436
  159.0 15.2 %all-to-all-start.4 = ((f32[8,48,256]{2,1,0:T(8,128)}), f32[8,48,256]{2,1,0:T(8,128)S(1)}, u32[]{:S(2)}, u32[]{:S(2)}) async-start(f32[8,48,256]{2,1,0:T(8,128)} %broadcast_in_dim.60), calls=%async_computation.4 | async-start | bytes 786432 | tf_op jit(solution)/shard_map/all_to_all | solution.py:34
  174.2 8.5 %collective-permute-start.12 = (f32[384,256]{1,0:T(8,128)S(1)}, f32[384,256]{1,0:T(8,128)S(1)}, u32[]{:S(2)}, u32[]{:S(2)}) collective-permute-start(f32[384,256]{1,0:T(8,128)S(1)} %bitcast.91), channel_id=1, source_target_pairs={{0,1},{1,0},{2,3},{3,2},{4,5},{5,4},{6,7},{7,6},{8,9},{9,8},{10,11... | collective-permute-start | bytes 1179656 | tf_op jit(solution)/shard_map/ppermute | solution.py:30
  181.5 0.8 copy-start.9
  182.9 0.7 copy-start.4
  183.6 0.7 copy-start.5

commit v8 on v4

--- a/solution.py
+++ b/solution.py
@@ -80,12 +80,15 @@
     for step in range(1, nx // 2):
         came = lax.ppermute(group, "x", [(i, i ^ (2 * step)) for i in range(nx)])
         rows = lax.dynamic_update_index_in_dim(rows, came, (place // 2) ^ step, 0)
-    rows = both(rows, lax.ppermute(rows, "x", [(i, i ^ 1) for i in range(nx)]), place % 2 == 0, 1)
+    near = lax.optimization_barrier(after(inverse_blocks, rows[0, 0]))
+    sent = after(rows, jnp.concatenate([panel[0, 0, :1]] * 2, axis=1))
+    came = lax.ppermute(sent, "x", [(i, i ^ 1) for i in range(nx)])
+    rows = both(rows, came, place % 2 == 0, 1)
     rows = both(rows, swap(rows, "core"), first, 3).reshape(-1, 2 * width)
     rows_two = rows[:, width:]
     rows_own = jnp.where(first, rows[:, :width], rows_two)
 
-    total = mm(inverse_blocks, own) + mm(blocks, other)
+    total = mm(near, own) + mm(blocks, other)
     came = swap(total[:, half:], "core")
     grams = jnp.concatenate(
         [
@@ -104,6 +107,9 @@
     col_two = jnp.where(first, sibling, column)
     column_one = pick(col_one.reshape(2, span, width), core)
     column_two = pick(col_two.reshape(2, span, width), core) - mm(column_one, link_block)
+
+    diag_one = lax.optimization_barrier(after(diag_one, column))
+    diag_two = lax.optimization_barrier(after(diag_two, column))
 
     grams = after(jnp.sum(gather(grams, "y"), axis=0), column)
     grams = after(jnp.sum(gather(grams, ("zh", "zl")), axis=0), sibling)

time: 183 us -> 195 us (1.066)
  waiting for transfers between devices: 37.8 us -> 56.7 us
  starting transfers between devices: 98.8 us -> 89.3 us
  blocking collectives: 27.6 us -> 33.1 us
  local copies, waits for them, and re-layouts: 8.58 us -> 6.41 us
    all_to_all x4, waiting for transfers between devices: 18.6 us -> 39.6 us  [exchange(): return lax.all_to_all(a, axes, 0, 0, tiled=True)]
    ppermute x7, starting transfers between devices: 46.6 us -> 40.6 us  [swap(): return lax.ppermute(a, axis, SWAP)]
    all_to_all x1, blocking collectives: 27.6 us -> 33.1 us  [exchange(): return lax.all_to_all(a, axes, 0, 0, tiled=True)]
    all_to_all x4, starting transfers between devices: 27.9 us -> 25.2 us  [exchange(): return lax.all_to_all(a, axes, 0, 0, tiled=True)]
    ppermute x1, waiting for transfers between devices: 5.75 us -> 3.66 us  [local(): came = lax.ppermute(sent, 'x', [(i, i ^ 1) for i in range(nx)])]
  transfers between devices with their start and end apart: 17 -> 17, of which waited for: 11 -> 10; matrix products, arithmetic and copies ran while one was open for 3% -> 3% of each run, Pallas kernels for 0% -> 0%
where the time goes in v8:
time: 195 us; the launch traced here: 194 us
  starting transfers between devices  89.3 us (46%)
  waiting for transfers between devices  56.7 us (29%)
  blocking collectives  33.1 us (17%)
  local copies, waits for them, and re-layouts  6.41 us (3%)
  matrix products  4.76 us (2%)
  other arithmetic  2.3 us (1%)
    ppermute x7, starting transfers between devices, swap(): return lax.ppermute(a, axis, SWAP)  40.6 us
    all_to_all x4, waiting for transfers between devices, exchange(): return lax.all_to_all(a, axes, 0, 0, tiled=True)  39.6 us
    all_to_all x1, blocking collectives, exchange(): return lax.all_to_all(a, axes, 0, 0, tiled=True)  33.1 us
    all_to_all x4, starting transfers between devices, exchange(): return lax.all_to_all(a, axes, 0, 0, tiled=True)  25.2 us
    ppermute x3, starting transfers between devices, local(): came = lax.ppermute(group, 'x', [(i, i ^ 2 * step) for i in range(nx)])  13 us
    ppermute x7, waiting for transfers between devices, swap(): return lax.ppermute(a, axis, SWAP)  9.01 us
    ppermute x1, starting transfers between devices, local(): came = lax.ppermute(sent, 'x', [(i, i ^ 1) for i in range(nx)])  5.03 us
    dot_general x8, matrix products, mm(): lax.dot_general(a, b, (dims, ((), ())), precision=lax.Precision.HIGH, pre...  4.76 us
  transfers between devices with their start and end apart: 17, of which 10 were waited for; matrix products, arithmetic and copies ran while one was open for 3% of the time, Pallas kernels for 0%

profile of v8, /device:TPU:1, one launch (start us, length us, event | category | flops | bytes accessed | tf_op | source)
XLA Modules:
  0.0 193.9 jit_solution(14300180749387369354)
XLA Ops:
  0.6 0.0 copy-start
  0.6 16.2 %collective-permute-start.1 = (f32[512,512]{1,0:T(8,128)}, f32[512,512]{1,0:T(8,128)S(1)}, u32[]{:S(2)}, u32[]{:S(2)}) collective-permute-start(f32[512,512]{1,0:T(8,128)} %param.7), channel_id=1, source_target_pairs={{0,1},{1,0},{2,3},{3,2},{4,5},{5,4},{6,7},{7,6},{8,9},{9,8},{10,11... | collective-permute-start | bytes 3145736 | tf_op jit(solution)/shard_map/ppermute | solution.py:30
  16.9 0.7 copy-done.11
  17.6 0.1 fusion.15
  17.6 0.5 fusion.18
  18.2 0.2 copy-done.9
  18.4 0.0 copy-done.10
  18.4 1.3 broadcast_select_fusion.7
  19.7 1.9 collective-permute-start.6
  21.6 3.5 %collective-permute-start.5 = (f32[16,256]{1,0:T(8,128)S(1)}, f32[16,256]{1,0:T(8,128)S(1)}, u32[]{:S(2)}, u32[]{:S(2)}) collective-permute-start(f32[16,256]{1,0:T(8,128)S(1)} %get-tuple-element.5), channel_id=1, source_target_pairs={{0,0},{1,32},{2,64},{3,96},{4,128},{5,160},{6,192},{7,224},{8,256}... | collective-permute-start | bytes 49160 | tf_op jit(solution)/shard_map/ppermute | solution.py:67
  25.2 8.2 %collective-permute-start = (f32[16,512]{1,0:T(8,128)S(1)}, f32[16,512]{1,0:T(8,128)S(1)}, u32[]{:S(2)}, u32[]{:S(2)}) collective-permute-start(f32[16,512]{1,0:T(8,128)S(1)} %pad_maximum_fusion.6), channel_id=1, source_target_pairs={{0,2},{2,0},{1,3},{3,1},{4,6},{6,4},{5,7},{7,5},{8,10},{10,8},{9,1... | collective-permute-start | bytes 98312 | tf_op jit(solution)/shard_map/ppermute | solution.py:30
  33.5 0.0 collective-permute-done.6
  33.5 0.0 collective-permute-done.5
  33.5 1.1 broadcast_in_dim.44
  34.6 13.0 %all-to-all-start = ((f32[32,2,16,256]{3,2,1,0:T(8,128)}), f32[32,2,16,256]{3,2,1,0:T(8,128)S(1)}, u32[]{:S(2)}, u32[]{:S(2)}) async-start(f32[32,2,16,256]{3,2,1,0:T(8,128)} %broadcast_in_dim.44), calls=%async_computation | async-start | bytes 2097152 | tf_op jit(solution)/shard_map/all_to_all | solution.py:34
  47.6 0.0 copy-start.3
  47.6 0.0 collective-permute-done
  47.7 6.8 %collective-permute-start.4 = (f32[2,16,512]{2,1,0:T(8,128)S(1)}, f32[2,16,512]{2,1,0:T(8,128)S(1)}, u32[]{:S(2)}, u32[]{:S(2)}) collective-permute-start(f32[2,16,512]{2,1,0:T(8,128)S(1)} %maximum_add_fusion.1), channel_id=1, source_target_pairs={{0,24},{4,28},{8,16},{12,20},{16,8},{20,12},{24,0},{28,4},{1,25},{... | collective-permute-start | bytes 196616 | tf_op jit(solution)/shard_map/ppermute | solution.py:81
  54.5 4.3 %collective-permute-start.3 = (f32[2,16,512]{2,1,0:T(8,128)S(1)}, f32[2,16,512]{2,1,0:T(8,128)S(1)}, u32[]{:S(2)}, u32[]{:S(2)}) collective-permute-start(f32[2,16,512]{2,1,0:T(8,128)S(1)} %maximum_add_fusion.1), channel_id=1, source_target_pairs={{0,16},{4,20},{8,24},{12,28},{16,0},{20,4},{24,8},{28,12},{1,17},{... | collective-permute-start | bytes 196616 | tf_op jit(solution)/shard_map/ppermute | solution.py:81
  58.8 1.9 collective-permute-start.2
  60.8 4.4 %collective-permute-done.2 = f32[2,16,512]{2,1,0:T(8,128)S(1)} collective-permute-done((f32[2,16,512]{2,1,0:T(8,128)S(1)}, f32[2,16,512]{2,1,0:T(8,128)S(1)}, u32[]{:S(2)}, u32[]{:S(2)}) %collective-permute-start.2) | collective-permute-done | bytes 65568 | tf_op jit(solution)/shard_map/ppermute | solution.py:81
  65.2 0.0 collective-permute-done.3
  65.3 0.1 broadcast_add_fusion
  65.4 8.1 %all-to-all-done = f32[32,2,16,256]{3,2,1,0:T(8,128)S(1)} async-done(((f32[32,2,16,256]{3,2,1,0:T(8,128)}), f32[32,2,16,256]{3,2,1,0:T(8,128)S(1)}, u32[]{:S(2)}, u32[]{:S(2)}) %all-to-all-start) | async-done | bytes 1048608 | tf_op jit(solution)/shard_map/all_to_all | solution.py:34
  73.6 5.0 %collective-permute-start.7 = (f32[4,2,16,512]{3,2,1,0:T(8,128)S(1)}, f32[4,2,16,512]{3,2,1,0:T(8,128)S(1)}, u32[]{:S(2)}, u32[]{:S(2)}) collective-permute-start(f32[4,2,16,512]{3,2,1,0:T(8,128)S(1)} %broadcast_add_fusion.3), channel_id=1, source_target_pairs={{0,4},{4,0},{8,12},{12,8},{16,20},{20,16},{24,28},{28,24},{1,5},{5... | collective-permute-start | bytes 786440 | tf_op jit(solution)/shard_map/ppermute | solution.py:85
  78.6 0.1 fusion.17
  78.7 3.7 %collective-permute-done.7 = f32[4,2,16,512]{3,2,1,0:T(8,128)S(1)} collective-permute-done((f32[4,2,16,512]{3,2,1,0:T(8,128)S(1)}, f32[4,2,16,512]{3,2,1,0:T(8,128)S(1)}, u32[]{:S(2)}, u32[]{:S(2)}) %collective-permute-start.7) | collective-permute-done | bytes 262176 | tf_op jit(solution)/shard_map/ppermute | solution.py:85
  82.5 6.8 %collective-permute-start.8 = (f32[4,2,2,16,512]{4,3,2,1,0:T(8,128)S(1)}, f32[4,2,2,16,512]{4,3,2,1,0:T(8,128)S(1)}, u32[]{:S(2)}, u32[]{:S(2)}) collective-permute-start(f32[4,2,2,16,512]{4,3,2,1,0:T(8,128)S(1)} %pad_maximum_fusion.2), channel_id=1, source_target_pairs={{0,1},{1,0},{2,3},{3,2},{4,5},{5,4},{6,7},{7,6},{8,9},{9,8},{10,11... | collective-permute-start | bytes 1572872 | tf_op jit(solution)/shard_map/ppermute | solution.py:30
  89.3 0.6 fusion.19
  89.9 0.6 copy-done.2
  90.5 0.6 fusion
  91.1 1.9 collective-permute-start.9
  93.0 0.1 select_bitcast_fusion.1
  93.2 0.1 pad_maximum_fusion
  93.3 0.6 fusion.3
  93.9 0.6 collective-permute-done.9
  94.5 0.4 fusion.4
  95.0 0.1 pad_maximum_fusion.1
  95.1 33.1 %all_to_all.25 = f32[8,112,256]{2,1,0:T(8,128)S(1)} all-to-all(f32[8,112,256]{2,1,0:T(8,128)S(1)} %pad_maximum_fusion.1), channel_id=1, replica_groups=mesh['zl'=4,'y'=8,'x'=8,'zh'=2,'core'=2] {'x'}, dimensions={0} | all-to-all | bytes 1835008 | tf_op jit(solution)/shard_map/all_to_all | solution.py:34
  128.2 0.1 reduce_sum.27
  128.2 0.8 broadcast_in_dim.45
  129.0 5.2 %all-to-all-start.2 = ((f32[8,48,256]{2,1,0:T(8,128)}), f32[8,48,256]{2,1,0:T(8,128)S(1)}, u32[]{:S(2)}, u32[]{:S(2)}) async-start(f32[8,48,256]{2,1,0:T(8,128)} %broadcast_in_dim.45), calls=%async_computation.2 | async-start | bytes 786432 | tf_op jit(solution)/shard_map/all_to_all | solution.py:34
  134.2 1.9 collective-permute-start.10
  136.1 7.1 %collective-permute-done.10 = f32[32,256]{1,0:T(8,128)S(1)} collective-permute-done((f32[32,256]{1,0:T(8,128)S(1)}, f32[32,256]{1,0:T(8,128)S(1)}, u32[]{:S(2)}, u32[]{:S(2)}) %collective-permute-start.10) | collective-permute-done | bytes 32800 | tf_op jit(solution)/shard_map/ppermute | solution.py:30
  143.2 5.8 %all-to-all-done.2 = f32[8,48,256]{2,1,0:T(8,128)S(1)} async-done(((f32[8,48,256]{2,1,0:T(8,128)}), f32[8,48,256]{2,1,0:T(8,128)S(1)}, u32[]{:S(2)}, u32[]{:S(2)}) %all-to-all-start.2) | async-done | bytes 393248 | tf_op jit(solution)/shard_map/all_to_all | solution.py:34
  149.0 0.8 broadcast_in_dim.46
  149.8 3.5 %all-to-all-start.3 = ((f32[8,48,256]{2,1,0:T(8,128)}), f32[8,48,256]{2,1,0:T(8,128)S(1)}, u32[]{:S(2)}, u32[]{:S(2)}) async-start(f32[8,48,256]{2,1,0:T(8,128)} %broadcast_in_dim.46), calls=%async_computation.3 | async-start | bytes 786432 | tf_op jit(solution)/shard_map/all_to_all | solution.py:34
  153.3 2.7 %collective-permute-start.11 = (f32[32,256]{1,0:T(8,128)S(1)}, f32[32,256]{1,0:T(8,128)S(1)}, u32[]{:S(2)}, u32[]{:S(2)}) collective-permute-start(f32[32,256]{1,0:T(8,128)S(1)} %fusion.10), channel_id=1, source_target_pairs={{0,1},{1,0},{2,3},{3,2},{4,5},{5,4},{6,7},{7,6},{8,9},{9,8},{10,11... | collective-permute-start | bytes 98312 | tf_op jit(solution)/shard_map/ppermute | solution.py:30
  156.0 0.8 collective-permute-done.11
  156.8 11.2 %all-to-all-done.3 = f32[8,48,256]{2,1,0:T(8,128)S(1)} async-done(((f32[8,48,256]{2,1,0:T(8,128)}), f32[8,48,256]{2,1,0:T(8,128)S(1)}, u32[]{:S(2)}, u32[]{:S(2)}) %all-to-all-start.3) | async-done | bytes 393248 | tf_op jit(solution)/shard_map/all_to_all | solution.py:34
  168.1 0.8 broadcast_in_dim.47
  168.8 3.6 %all-to-all-start.4 = ((f32[8,48,256]{2,1,0:T(8,128)}), f32[8,48,256]{2,1,0:T(8,128)S(1)}, u32[]{:S(2)}, u32[]{:S(2)}) async-start(f32[8,48,256]{2,1,0:T(8,128)} %broadcast_in_dim.47), calls=%async_computation.4 | async-start | bytes 786432 | tf_op jit(solution)/shard_map/all_to_all | solution.py:34
  172.5 14.6 %all-to-all-done.4 = f32[8,48,256]{2,1,0:T(8,128)S(1)} async-done(((f32[8,48,256]{2,1,0:T(8,128)}), f32[8,48,256]{2,1,0:T(8,128)S(1)}, u32[]{:S(2)}, u32[]{:S(2)}) %all-to-all-start.4) | async-done | bytes 393248 | tf_op jit(solution)/shard_map/all_to_all | solution.py:34
  187.0 2.8 %collective-permute-start.12 = (f32[384,256]{1,0:T(8,128)S(1)}, f32[384,256]{1,0:T(8,128)S(1)}, u32[]{:S(2)}, u32[]{:S(2)}) collective-permute-start(f32[384,256]{1,0:T(8,128)S(1)} %bitcast.80), channel_id=1, source_target_pairs={{0,1},{1,0},{2,3},{3,2},{4,5},{5,4},{6,7},{7,6},{8,9},{9,8},{10,11... | collective-permute-start | bytes 1179656 | tf_op jit(solution)/shard_map/ppermute | solution.py:30
  189.9 0.0 copy-start.8
  189.9 0.8 bitcast_subtract_fusion
  190.7 0.5 collective-permute-done.12
  191.2 0.1 broadcast_select_fusion
  191.4 0.0 copy-start.4
  191.4 0.3 convolution_subtract_fusion.1
  191.6 0.4 copy-done.4
  192.1 0.4 convolution_bitcast_fusion.1
  192.5 0.3 copy-done.5
  192.8 1.1 fusion.2
  (52 shorter events, 0.5 us)
Async XLA Ops:
  0.6 189.3 %copy-start = (f32[256,256]{1,0:T(8,128)S(1)}, f32[256,256]{1,0:T(8,128)}, u32[]{:S(2)}) copy-start(f32[256,256]{1,0:T(8,128)} %param.13) | copy-start | bytes 786436
  0.6 47.0 %collective-permute-start.1 = (f32[512,512]{1,0:T(8,128)}, f32[512,512]{1,0:T(8,128)S(1)}, u32[]{:S(2)}, u32[]{:S(2)}) collective-permute-start(f32[512,512]{1,0:T(8,128)} %param.7), channel_id=1, source_target_pairs={{0,1},{1,0},{2,3},{3,2},{4,5},{5,4},{6,7},{7,6},{8,9},{9,8},{10,11... | collective-permute-start | bytes 3145736 | tf_op jit(solution)/shard_map/ppermute | solution.py:30
  16.9 0.7 copy-start.11
  17.6 0.7 copy-start.9
  17.6 0.7 copy-start.10
  19.7 13.8 %collective-permute-start.6 = (f32[16,256]{1,0:T(8,128)S(1)}, f32[16,256]{1,0:T(8,128)S(1)}, u32[]{:S(2)}, u32[]{:S(2)}) collective-permute-start(f32[16,256]{1,0:T(8,128)S(1)} %broadcast_select_fusion.6), channel_id=1, source_target_pairs={{0,1},{1,33},{2,65},{3,97},{4,129},{5,161},{6,193},{7,225},{8,257}... | collective-permute-start | bytes 49160 | tf_op jit(solution)/shard_map/ppermute | solution.py:68
  21.6 11.9 %collective-permute-start.5 = (f32[16,256]{1,0:T(8,128)S(1)}, f32[16,256]{1,0:T(8,128)S(1)}, u32[]{:S(2)}, u32[]{:S(2)}) collective-permute-start(f32[16,256]{1,0:T(8,128)S(1)} %get-tuple-element.5), channel_id=1, source_target_pairs={{0,0},{1,32},{2,64},{3,96},{4,128},{5,160},{6,192},{7,224},{8,256}... | collective-permute-start | bytes 49160 | tf_op jit(solution)/shard_map/ppermute | solution.py:67
  25.2 22.4 %collective-permute-start = (f32[16,512]{1,0:T(8,128)S(1)}, f32[16,512]{1,0:T(8,128)S(1)}, u32[]{:S(2)}, u32[]{:S(2)}) collective-permute-start(f32[16,512]{1,0:T(8,128)S(1)} %pad_maximum_fusion.6), channel_id=1, source_target_pairs={{0,2},{2,0},{1,3},{3,1},{4,6},{6,4},{5,7},{7,5},{8,10},{10,8},{9,1... | collective-permute-start | bytes 98312 | tf_op jit(solution)/shard_map/ppermute | solution.py:30
  34.6 38.9 %all-to-all-start = ((f32[32,2,16,256]{3,2,1,0:T(8,128)}), f32[32,2,16,256]{3,2,1,0:T(8,128)S(1)}, u32[]{:S(2)}, u32[]{:S(2)}) async-start(f32[32,2,16,256]{3,2,1,0:T(8,128)} %broadcast_in_dim.44), calls=%async_computation | async-start | bytes 2097152 | tf_op jit(solution)/shard_map/all_to_all | solution.py:34
  47.6 17.7 %copy-start.3 = (f32[512,512]{1,0:T(8,128)S(1)}, f32[512,512]{1,0:T(8,128)}, u32[]{:S(2)}) copy-start(f32[512,512]{1,0:T(8,128)} %param.7) | copy-start | bytes 3145732
  47.7 17.6 %copy-start.1 = (f32[512,512]{1,0:T(8,128)}, f32[512,512]{1,0:T(8,128)S(1)}, u32[]{:S(2)}) copy-start(f32[512,512]{1,0:T(8,128)S(1)} %collective-permute-done.1) | copy-start | bytes 3145732
  47.7 17.5 %collective-permute-start.4 = (f32[2,16,512]{2,1,0:T(8,128)S(1)}, f32[2,16,512]{2,1,0:T(8,128)S(1)}, u32[]{:S(2)}, u32[]{:S(2)}) collective-permute-start(f32[2,16,512]{2,1,0:T(8,128)S(1)} %maximum_add_fusion.1), channel_id=1, source_target_pairs={{0,24},{4,28},{8,16},{12,20},{16,8},{20,12},{24,0},{28,4},{1,25},{... | collective-permute-start | bytes 196616 | tf_op jit(solution)/shard_map/ppermute | solution.py:81
  54.5 10.7 %collective-permute-start.3 = (f32[2,16,512]{2,1,0:T(8,128)S(1)}, f32[2,16,512]{2,1,0:T(8,128)S(1)}, u32[]{:S(2)}, u32[]{:S(2)}) collective-permute-start(f32[2,16,512]{2,1,0:T(8,128)S(1)} %maximum_add_fusion.1), channel_id=1, source_target_pairs={{0,16},{4,20},{8,24},{12,28},{16,0},{20,4},{24,8},{28,12},{1,17},{... | collective-permute-start | bytes 196616 | tf_op jit(solution)/shard_map/ppermute | solution.py:81
  58.8 6.4 %collective-permute-start.2 = (f32[2,16,512]{2,1,0:T(8,128)S(1)}, f32[2,16,512]{2,1,0:T(8,128)S(1)}, u32[]{:S(2)}, u32[]{:S(2)}) collective-permute-start(f32[2,16,512]{2,1,0:T(8,128)S(1)} %maximum_add_fusion.1), channel_id=1, source_target_pairs={{0,8},{4,12},{8,0},{12,4},{16,24},{20,28},{24,16},{28,20},{1,9},{5... | collective-permute-start | bytes 196616 | tf_op jit(solution)/shard_map/ppermute | solution.py:81
  73.6 8.8 %collective-permute-start.7 = (f32[4,2,16,512]{3,2,1,0:T(8,128)S(1)}, f32[4,2,16,512]{3,2,1,0:T(8,128)S(1)}, u32[]{:S(2)}, u32[]{:S(2)}) collective-permute-start(f32[4,2,16,512]{3,2,1,0:T(8,128)S(1)} %broadcast_add_fusion.3), channel_id=1, source_target_pairs={{0,4},{4,0},{8,12},{12,8},{16,20},{20,16},{24,28},{28,24},{1,5},{5... | collective-permute-start | bytes 786440 | tf_op jit(solution)/shard_map/ppermute | solution.py:85
  82.5 10.6 %collective-permute-start.8 = (f32[4,2,2,16,512]{4,3,2,1,0:T(8,128)S(1)}, f32[4,2,2,16,512]{4,3,2,1,0:T(8,128)S(1)}, u32[]{:S(2)}, u32[]{:S(2)}) collective-permute-start(f32[4,2,2,16,512]{4,3,2,1,0:T(8,128)S(1)} %pad_maximum_fusion.2), channel_id=1, source_target_pairs={{0,1},{1,0},{2,3},{3,2},{4,5},{5,4},{6,7},{7,6},{8,9},{9,8},{10,11... | collective-permute-start | bytes 1572872 | tf_op jit(solution)/shard_map/ppermute | solution.py:30
  89.3 1.2 copy-start.2
  91.1 3.4 %collective-permute-start.9 = (f32[512,128]{1,0:T(8,128)S(1)}, f32[512,128]{1,0:T(8,128)S(1)}, u32[]{:S(2)}, u32[]{:S(2)}) collective-permute-start(f32[512,128]{1,0:T(8,128)S(1)} %slice.89), channel_id=1, source_target_pairs={{0,1},{1,0},{2,3},{3,2},{4,5},{5,4},{6,7},{7,6},{8,9},{9,8},{10,11... | collective-permute-start | bytes 786440 | tf_op jit(solution)/shard_map/ppermute | solution.py:30
  129.0 20.0 %all-to-all-start.2 = ((f32[8,48,256]{2,1,0:T(8,128)}), f32[8,48,256]{2,1,0:T(8,128)S(1)}, u32[]{:S(2)}, u32[]{:S(2)}) async-start(f32[8,48,256]{2,1,0:T(8,128)} %broadcast_in_dim.45), calls=%async_computation.2 | async-start | bytes 786432 | tf_op jit(solution)/shard_map/all_to_all | solution.py:34
  134.2 9.0 %collective-permute-start.10 = (f32[32,256]{1,0:T(8,128)S(1)}, f32[32,256]{1,0:T(8,128)S(1)}, u32[]{:S(2)}, u32[]{:S(2)}) collective-permute-start(f32[32,256]{1,0:T(8,128)S(1)} %dynamic-slice_bitcast_fusion), channel_id=1, source_target_pairs={{0,2},{2,0},{1,3},{3,1},{4,6},{6,4},{5,7},{7,5},{8,10},{10,8},{9,1... | collective-permute-start | bytes 98312 | tf_op jit(solution)/shard_map/ppermute | solution.py:30
  149.8 18.2 %all-to-all-start.3 = ((f32[8,48,256]{2,1,0:T(8,128)}), f32[8,48,256]{2,1,0:T(8,128)S(1)}, u32[]{:S(2)}, u32[]{:S(2)}) async-start(f32[8,48,256]{2,1,0:T(8,128)} %broadcast_in_dim.46), calls=%async_computation.3 | async-start | bytes 786432 | tf_op jit(solution)/shard_map/all_to_all | solution.py:34
  153.3 3.6 %collective-permute-start.11 = (f32[32,256]{1,0:T(8,128)S(1)}, f32[32,256]{1,0:T(8,128)S(1)}, u32[]{:S(2)}, u32[]{:S(2)}) collective-permute-start(f32[32,256]{1,0:T(8,128)S(1)} %fusion.10), channel_id=1, source_target_pairs={{0,1},{1,0},{2,3},{3,2},{4,5},{5,4},{6,7},{7,6},{8,9},{9,8},{10,11... | collective-permute-start | bytes 98312 | tf_op jit(solution)/shard_map/ppermute | solution.py:30
  168.8 3.6 %copy-start.6 = (f32[256,256]{1,0:T(8,128)S(1)}, f32[256,256]{1,0:T(8,128)}, u32[]{:S(2)}) copy-start(f32[256,256]{1,0:T(8,128)} %param.12) | copy-start | bytes 786436
  168.8 3.6 %copy-start.7 = (f32[256,256]{1,0:T(8,128)S(1)}, f32[256,256]{1,0:T(8,128)}, u32[]{:S(2)}) copy-start(f32[256,256]{1,0:T(8,128)} %param.11) | copy-start | bytes 786436
  168.8 18.2 %all-to-all-start.4 = ((f32[8,48,256]{2,1,0:T(8,128)}), f32[8,48,256]{2,1,0:T(8,128)S(1)}, u32[]{:S(2)}, u32[]{:S(2)}) async-start(f32[8,48,256]{2,1,0:T(8,128)} %broadcast_in_dim.47), calls=%async_computation.4 | async-start | bytes 786432 | tf_op jit(solution)/shard_map/all_to_all | solution.py:34
  187.0 4.2 %collective-permute-start.12 = (f32[384,256]{1,0:T(8,128)S(1)}, f32[384,256]{1,0:T(8,128)S(1)}, u32[]{:S(2)}, u32[]{:S(2)}) collective-permute-start(f32[384,256]{1,0:T(8,128)S(1)} %bitcast.80), channel_id=1, source_target_pairs={{0,1},{1,0},{2,3},{3,2},{4,5},{5,4},{6,7},{7,6},{8,9},{9,8},{10,11... | collective-permute-start | bytes 1179656 | tf_op jit(solution)/shard_map/ppermute | solution.py:30
  189.9 0.8 copy-start.8
  191.4 0.7 copy-start.4
  192.1 0.7 copy-start.5

commit v9 on v8

--- a/solution.py
+++ b/solution.py
@@ -81,9 +81,7 @@
         came = lax.ppermute(group, "x", [(i, i ^ (2 * step)) for i in range(nx)])
         rows = lax.dynamic_update_index_in_dim(rows, came, (place // 2) ^ step, 0)
     near = lax.optimization_barrier(after(inverse_blocks, rows[0, 0]))
-    sent = after(rows, jnp.concatenate([panel[0, 0, :1]] * 2, axis=1))
-    came = lax.ppermute(sent, "x", [(i, i ^ 1) for i in range(nx)])
-    rows = both(rows, came, place % 2 == 0, 1)
+    rows = both(rows, lax.ppermute(rows, "x", [(i, i ^ 1) for i in range(nx)]), place % 2 == 0, 1)
     rows = both(rows, swap(rows, "core"), first, 3).reshape(-1, 2 * width)
     rows_two = rows[:, width:]
     rows_own = jnp.where(first, rows[:, :width], rows_two)

time: 195 us -> 183 us (0.938)
  waiting for transfers between devices: 56.7 us -> 36.9 us
  starting transfers between devices: 89.3 us -> 99 us
  blocking collectives: 33.1 us -> 27.6 us
  other arithmetic: 2.3 us -> 6.13 us
    all_to_all x4, waiting for transfers between devices: 39.6 us -> 18.5 us  [exchange(): return lax.all_to_all(a, axes, 0, 0, tiled=True)]
    ppermute x7, starting transfers between devices: 40.6 us -> 46.7 us  [swap(): return lax.ppermute(a, axis, SWAP)]
    all_to_all x1, blocking collectives: 33.1 us -> 27.6 us  [exchange(): return lax.all_to_all(a, axes, 0, 0, tiled=True)]
    all_to_all x4, starting transfers between devices: 25.2 us -> 28 us  [exchange(): return lax.all_to_all(a, axes, 0, 0, tiled=True)]
    another operation x4, other arithmetic: 0.32 us -> 2.96 us  [both(): jnp.stack([jnp.where(ahead, mine, came), jnp.where(ahead, came, mine)], a...]
    ppermute x1, waiting for transfers between devices: 3.66 us -> 5.76 us  [local(): lax.ppermute(rows, 'x', [(i, i ^ 1) for i in range(nx)])]
  transfers between devices with their start and end apart: 17 -> 17, of which waited for: 10 -> 11; matrix products, arithmetic and copies ran while one was open for 3% -> 5% of each run, Pallas kernels for 0% -> 0%
where the time goes in v9:
time: 183 us; the launch traced here: 182 us
  starting transfers between devices  99 us (54%)
  waiting for transfers between devices  36.9 us (20%)
  blocking collectives  27.6 us (15%)
  local copies, waits for them, and re-layouts  6.39 us (3%)
  other arithmetic  6.13 us (3%)
  matrix products  4.77 us (3%)
    ppermute x7, starting transfers between devices, swap(): return lax.ppermute(a, axis, SWAP)  46.7 us
    all_to_all x4, starting transfers between devices, exchange(): return lax.all_to_all(a, axes, 0, 0, tiled=True)  28 us
    all_to_all x1, blocking collectives, exchange(): return lax.all_to_all(a, axes, 0, 0, tiled=True)  27.6 us
    all_to_all x4, waiting for transfers between devices, exchange(): return lax.all_to_all(a, axes, 0, 0, tiled=True)  18.5 us
    ppermute x3, starting transfers between devices, local(): came = lax.ppermute(group, 'x', [(i, i ^ 2 * step) for i in range(nx)])  12.9 us
    ppermute x7, waiting for transfers between devices, swap(): return lax.ppermute(a, axis, SWAP)  7.12 us
    ppermute x1, starting transfers between devices, local(): lax.ppermute(rows, 'x', [(i, i ^ 1) for i in range(nx)])  5.93 us
    ppermute x1, waiting for transfers between devices, local(): lax.ppermute(rows, 'x', [(i, i ^ 1) for i in range(nx)])  5.76 us
  transfers between devices with their start and end apart: 17, of which 11 were waited for; matrix products, arithmetic and copies ran while one was open for 5% of the time, Pallas kernels for 0%

profile of v9, /device:TPU:1, one launch (start us, length us, event | category | flops | bytes accessed | tf_op | source)
XLA Modules:
  0.0 182.2 jit_solution(5344425986342293614)
XLA Ops:
  0.6 0.0 copy-start
  0.6 16.2 %collective-permute-start.1 = (f32[512,512]{1,0:T(8,128)}, f32[512,512]{1,0:T(8,128)S(1)}, u32[]{:S(2)}, u32[]{:S(2)}) collective-permute-start(f32[512,512]{1,0:T(8,128)} %param.7), channel_id=1, source_target_pairs={{0,1},{1,0},{2,3},{3,2},{4,5},{5,4},{6,7},{7,6},{8,9},{9,8},{10,11... | collective-permute-start | bytes 3145736 | tf_op jit(solution)/shard_map/ppermute | solution.py:30
  16.9 0.7 copy-done.11
  17.6 0.1 fusion.15
  17.6 0.5 fusion.18
  18.2 0.2 copy-done.9
  18.4 0.0 copy-done.10
  18.4 1.3 broadcast_select_fusion.7
  19.7 1.9 %collective-permute-start.6 = (f32[16,256]{1,0:T(8,128)S(1)}, f32[16,256]{1,0:T(8,128)S(1)}, u32[]{:S(2)}, u32[]{:S(2)}) collective-permute-start(f32[16,256]{1,0:T(8,128)S(1)} %broadcast_select_fusion.6), channel_id=1, source_target_pairs={{0,1},{1,33},{2,65},{3,97},{4,129},{5,161},{6,193},{7,225},{8,257}... | collective-permute-start | bytes 49160 | tf_op jit(solution)/shard_map/ppermute | solution.py:68
  21.6 3.5 %collective-permute-start.5 = (f32[16,256]{1,0:T(8,128)S(1)}, f32[16,256]{1,0:T(8,128)S(1)}, u32[]{:S(2)}, u32[]{:S(2)}) collective-permute-start(f32[16,256]{1,0:T(8,128)S(1)} %get-tuple-element.5), channel_id=1, source_target_pairs={{0,0},{1,32},{2,64},{3,96},{4,128},{5,160},{6,192},{7,224},{8,256}... | collective-permute-start | bytes 49160 | tf_op jit(solution)/shard_map/ppermute | solution.py:67
  25.2 8.2 %collective-permute-start = (f32[16,512]{1,0:T(8,128)S(1)}, f32[16,512]{1,0:T(8,128)S(1)}, u32[]{:S(2)}, u32[]{:S(2)}) collective-permute-start(f32[16,512]{1,0:T(8,128)S(1)} %pad_maximum_fusion.6), channel_id=1, source_target_pairs={{0,2},{2,0},{1,3},{3,1},{4,6},{6,4},{5,7},{7,5},{8,10},{10,8},{9,1... | collective-permute-start | bytes 98312 | tf_op jit(solution)/shard_map/ppermute | solution.py:30
  33.5 0.0 collective-permute-done.6
  33.5 0.0 collective-permute-done.5
  33.5 1.1 broadcast_in_dim.43
  34.6 13.0 %all-to-all-start = ((f32[32,2,16,256]{3,2,1,0:T(8,128)}), f32[32,2,16,256]{3,2,1,0:T(8,128)S(1)}, u32[]{:S(2)}, u32[]{:S(2)}) async-start(f32[32,2,16,256]{3,2,1,0:T(8,128)} %broadcast_in_dim.43), calls=%async_computation | async-start | bytes 2097152 | tf_op jit(solution)/shard_map/all_to_all | solution.py:34
  47.6 0.0 collective-permute-done
  47.7 5.8 %collective-permute-start.2 = (f32[2,16,512]{2,1,0:T(8,128)S(1)}, f32[2,16,512]{2,1,0:T(8,128)S(1)}, u32[]{:S(2)}, u32[]{:S(2)}) collective-permute-start(f32[2,16,512]{2,1,0:T(8,128)S(1)} %maximum_add_fusion.1), channel_id=1, source_target_pairs={{0,8},{4,12},{8,0},{12,4},{16,24},{20,28},{24,16},{28,20},{1,9},{5... | collective-permute-start | bytes 196616 | tf_op jit(solution)/shard_map/ppermute | solution.py:81
  53.5 4.9 %collective-permute-start.3 = (f32[2,16,512]{2,1,0:T(8,128)S(1)}, f32[2,16,512]{2,1,0:T(8,128)S(1)}, u32[]{:S(2)}, u32[]{:S(2)}) collective-permute-start(f32[2,16,512]{2,1,0:T(8,128)S(1)} %maximum_add_fusion.1), channel_id=1, source_target_pairs={{0,16},{4,20},{8,24},{12,28},{16,0},{20,4},{24,8},{28,12},{1,17},{... | collective-permute-start | bytes 196616 | tf_op jit(solution)/shard_map/ppermute | solution.py:81
  58.3 2.2 %collective-permute-start.4 = (f32[2,16,512]{2,1,0:T(8,128)S(1)}, f32[2,16,512]{2,1,0:T(8,128)S(1)}, u32[]{:S(2)}, u32[]{:S(2)}) collective-permute-start(f32[2,16,512]{2,1,0:T(8,128)S(1)} %maximum_add_fusion.1), channel_id=1, source_target_pairs={{0,24},{4,28},{8,16},{12,20},{16,8},{20,12},{24,0},{28,4},{1,25},{... | collective-permute-start | bytes 196616 | tf_op jit(solution)/shard_map/ppermute | solution.py:81
  60.7 1.7 collective-permute-done.3
  62.4 3.9 %collective-permute-done.4 = f32[2,16,512]{2,1,0:T(8,128)S(1)} collective-permute-done((f32[2,16,512]{2,1,0:T(8,128)S(1)}, f32[2,16,512]{2,1,0:T(8,128)S(1)}, u32[]{:S(2)}, u32[]{:S(2)}) %collective-permute-start.4) | collective-permute-done | bytes 65568 | tf_op jit(solution)/shard_map/ppermute | solution.py:81
  66.3 5.9 %collective-permute-start.7 = (f32[4,2,16,512]{3,2,1,0:T(8,128)S(1)}, f32[4,2,16,512]{3,2,1,0:T(8,128)S(1)}, u32[]{:S(2)}, u32[]{:S(2)}) collective-permute-start(f32[4,2,16,512]{3,2,1,0:T(8,128)S(1)} %bitcast_dynamic-update-slice_fusion), channel_id=1, source_target_pairs={{0,4},{4,0},{8,12},{12,8},{16,20},{20,16},{24,28},{28,24},{1,5},{5... | collective-permute-start | bytes 786440 | tf_op jit(solution)/shard_map/ppermute | solution.py:84
  72.2 5.8 %collective-permute-done.7 = f32[4,2,16,512]{3,2,1,0:T(8,128)S(1)} collective-permute-done((f32[4,2,16,512]{3,2,1,0:T(8,128)S(1)}, f32[4,2,16,512]{3,2,1,0:T(8,128)S(1)}, u32[]{:S(2)}, u32[]{:S(2)}) %collective-permute-start.7) | collective-permute-done | bytes 262176 | tf_op jit(solution)/shard_map/ppermute | solution.py:84
  78.0 0.8 pad_maximum_fusion.2
  78.9 3.4 %collective-permute-start.8 = (f32[4,2,2,16,512]{4,3,2,1,0:T(8,128)}, f32[4,2,2,16,512]{4,3,2,1,0:T(8,128)}, u32[]{:S(2)}, u32[]{:S(2)}) collective-permute-start(f32[4,2,2,16,512]{4,3,2,1,0:T(8,128)} %pad_maximum_fusion.2), channel_id=1, source_target_pairs={{0,1},{1,0},{2,3},{3,2},{4,5},{5,4},{6,7},{7,6},{8,9},{9,8},{10,11... | collective-permute-start | bytes 1572872 | tf_op jit(solution)/shard_map/ppermute | solution.py:30
  82.3 1.4 broadcast_add_fusion
  83.6 0.5 collective-permute-done.8
  84.1 2.0 %select_bitcast_fusion.1 = (f32[4,2,2,1,16,512]{5,4,3,2,1,0:T(8,128)S(1)}, f32[4,2,2,1,16,512]{5,4,3,2,1,0:T(8,128)}) fusion(f32[4,2,2,16,512]{4,3,2,1,0:T(8,128)} %collective-permute-done.8, pred[]{:T(512)S(6)} %eq.16, f32[4,1,2,16,512]{4,3,2,1,0:T(8,128)S(1)} %get-tuple-element.15, f32[4,1,2,16,512]{4,3,2,1,0:T(8,128)S(1)} %get-tuple-element.14), kind=kLoop, calls=%fused_computation.13 | loop fusion | flops 393216 | bytes 2097153 | tf_op jit(solution)/shard_map/stack | solution.py:46
  86.1 0.1 fusion.17
  86.2 0.6 fusion.19
  86.8 0.6 copy-done.3
  87.4 0.6 fusion
  88.0 2.4 %collective-permute-start.9 = (f32[512,128]{1,0:T(8,128)S(1)}, f32[512,128]{1,0:T(8,128)S(1)}, u32[]{:S(2)}, u32[]{:S(2)}) collective-permute-start(f32[512,128]{1,0:T(8,128)S(1)} %slice.84), channel_id=1, source_target_pairs={{0,1},{1,0},{2,3},{3,2},{4,5},{5,4},{6,7},{7,6},{8,9},{9,8},{10,11... | collective-permute-start | bytes 786440 | tf_op jit(solution)/shard_map/ppermute | solution.py:30
  90.5 0.1 pad_maximum_fusion
  90.6 0.6 fusion.3
  91.2 0.4 collective-permute-done.9
  91.6 0.4 fusion.4
  92.0 0.1 pad_maximum_fusion.1
  92.1 27.6 %all_to_all.25 = f32[8,112,256]{2,1,0:T(8,128)S(1)} all-to-all(f32[8,112,256]{2,1,0:T(8,128)S(1)} %pad_maximum_fusion.1), channel_id=1, replica_groups=mesh['zl'=4,'y'=8,'x'=8,'zh'=2,'core'=2] {'x'}, dimensions={0} | all-to-all | bytes 1835008 | tf_op jit(solution)/shard_map/all_to_all | solution.py:34
  119.8 0.1 reduce_sum.27
  119.9 0.8 broadcast_in_dim.44
  120.6 6.3 %all-to-all-start.2 = ((f32[8,48,256]{2,1,0:T(8,128)}), f32[8,48,256]{2,1,0:T(8,128)S(1)}, u32[]{:S(2)}, u32[]{:S(2)}) async-start(f32[8,48,256]{2,1,0:T(8,128)} %broadcast_in_dim.44), calls=%async_computation.2 | async-start | bytes 786432 | tf_op jit(solution)/shard_map/all_to_all | solution.py:34
  127.0 3.7 %collective-permute-start.10 = (f32[32,256]{1,0:T(8,128)S(1)}, f32[32,256]{1,0:T(8,128)S(1)}, u32[]{:S(2)}, u32[]{:S(2)}) collective-permute-start(f32[32,256]{1,0:T(8,128)S(1)} %dynamic-slice_bitcast_fusion), channel_id=1, source_target_pairs={{0,2},{2,0},{1,3},{3,1},{4,6},{6,4},{5,7},{7,5},{8,10},{10,8},{9,1... | collective-permute-start | bytes 98312 | tf_op jit(solution)/shard_map/ppermute | solution.py:30
  130.7 4.9 %collective-permute-done.10 = f32[32,256]{1,0:T(8,128)S(1)} collective-permute-done((f32[32,256]{1,0:T(8,128)S(1)}, f32[32,256]{1,0:T(8,128)S(1)}, u32[]{:S(2)}, u32[]{:S(2)}) %collective-permute-start.10) | collective-permute-done | bytes 32800 | tf_op jit(solution)/shard_map/ppermute | solution.py:30
  135.7 3.5 %all-to-all-done.2 = f32[8,48,256]{2,1,0:T(8,128)S(1)} async-done(((f32[8,48,256]{2,1,0:T(8,128)}), f32[8,48,256]{2,1,0:T(8,128)S(1)}, u32[]{:S(2)}, u32[]{:S(2)}) %all-to-all-start.2) | async-done | bytes 393248 | tf_op jit(solution)/shard_map/all_to_all | solution.py:34
  139.2 0.8 broadcast_in_dim.45
  140.0 4.2 %all-to-all-start.3 = ((f32[8,48,256]{2,1,0:T(8,128)}), f32[8,48,256]{2,1,0:T(8,128)S(1)}, u32[]{:S(2)}, u32[]{:S(2)}) async-start(f32[8,48,256]{2,1,0:T(8,128)} %broadcast_in_dim.45), calls=%async_computation.3 | async-start | bytes 786432 | tf_op jit(solution)/shard_map/all_to_all | solution.py:34
  144.2 5.6 %collective-permute-start.11 = (f32[32,256]{1,0:T(8,128)S(1)}, f32[32,256]{1,0:T(8,128)S(1)}, u32[]{:S(2)}, u32[]{:S(2)}) collective-permute-start(f32[32,256]{1,0:T(8,128)S(1)} %fusion.10), channel_id=1, source_target_pairs={{0,1},{1,0},{2,3},{3,2},{4,5},{5,4},{6,7},{7,6},{8,9},{9,8},{10,11... | collective-permute-start | bytes 98312 | tf_op jit(solution)/shard_map/ppermute | solution.py:30
  149.8 0.8 collective-permute-done.11
  150.7 4.2 %all-to-all-done.3 = f32[8,48,256]{2,1,0:T(8,128)S(1)} async-done(((f32[8,48,256]{2,1,0:T(8,128)}), f32[8,48,256]{2,1,0:T(8,128)S(1)}, u32[]{:S(2)}, u32[]{:S(2)}) %all-to-all-start.3) | async-done | bytes 393248 | tf_op jit(solution)/shard_map/all_to_all | solution.py:34
  155.0 0.8 broadcast_in_dim.46
  155.7 4.5 %all-to-all-start.4 = ((f32[8,48,256]{2,1,0:T(8,128)}), f32[8,48,256]{2,1,0:T(8,128)S(1)}, u32[]{:S(2)}, u32[]{:S(2)}) async-start(f32[8,48,256]{2,1,0:T(8,128)} %broadcast_in_dim.46), calls=%async_computation.4 | async-start | bytes 786432 | tf_op jit(solution)/shard_map/all_to_all | solution.py:34
  160.3 10.7 %all-to-all-done.4 = f32[8,48,256]{2,1,0:T(8,128)S(1)} async-done(((f32[8,48,256]{2,1,0:T(8,128)}), f32[8,48,256]{2,1,0:T(8,128)S(1)}, u32[]{:S(2)}, u32[]{:S(2)}) %all-to-all-start.4) | async-done | bytes 393248 | tf_op jit(solution)/shard_map/all_to_all | solution.py:34
  171.0 7.2 %collective-permute-start.12 = (f32[384,256]{1,0:T(8,128)S(1)}, f32[384,256]{1,0:T(8,128)S(1)}, u32[]{:S(2)}, u32[]{:S(2)}) collective-permute-start(f32[384,256]{1,0:T(8,128)S(1)} %bitcast.79), channel_id=1, source_target_pairs={{0,1},{1,0},{2,3},{3,2},{4,5},{5,4},{6,7},{7,6},{8,9},{9,8},{10,11... | collective-permute-start | bytes 1179656 | tf_op jit(solution)/shard_map/ppermute | solution.py:30
  178.2 0.0 copy-start.8
  178.3 0.8 bitcast_subtract_fusion
  179.1 0.5 collective-permute-done.12
  179.5 0.1 broadcast_select_fusion
  179.6 0.0 copy-start.4
  179.7 0.3 convolution_subtract_fusion.1
  180.0 0.4 copy-done.4
  180.4 0.4 convolution_bitcast_fusion.1
  180.8 0.3 copy-done.5
  181.1 1.1 fusion.2
  (49 shorter events, 0.5 us)
Async XLA Ops:
  0.6 177.6 %copy-start = (f32[256,256]{1,0:T(8,128)S(1)}, f32[256,256]{1,0:T(8,128)}, u32[]{:S(2)}) copy-start(f32[256,256]{1,0:T(8,128)} %param.13) | copy-start | bytes 786436
  0.6 47.0 %collective-permute-start.1 = (f32[512,512]{1,0:T(8,128)}, f32[512,512]{1,0:T(8,128)S(1)}, u32[]{:S(2)}, u32[]{:S(2)}) collective-permute-start(f32[512,512]{1,0:T(8,128)} %param.7), channel_id=1, source_target_pairs={{0,1},{1,0},{2,3},{3,2},{4,5},{5,4},{6,7},{7,6},{8,9},{9,8},{10,11... | collective-permute-start | bytes 3145736 | tf_op jit(solution)/shard_map/ppermute | solution.py:30
  16.9 0.7 copy-start.11
  17.6 0.7 copy-start.9
  17.6 0.7 copy-start.10
  19.7 13.8 %collective-permute-start.6 = (f32[16,256]{1,0:T(8,128)S(1)}, f32[16,256]{1,0:T(8,128)S(1)}, u32[]{:S(2)}, u32[]{:S(2)}) collective-permute-start(f32[16,256]{1,0:T(8,128)S(1)} %broadcast_select_fusion.6), channel_id=1, source_target_pairs={{0,1},{1,33},{2,65},{3,97},{4,129},{5,161},{6,193},{7,225},{8,257}... | collective-permute-start | bytes 49160 | tf_op jit(solution)/shard_map/ppermute | solution.py:68
  21.6 11.8 %collective-permute-start.5 = (f32[16,256]{1,0:T(8,128)S(1)}, f32[16,256]{1,0:T(8,128)S(1)}, u32[]{:S(2)}, u32[]{:S(2)}) collective-permute-start(f32[16,256]{1,0:T(8,128)S(1)} %get-tuple-element.5), channel_id=1, source_target_pairs={{0,0},{1,32},{2,64},{3,96},{4,128},{5,160},{6,192},{7,224},{8,256}... | collective-permute-start | bytes 49160 | tf_op jit(solution)/shard_map/ppermute | solution.py:67
  25.2 22.4 %collective-permute-start = (f32[16,512]{1,0:T(8,128)S(1)}, f32[16,512]{1,0:T(8,128)S(1)}, u32[]{:S(2)}, u32[]{:S(2)}) collective-permute-start(f32[16,512]{1,0:T(8,128)S(1)} %pad_maximum_fusion.6), channel_id=1, source_target_pairs={{0,2},{2,0},{1,3},{3,1},{4,6},{6,4},{5,7},{7,5},{8,10},{10,8},{9,1... | collective-permute-start | bytes 98312 | tf_op jit(solution)/shard_map/ppermute | solution.py:30
  34.6 51.5 %all-to-all-start = ((f32[32,2,16,256]{3,2,1,0:T(8,128)}), f32[32,2,16,256]{3,2,1,0:T(8,128)S(1)}, u32[]{:S(2)}, u32[]{:S(2)}) async-start(f32[32,2,16,256]{3,2,1,0:T(8,128)} %broadcast_in_dim.43), calls=%async_computation | async-start | bytes 2097152 | tf_op jit(solution)/shard_map/all_to_all | solution.py:34
  47.6 13.0 %copy-start.2 = (f32[512,512]{1,0:T(8,128)}, f32[512,512]{1,0:T(8,128)S(1)}, u32[]{:S(2)}) copy-start(f32[512,512]{1,0:T(8,128)S(1)} %collective-permute-done.1) | copy-start | bytes 3145732
  47.7 13.0 %collective-permute-start.2 = (f32[2,16,512]{2,1,0:T(8,128)S(1)}, f32[2,16,512]{2,1,0:T(8,128)S(1)}, u32[]{:S(2)}, u32[]{:S(2)}) collective-permute-start(f32[2,16,512]{2,1,0:T(8,128)S(1)} %maximum_add_fusion.1), channel_id=1, source_target_pairs={{0,8},{4,12},{8,0},{12,4},{16,24},{20,28},{24,16},{28,20},{1,9},{5... | collective-permute-start | bytes 196616 | tf_op jit(solution)/shard_map/ppermute | solution.py:81
  53.5 8.9 %collective-permute-start.3 = (f32[2,16,512]{2,1,0:T(8,128)S(1)}, f32[2,16,512]{2,1,0:T(8,128)S(1)}, u32[]{:S(2)}, u32[]{:S(2)}) collective-permute-start(f32[2,16,512]{2,1,0:T(8,128)S(1)} %maximum_add_fusion.1), channel_id=1, source_target_pairs={{0,16},{4,20},{8,24},{12,28},{16,0},{20,4},{24,8},{28,12},{1,17},{... | collective-permute-start | bytes 196616 | tf_op jit(solution)/shard_map/ppermute | solution.py:81
  58.3 7.9 %collective-permute-start.4 = (f32[2,16,512]{2,1,0:T(8,128)S(1)}, f32[2,16,512]{2,1,0:T(8,128)S(1)}, u32[]{:S(2)}, u32[]{:S(2)}) collective-permute-start(f32[2,16,512]{2,1,0:T(8,128)S(1)} %maximum_add_fusion.1), channel_id=1, source_target_pairs={{0,24},{4,28},{8,16},{12,20},{16,8},{20,12},{24,0},{28,4},{1,25},{... | collective-permute-start | bytes 196616 | tf_op jit(solution)/shard_map/ppermute | solution.py:81
  66.3 11.7 %collective-permute-start.7 = (f32[4,2,16,512]{3,2,1,0:T(8,128)S(1)}, f32[4,2,16,512]{3,2,1,0:T(8,128)S(1)}, u32[]{:S(2)}, u32[]{:S(2)}) collective-permute-start(f32[4,2,16,512]{3,2,1,0:T(8,128)S(1)} %bitcast_dynamic-update-slice_fusion), channel_id=1, source_target_pairs={{0,4},{4,0},{8,12},{12,8},{16,20},{20,16},{24,28},{28,24},{1,5},{5... | collective-permute-start | bytes 786440 | tf_op jit(solution)/shard_map/ppermute | solution.py:84
  78.9 5.2 %collective-permute-start.8 = (f32[4,2,2,16,512]{4,3,2,1,0:T(8,128)}, f32[4,2,2,16,512]{4,3,2,1,0:T(8,128)}, u32[]{:S(2)}, u32[]{:S(2)}) collective-permute-start(f32[4,2,2,16,512]{4,3,2,1,0:T(8,128)} %pad_maximum_fusion.2), channel_id=1, source_target_pairs={{0,1},{1,0},{2,3},{3,2},{4,5},{5,4},{6,7},{7,6},{8,9},{9,8},{10,11... | collective-permute-start | bytes 1572872 | tf_op jit(solution)/shard_map/ppermute | solution.py:30
  86.2 1.2 copy-start.3
  88.0 2.5 %copy-start.1 = (f32[4,2,2,1,16,512]{5,4,3,2,1,0:T(8,128)S(1)}, f32[4,2,2,1,16,512]{5,4,3,2,1,0:T(8,128)}, u32[]{:S(2)}) copy-start(f32[4,2,2,1,16,512]{5,4,3,2,1,0:T(8,128)} %get-tuple-element.11) | copy-start | bytes 1572868
  88.0 3.6 %collective-permute-start.9 = (f32[512,128]{1,0:T(8,128)S(1)}, f32[512,128]{1,0:T(8,128)S(1)}, u32[]{:S(2)}, u32[]{:S(2)}) collective-permute-start(f32[512,128]{1,0:T(8,128)S(1)} %slice.84), channel_id=1, source_target_pairs={{0,1},{1,0},{2,3},{3,2},{4,5},{5,4},{6,7},{7,6},{8,9},{9,8},{10,11... | collective-permute-start | bytes 786440 | tf_op jit(solution)/shard_map/ppermute | solution.py:30
  120.6 18.6 %all-to-all-start.2 = ((f32[8,48,256]{2,1,0:T(8,128)}), f32[8,48,256]{2,1,0:T(8,128)S(1)}, u32[]{:S(2)}, u32[]{:S(2)}) async-start(f32[8,48,256]{2,1,0:T(8,128)} %broadcast_in_dim.44), calls=%async_computation.2 | async-start | bytes 786432 | tf_op jit(solution)/shard_map/all_to_all | solution.py:34
  127.0 8.7 %collective-permute-start.10 = (f32[32,256]{1,0:T(8,128)S(1)}, f32[32,256]{1,0:T(8,128)S(1)}, u32[]{:S(2)}, u32[]{:S(2)}) collective-permute-start(f32[32,256]{1,0:T(8,128)S(1)} %dynamic-slice_bitcast_fusion), channel_id=1, source_target_pairs={{0,2},{2,0},{1,3},{3,1},{4,6},{6,4},{5,7},{7,5},{8,10},{10,8},{9,1... | collective-permute-start | bytes 98312 | tf_op jit(solution)/shard_map/ppermute | solution.py:30
  140.0 14.9 %all-to-all-start.3 = ((f32[8,48,256]{2,1,0:T(8,128)}), f32[8,48,256]{2,1,0:T(8,128)S(1)}, u32[]{:S(2)}, u32[]{:S(2)}) async-start(f32[8,48,256]{2,1,0:T(8,128)} %broadcast_in_dim.45), calls=%async_computation.3 | async-start | bytes 786432 | tf_op jit(solution)/shard_map/all_to_all | solution.py:34
  144.2 6.4 %collective-permute-start.11 = (f32[32,256]{1,0:T(8,128)S(1)}, f32[32,256]{1,0:T(8,128)S(1)}, u32[]{:S(2)}, u32[]{:S(2)}) collective-permute-start(f32[32,256]{1,0:T(8,128)S(1)} %fusion.10), channel_id=1, source_target_pairs={{0,1},{1,0},{2,3},{3,2},{4,5},{5,4},{6,7},{7,6},{8,9},{9,8},{10,11... | collective-permute-start | bytes 98312 | tf_op jit(solution)/shard_map/ppermute | solution.py:30
  155.7 4.5 %copy-start.6 = (f32[256,256]{1,0:T(8,128)S(1)}, f32[256,256]{1,0:T(8,128)}, u32[]{:S(2)}) copy-start(f32[256,256]{1,0:T(8,128)} %param.12) | copy-start | bytes 786436
  155.7 4.5 %copy-start.7 = (f32[256,256]{1,0:T(8,128)S(1)}, f32[256,256]{1,0:T(8,128)}, u32[]{:S(2)}) copy-start(f32[256,256]{1,0:T(8,128)} %param.11) | copy-start | bytes 786436
  155.7 15.2 %all-to-all-start.4 = ((f32[8,48,256]{2,1,0:T(8,128)}), f32[8,48,256]{2,1,0:T(8,128)S(1)}, u32[]{:S(2)}, u32[]{:S(2)}) async-start(f32[8,48,256]{2,1,0:T(8,128)} %broadcast_in_dim.46), calls=%async_computation.4 | async-start | bytes 786432 | tf_op jit(solution)/shard_map/all_to_all | solution.py:34
  171.0 8.5 %collective-permute-start.12 = (f32[384,256]{1,0:T(8,128)S(1)}, f32[384,256]{1,0:T(8,128)S(1)}, u32[]{:S(2)}, u32[]{:S(2)}) collective-permute-start(f32[384,256]{1,0:T(8,128)S(1)} %bitcast.79), channel_id=1, source_target_pairs={{0,1},{1,0},{2,3},{3,2},{4,5},{5,4},{6,7},{7,6},{8,9},{9,8},{10,11... | collective-permute-start | bytes 1179656 | tf_op jit(solution)/shard_map/ppermute | solution.py:30
  178.2 0.8 copy-start.8
  179.6 0.7 copy-start.4
  180.4 0.7 copy-start.5

commit v10 on v4

--- a/solution.py
+++ b/solution.py
@@ -105,6 +105,9 @@
     column_one = pick(col_one.reshape(2, span, width), core)
     column_two = pick(col_two.reshape(2, span, width), core) - mm(column_one, link_block)
 
+    diag_one = lax.optimization_barrier(after(diag_one, column))
+    diag_two = lax.optimization_barrier(after(diag_two, column))
+
     grams = after(jnp.sum(gather(grams, "y"), axis=0), column)
     grams = after(jnp.sum(gather(grams, ("zh", "zl")), axis=0), sibling)
     grams = gather(grams, "x").reshape(-1, width)

time: 183 us -> 182 us (level)
  no operation moved by 1% of the time
where the time goes in v10:
time: 182 us; the launch traced here: 181 us
  starting transfers between devices  98.9 us (54%)
  waiting for transfers between devices  37.8 us (21%)
  blocking collectives  27.6 us (15%)
  local copies, waits for them, and re-layouts  7.27 us (4%)
  matrix products  5.54 us (3%)
  other arithmetic  2.14 us (1%)
    ppermute x7, starting transfers between devices, swap(): return lax.ppermute(a, axis, SWAP)  46.6 us
    all_to_all x4, starting transfers between devices, exchange(): return lax.all_to_all(a, axes, 0, 0, tiled=True)  28 us
    all_to_all x1, blocking collectives, exchange(): return lax.all_to_all(a, axes, 0, 0, tiled=True)  27.6 us
    all_to_all x4, waiting for transfers between devices, exchange(): return lax.all_to_all(a, axes, 0, 0, tiled=True)  18.5 us
    ppermute x3, starting transfers between devices, local(): came = lax.ppermute(group, 'x', [(i, i ^ 2 * step) for i in range(nx)])  12.9 us
    ppermute x7, waiting for transfers between devices, swap(): return lax.ppermute(a, axis, SWAP)  7.94 us
    ppermute x1, starting transfers between devices, local(): lax.ppermute(rows, 'x', [(i, i ^ 1) for i in range(nx)])  5.93 us
    ppermute x1, waiting for transfers between devices, local(): lax.ppermute(rows, 'x', [(i, i ^ 1) for i in range(nx)])  5.75 us
  transfers between devices with their start and end apart: 17, of which 11 were waited for; matrix products, arithmetic and copies ran while one was open for 3% of the time, Pallas kernels for 0%

profile of v10, /device:TPU:1, one launch (start us, length us, event | category | flops | bytes accessed | tf_op | source)
XLA Modules:
  0.0 180.5 jit_solution(5836187717274481553)
XLA Ops:
  0.6 0.0 copy-start
  0.6 16.2 %collective-permute-start.2 = (f32[512,512]{1,0:T(8,128)}, f32[512,512]{1,0:T(8,128)S(1)}, u32[]{:S(2)}, u32[]{:S(2)}) collective-permute-start(f32[512,512]{1,0:T(8,128)} %param.7), channel_id=1, source_target_pairs={{0,1},{1,0},{2,3},{3,2},{4,5},{5,4},{6,7},{7,6},{8,9},{9,8},{10,11... | collective-permute-start | bytes 3145736 | tf_op jit(solution)/shard_map/ppermute | solution.py:30
  16.9 0.7 copy-done.11
  17.6 0.1 fusion.14
  17.6 0.5 fusion.17
  18.2 0.2 copy-done.9
  18.4 0.0 copy-done.10
  18.4 1.3 broadcast_select_fusion.7
  19.7 1.9 %collective-permute-start.1 = (f32[16,256]{1,0:T(8,128)S(1)}, f32[16,256]{1,0:T(8,128)S(1)}, u32[]{:S(2)}, u32[]{:S(2)}) collective-permute-start(f32[16,256]{1,0:T(8,128)S(1)} %broadcast_select_fusion.6), channel_id=1, source_target_pairs={{0,1},{1,33},{2,65},{3,97},{4,129},{5,161},{6,193},{7,225},{8,257}... | collective-permute-start | bytes 49160 | tf_op jit(solution)/shard_map/ppermute | solution.py:68
  21.6 3.5 %collective-permute-start = (f32[16,256]{1,0:T(8,128)S(1)}, f32[16,256]{1,0:T(8,128)S(1)}, u32[]{:S(2)}, u32[]{:S(2)}) collective-permute-start(f32[16,256]{1,0:T(8,128)S(1)} %get-tuple-element.5), channel_id=1, source_target_pairs={{0,0},{1,32},{2,64},{3,96},{4,128},{5,160},{6,192},{7,224},{8,256}... | collective-permute-start | bytes 49160 | tf_op jit(solution)/shard_map/ppermute | solution.py:67
  25.2 8.2 %collective-permute-start.3 = (f32[16,512]{1,0:T(8,128)S(1)}, f32[16,512]{1,0:T(8,128)S(1)}, u32[]{:S(2)}, u32[]{:S(2)}) collective-permute-start(f32[16,512]{1,0:T(8,128)S(1)} %pad_maximum_fusion.7), channel_id=1, source_target_pairs={{0,2},{2,0},{1,3},{3,1},{4,6},{6,4},{5,7},{7,5},{8,10},{10,8},{9,1... | collective-permute-start | bytes 98312 | tf_op jit(solution)/shard_map/ppermute | solution.py:30
  33.5 0.0 collective-permute-done.1
  33.5 0.0 collective-permute-done
  33.5 1.1 broadcast_in_dim.39
  34.6 13.0 %all-to-all-start = ((f32[32,2,16,256]{3,2,1,0:T(8,128)}), f32[32,2,16,256]{3,2,1,0:T(8,128)S(1)}, u32[]{:S(2)}, u32[]{:S(2)}) async-start(f32[32,2,16,256]{3,2,1,0:T(8,128)} %broadcast_in_dim.39), calls=%async_computation | async-start | bytes 2097152 | tf_op jit(solution)/shard_map/all_to_all | solution.py:34
  47.7 5.8 %collective-permute-start.4 = (f32[2,16,512]{2,1,0:T(8,128)S(1)}, f32[2,16,512]{2,1,0:T(8,128)S(1)}, u32[]{:S(2)}, u32[]{:S(2)}) collective-permute-start(f32[2,16,512]{2,1,0:T(8,128)S(1)} %maximum_add_fusion.1), channel_id=1, source_target_pairs={{0,8},{4,12},{8,0},{12,4},{16,24},{20,28},{24,16},{28,20},{1,9},{5... | collective-permute-start | bytes 196616 | tf_op jit(solution)/shard_map/ppermute | solution.py:81
  53.5 4.9 %collective-permute-start.5 = (f32[2,16,512]{2,1,0:T(8,128)S(1)}, f32[2,16,512]{2,1,0:T(8,128)S(1)}, u32[]{:S(2)}, u32[]{:S(2)}) collective-permute-start(f32[2,16,512]{2,1,0:T(8,128)S(1)} %maximum_add_fusion.1), channel_id=1, source_target_pairs={{0,16},{4,20},{8,24},{12,28},{16,0},{20,4},{24,8},{28,12},{1,17},{... | collective-permute-start | bytes 196616 | tf_op jit(solution)/shard_map/ppermute | solution.py:81
  58.3 2.2 %collective-permute-start.6 = (f32[2,16,512]{2,1,0:T(8,128)S(1)}, f32[2,16,512]{2,1,0:T(8,128)S(1)}, u32[]{:S(2)}, u32[]{:S(2)}) collective-permute-start(f32[2,16,512]{2,1,0:T(8,128)S(1)} %maximum_add_fusion.1), channel_id=1, source_target_pairs={{0,24},{4,28},{8,16},{12,20},{16,8},{20,12},{24,0},{28,4},{1,25},{... | collective-permute-start | bytes 196616 | tf_op jit(solution)/shard_map/ppermute | solution.py:81
  60.7 1.7 collective-permute-done.5
  62.4 3.9 %collective-permute-done.6 = f32[2,16,512]{2,1,0:T(8,128)S(1)} collective-permute-done((f32[2,16,512]{2,1,0:T(8,128)S(1)}, f32[2,16,512]{2,1,0:T(8,128)S(1)}, u32[]{:S(2)}, u32[]{:S(2)}) %collective-permute-start.6) | collective-permute-done | bytes 65568 | tf_op jit(solution)/shard_map/ppermute | solution.py:81
  66.3 5.9 %collective-permute-start.7 = (f32[4,2,16,512]{3,2,1,0:T(8,128)S(1)}, f32[4,2,16,512]{3,2,1,0:T(8,128)S(1)}, u32[]{:S(2)}, u32[]{:S(2)}) collective-permute-start(f32[4,2,16,512]{3,2,1,0:T(8,128)S(1)} %bitcast_dynamic-update-slice_fusion), channel_id=1, source_target_pairs={{0,4},{4,0},{8,12},{12,8},{16,20},{20,16},{24,28},{28,24},{1,5},{5... | collective-permute-start | bytes 786440 | tf_op jit(solution)/shard_map/ppermute | solution.py:83
  72.2 5.8 %collective-permute-done.7 = f32[4,2,16,512]{3,2,1,0:T(8,128)S(1)} collective-permute-done((f32[4,2,16,512]{3,2,1,0:T(8,128)S(1)}, f32[4,2,16,512]{3,2,1,0:T(8,128)S(1)}, u32[]{:S(2)}, u32[]{:S(2)}) %collective-permute-start.7) | collective-permute-done | bytes 262176 | tf_op jit(solution)/shard_map/ppermute | solution.py:83
  78.1 3.4 %collective-permute-start.8 = (f32[4,2,2,16,512]{4,3,2,1,0:T(8,128)S(1)}, f32[4,2,2,16,512]{4,3,2,1,0:T(8,128)S(1)}, u32[]{:S(2)}, u32[]{:S(2)}) collective-permute-start(f32[4,2,2,16,512]{4,3,2,1,0:T(8,128)S(1)} %pad_maximum_fusion.2), channel_id=1, source_target_pairs={{0,1},{1,0},{2,3},{3,2},{4,5},{5,4},{6,7},{7,6},{8,9},{9,8},{10,11... | collective-permute-start | bytes 1572872 | tf_op jit(solution)/shard_map/ppermute | solution.py:30
  81.5 1.5 collective-permute-done.8
  83.0 0.1 select_bitcast_fusion.1
  83.1 0.0 copy-start.3
  83.1 0.1 fusion.16
  83.2 1.1 copy-done.3
  84.4 1.0 fusion.18
  85.4 0.2 copy-done.2
  85.6 1.0 convolution_add_fusion
  86.7 2.3 %collective-permute-start.9 = (f32[512,128]{0,1:T(8,128)S(1)}, f32[512,128]{0,1:T(8,128)S(1)}, u32[]{:S(2)}, u32[]{:S(2)}) collective-permute-start(f32[512,128]{0,1:T(8,128)S(1)} %slice.76), channel_id=1, source_target_pairs={{0,1},{1,0},{2,3},{3,2},{4,5},{5,4},{6,7},{7,6},{8,9},{9,8},{10,11... | collective-permute-start | bytes 786440 | tf_op jit(solution)/shard_map/ppermute | solution.py:30
  89.0 0.1 pad_maximum_fusion
  89.1 0.2 copy.18
  89.3 0.6 fusion.2
  89.9 0.2 collective-permute-done.9
  90.1 0.3 fusion.3
  90.4 0.1 pad_maximum_fusion.1
  90.5 27.6 %all_to_all.25 = f32[8,112,256]{2,1,0:T(8,128)S(1)} all-to-all(f32[8,112,256]{2,1,0:T(8,128)S(1)} %pad_maximum_fusion.1), channel_id=1, replica_groups=mesh['zl'=4,'y'=8,'x'=8,'zh'=2,'core'=2] {'x'}, dimensions={0} | all-to-all | bytes 1835008 | tf_op jit(solution)/shard_map/all_to_all | solution.py:34
  118.2 0.1 reduce_sum.27
  118.2 0.8 broadcast_in_dim.44
  119.0 6.3 %all-to-all-start.2 = ((f32[8,48,256]{2,1,0:T(8,128)}), f32[8,48,256]{2,1,0:T(8,128)S(1)}, u32[]{:S(2)}, u32[]{:S(2)}) async-start(f32[8,48,256]{2,1,0:T(8,128)} %broadcast_in_dim.44), calls=%async_computation.2 | async-start | bytes 786432 | tf_op jit(solution)/shard_map/all_to_all | solution.py:34
  125.3 3.7 %collective-permute-start.10 = (f32[32,256]{1,0:T(8,128)S(1)}, f32[32,256]{1,0:T(8,128)S(1)}, u32[]{:S(2)}, u32[]{:S(2)}) collective-permute-start(f32[32,256]{1,0:T(8,128)S(1)} %dynamic-slice_bitcast_fusion), channel_id=1, source_target_pairs={{0,2},{2,0},{1,3},{3,1},{4,6},{6,4},{5,7},{7,5},{8,10},{10,8},{9,1... | collective-permute-start | bytes 98312 | tf_op jit(solution)/shard_map/ppermute | solution.py:30
  129.1 4.9 %collective-permute-done.10 = f32[32,256]{1,0:T(8,128)S(1)} collective-permute-done((f32[32,256]{1,0:T(8,128)S(1)}, f32[32,256]{1,0:T(8,128)S(1)}, u32[]{:S(2)}, u32[]{:S(2)}) %collective-permute-start.10) | collective-permute-done | bytes 32800 | tf_op jit(solution)/shard_map/ppermute | solution.py:30
  134.0 3.5 %all-to-all-done.2 = f32[8,48,256]{2,1,0:T(8,128)S(1)} async-done(((f32[8,48,256]{2,1,0:T(8,128)}), f32[8,48,256]{2,1,0:T(8,128)S(1)}, u32[]{:S(2)}, u32[]{:S(2)}) %all-to-all-start.2) | async-done | bytes 393248 | tf_op jit(solution)/shard_map/all_to_all | solution.py:34
  137.6 0.8 broadcast_in_dim.45
  138.4 4.2 %all-to-all-start.3 = ((f32[8,48,256]{2,1,0:T(8,128)}), f32[8,48,256]{2,1,0:T(8,128)S(1)}, u32[]{:S(2)}, u32[]{:S(2)}) async-start(f32[8,48,256]{2,1,0:T(8,128)} %broadcast_in_dim.45), calls=%async_computation.3 | async-start | bytes 786432 | tf_op jit(solution)/shard_map/all_to_all | solution.py:34
  142.6 5.6 %collective-permute-start.11 = (f32[32,256]{1,0:T(8,128)S(1)}, f32[32,256]{1,0:T(8,128)S(1)}, u32[]{:S(2)}, u32[]{:S(2)}) collective-permute-start(f32[32,256]{1,0:T(8,128)S(1)} %fusion.9), channel_id=1, source_target_pairs={{0,1},{1,0},{2,3},{3,2},{4,5},{5,4},{6,7},{7,6},{8,9},{9,8},{10,11... | collective-permute-start | bytes 98312 | tf_op jit(solution)/shard_map/ppermute | solution.py:30
  148.2 0.8 collective-permute-done.11
  149.0 4.2 %all-to-all-done.3 = f32[8,48,256]{2,1,0:T(8,128)S(1)} async-done(((f32[8,48,256]{2,1,0:T(8,128)}), f32[8,48,256]{2,1,0:T(8,128)S(1)}, u32[]{:S(2)}, u32[]{:S(2)}) %all-to-all-start.3) | async-done | bytes 393248 | tf_op jit(solution)/shard_map/all_to_all | solution.py:34
  153.3 0.8 broadcast_in_dim.46
  154.1 4.5 %all-to-all-start.4 = ((f32[8,48,256]{2,1,0:T(8,128)}), f32[8,48,256]{2,1,0:T(8,128)S(1)}, u32[]{:S(2)}, u32[]{:S(2)}) async-start(f32[8,48,256]{2,1,0:T(8,128)} %broadcast_in_dim.46), calls=%async_computation.4 | async-start | bytes 786432 | tf_op jit(solution)/shard_map/all_to_all | solution.py:34
  158.6 10.7 %all-to-all-done.4 = f32[8,48,256]{2,1,0:T(8,128)S(1)} async-done(((f32[8,48,256]{2,1,0:T(8,128)}), f32[8,48,256]{2,1,0:T(8,128)S(1)}, u32[]{:S(2)}, u32[]{:S(2)}) %all-to-all-start.4) | async-done | bytes 393248 | tf_op jit(solution)/shard_map/all_to_all | solution.py:34
  169.4 7.2 %collective-permute-start.12 = (f32[384,256]{1,0:T(8,128)S(1)}, f32[384,256]{1,0:T(8,128)S(1)}, u32[]{:S(2)}, u32[]{:S(2)}) collective-permute-start(f32[384,256]{1,0:T(8,128)S(1)} %bitcast.78), channel_id=1, source_target_pairs={{0,1},{1,0},{2,3},{3,2},{4,5},{5,4},{6,7},{7,6},{8,9},{9,8},{10,11... | collective-permute-start | bytes 1179656 | tf_op jit(solution)/shard_map/ppermute | solution.py:30
  176.6 0.0 copy-start.8
  176.6 0.8 bitcast_subtract_fusion
  177.4 0.5 collective-permute-done.12
  177.9 0.1 broadcast_select_fusion
  178.0 0.0 copy-start.4
  178.1 0.3 convolution_subtract_fusion.1
  178.3 0.4 copy-done.4
  178.7 0.4 convolution_bitcast_fusion
  179.1 0.3 copy-done.5
  179.4 1.1 fusion.1
  (48 shorter events, 0.5 us)
Async XLA Ops:
  0.6 176.0 %copy-start = (f32[256,256]{1,0:T(8,128)S(1)}, f32[256,256]{1,0:T(8,128)}, u32[]{:S(2)}) copy-start(f32[256,256]{1,0:T(8,128)} %param.13) | copy-start | bytes 786436
  0.6 47.0 %collective-permute-start.2 = (f32[512,512]{1,0:T(8,128)}, f32[512,512]{1,0:T(8,128)S(1)}, u32[]{:S(2)}, u32[]{:S(2)}) collective-permute-start(f32[512,512]{1,0:T(8,128)} %param.7), channel_id=1, source_target_pairs={{0,1},{1,0},{2,3},{3,2},{4,5},{5,4},{6,7},{7,6},{8,9},{9,8},{10,11... | collective-permute-start | bytes 3145736 | tf_op jit(solution)/shard_map/ppermute | solution.py:30
  16.9 0.7 copy-start.11
  17.6 0.7 copy-start.9
  17.6 0.7 copy-start.10
  19.7 13.8 %collective-permute-start.1 = (f32[16,256]{1,0:T(8,128)S(1)}, f32[16,256]{1,0:T(8,128)S(1)}, u32[]{:S(2)}, u32[]{:S(2)}) collective-permute-start(f32[16,256]{1,0:T(8,128)S(1)} %broadcast_select_fusion.6), channel_id=1, source_target_pairs={{0,1},{1,33},{2,65},{3,97},{4,129},{5,161},{6,193},{7,225},{8,257}... | collective-permute-start | bytes 49160 | tf_op jit(solution)/shard_map/ppermute | solution.py:68
  21.6 11.8 %collective-permute-start = (f32[16,256]{1,0:T(8,128)S(1)}, f32[16,256]{1,0:T(8,128)S(1)}, u32[]{:S(2)}, u32[]{:S(2)}) collective-permute-start(f32[16,256]{1,0:T(8,128)S(1)} %get-tuple-element.5), channel_id=1, source_target_pairs={{0,0},{1,32},{2,64},{3,96},{4,128},{5,160},{6,192},{7,224},{8,256}... | collective-permute-start | bytes 49160 | tf_op jit(solution)/shard_map/ppermute | solution.py:67
  25.2 22.4 %collective-permute-start.3 = (f32[16,512]{1,0:T(8,128)S(1)}, f32[16,512]{1,0:T(8,128)S(1)}, u32[]{:S(2)}, u32[]{:S(2)}) collective-permute-start(f32[16,512]{1,0:T(8,128)S(1)} %pad_maximum_fusion.7), channel_id=1, source_target_pairs={{0,2},{2,0},{1,3},{3,1},{4,6},{6,4},{5,7},{7,5},{8,10},{10,8},{9,1... | collective-permute-start | bytes 98312 | tf_op jit(solution)/shard_map/ppermute | solution.py:30
  34.6 48.5 %all-to-all-start = ((f32[32,2,16,256]{3,2,1,0:T(8,128)}), f32[32,2,16,256]{3,2,1,0:T(8,128)S(1)}, u32[]{:S(2)}, u32[]{:S(2)}) async-start(f32[32,2,16,256]{3,2,1,0:T(8,128)} %broadcast_in_dim.39), calls=%async_computation | async-start | bytes 2097152 | tf_op jit(solution)/shard_map/all_to_all | solution.py:34
  47.6 24.6 %copy-start.1 = (f32[512,512]{1,0:T(8,128)}, f32[512,512]{1,0:T(8,128)S(1)}, u32[]{:S(2)}) copy-start(f32[512,512]{1,0:T(8,128)S(1)} %collective-permute-done.2) | copy-start | bytes 3145732
  47.7 13.0 %collective-permute-start.4 = (f32[2,16,512]{2,1,0:T(8,128)S(1)}, f32[2,16,512]{2,1,0:T(8,128)S(1)}, u32[]{:S(2)}, u32[]{:S(2)}) collective-permute-start(f32[2,16,512]{2,1,0:T(8,128)S(1)} %maximum_add_fusion.1), channel_id=1, source_target_pairs={{0,8},{4,12},{8,0},{12,4},{16,24},{20,28},{24,16},{28,20},{1,9},{5... | collective-permute-start | bytes 196616 | tf_op jit(solution)/shard_map/ppermute | solution.py:81
  53.5 8.9 %collective-permute-start.5 = (f32[2,16,512]{2,1,0:T(8,128)S(1)}, f32[2,16,512]{2,1,0:T(8,128)S(1)}, u32[]{:S(2)}, u32[]{:S(2)}) collective-permute-start(f32[2,16,512]{2,1,0:T(8,128)S(1)} %maximum_add_fusion.1), channel_id=1, source_target_pairs={{0,16},{4,20},{8,24},{12,28},{16,0},{20,4},{24,8},{28,12},{1,17},{... | collective-permute-start | bytes 196616 | tf_op jit(solution)/shard_map/ppermute | solution.py:81
  58.3 7.9 %collective-permute-start.6 = (f32[2,16,512]{2,1,0:T(8,128)S(1)}, f32[2,16,512]{2,1,0:T(8,128)S(1)}, u32[]{:S(2)}, u32[]{:S(2)}) collective-permute-start(f32[2,16,512]{2,1,0:T(8,128)S(1)} %maximum_add_fusion.1), channel_id=1, source_target_pairs={{0,24},{4,28},{8,16},{12,20},{16,8},{20,12},{24,0},{28,4},{1,25},{... | collective-permute-start | bytes 196616 | tf_op jit(solution)/shard_map/ppermute | solution.py:81
  66.3 11.7 %collective-permute-start.7 = (f32[4,2,16,512]{3,2,1,0:T(8,128)S(1)}, f32[4,2,16,512]{3,2,1,0:T(8,128)S(1)}, u32[]{:S(2)}, u32[]{:S(2)}) collective-permute-start(f32[4,2,16,512]{3,2,1,0:T(8,128)S(1)} %bitcast_dynamic-update-slice_fusion), channel_id=1, source_target_pairs={{0,4},{4,0},{8,12},{12,8},{16,20},{20,16},{24,28},{28,24},{1,5},{5... | collective-permute-start | bytes 786440 | tf_op jit(solution)/shard_map/ppermute | solution.py:83
  78.1 4.9 %collective-permute-start.8 = (f32[4,2,2,16,512]{4,3,2,1,0:T(8,128)S(1)}, f32[4,2,2,16,512]{4,3,2,1,0:T(8,128)S(1)}, u32[]{:S(2)}, u32[]{:S(2)}) collective-permute-start(f32[4,2,2,16,512]{4,3,2,1,0:T(8,128)S(1)} %pad_maximum_fusion.2), channel_id=1, source_target_pairs={{0,1},{1,0},{2,3},{3,2},{4,5},{5,4},{6,7},{7,6},{8,9},{9,8},{10,11... | collective-permute-start | bytes 1572872 | tf_op jit(solution)/shard_map/ppermute | solution.py:30
  83.1 1.2 copy-start.3
  84.4 1.2 copy-start.2
  86.7 3.4 %collective-permute-start.9 = (f32[512,128]{0,1:T(8,128)S(1)}, f32[512,128]{0,1:T(8,128)S(1)}, u32[]{:S(2)}, u32[]{:S(2)}) collective-permute-start(f32[512,128]{0,1:T(8,128)S(1)} %slice.76), channel_id=1, source_target_pairs={{0,1},{1,0},{2,3},{3,2},{4,5},{5,4},{6,7},{7,6},{8,9},{9,8},{10,11... | collective-permute-start | bytes 786440 | tf_op jit(solution)/shard_map/ppermute | solution.py:30
  119.0 18.6 %all-to-all-start.2 = ((f32[8,48,256]{2,1,0:T(8,128)}), f32[8,48,256]{2,1,0:T(8,128)S(1)}, u32[]{:S(2)}, u32[]{:S(2)}) async-start(f32[8,48,256]{2,1,0:T(8,128)} %broadcast_in_dim.44), calls=%async_computation.2 | async-start | bytes 786432 | tf_op jit(solution)/shard_map/all_to_all | solution.py:34
  125.3 8.7 %collective-permute-start.10 = (f32[32,256]{1,0:T(8,128)S(1)}, f32[32,256]{1,0:T(8,128)S(1)}, u32[]{:S(2)}, u32[]{:S(2)}) collective-permute-start(f32[32,256]{1,0:T(8,128)S(1)} %dynamic-slice_bitcast_fusion), channel_id=1, source_target_pairs={{0,2},{2,0},{1,3},{3,1},{4,6},{6,4},{5,7},{7,5},{8,10},{10,8},{9,1... | collective-permute-start | bytes 98312 | tf_op jit(solution)/shard_map/ppermute | solution.py:30
  138.4 14.9 %all-to-all-start.3 = ((f32[8,48,256]{2,1,0:T(8,128)}), f32[8,48,256]{2,1,0:T(8,128)S(1)}, u32[]{:S(2)}, u32[]{:S(2)}) async-start(f32[8,48,256]{2,1,0:T(8,128)} %broadcast_in_dim.45), calls=%async_computation.3 | async-start | bytes 786432 | tf_op jit(solution)/shard_map/all_to_all | solution.py:34
  142.6 6.4 %collective-permute-start.11 = (f32[32,256]{1,0:T(8,128)S(1)}, f32[32,256]{1,0:T(8,128)S(1)}, u32[]{:S(2)}, u32[]{:S(2)}) collective-permute-start(f32[32,256]{1,0:T(8,128)S(1)} %fusion.9), channel_id=1, source_target_pairs={{0,1},{1,0},{2,3},{3,2},{4,5},{5,4},{6,7},{7,6},{8,9},{9,8},{10,11... | collective-permute-start | bytes 98312 | tf_op jit(solution)/shard_map/ppermute | solution.py:30
  154.1 4.5 %copy-start.6 = (f32[256,256]{1,0:T(8,128)S(1)}, f32[256,256]{1,0:T(8,128)}, u32[]{:S(2)}) copy-start(f32[256,256]{1,0:T(8,128)} %param.12) | copy-start | bytes 786436
  154.1 4.5 %copy-start.7 = (f32[256,256]{1,0:T(8,128)S(1)}, f32[256,256]{1,0:T(8,128)}, u32[]{:S(2)}) copy-start(f32[256,256]{1,0:T(8,128)} %param.11) | copy-start | bytes 786436
  154.1 15.2 %all-to-all-start.4 = ((f32[8,48,256]{2,1,0:T(8,128)}), f32[8,48,256]{2,1,0:T(8,128)S(1)}, u32[]{:S(2)}, u32[]{:S(2)}) async-start(f32[8,48,256]{2,1,0:T(8,128)} %broadcast_in_dim.46), calls=%async_computation.4 | async-start | bytes 786432 | tf_op jit(solution)/shard_map/all_to_all | solution.py:34
  169.4 8.5 %collective-permute-start.12 = (f32[384,256]{1,0:T(8,128)S(1)}, f32[384,256]{1,0:T(8,128)S(1)}, u32[]{:S(2)}, u32[]{:S(2)}) collective-permute-start(f32[384,256]{1,0:T(8,128)S(1)} %bitcast.78), channel_id=1, source_target_pairs={{0,1},{1,0},{2,3},{3,2},{4,5},{5,4},{6,7},{7,6},{8,9},{9,8},{10,11... | collective-permute-start | bytes 1179656 | tf_op jit(solution)/shard_map/ppermute | solution.py:30
  176.6 0.8 copy-start.8
  178.0 0.7 copy-start.4
  178.7 0.7 copy-start.5

commit v11 on v10

--- a/solution.py
+++ b/solution.py
@@ -108,7 +108,7 @@
     diag_one = lax.optimization_barrier(after(diag_one, column))
     diag_two = lax.optimization_barrier(after(diag_two, column))
 
-    grams = after(jnp.sum(gather(grams, "y"), axis=0), column)
+    grams = jnp.sum(gather(grams, "y"), axis=0)
     grams = after(jnp.sum(gather(grams, ("zh", "zl")), axis=0), sibling)
     grams = gather(grams, "x").reshape(-1, width)
     came = swap(grams, "core")

time: 182 us -> 188 us (1.033)
  blocking collectives: 27.6 us -> 45.4 us
  starting transfers between devices: 98.9 us -> 93.1 us
  waiting for transfers between devices: 37.8 us -> 33.3 us
    all_to_all x1 -> x2, blocking collectives: 27.6 us -> 45.4 us  [exchange(): return lax.all_to_all(a, axes, 0, 0, tiled=True)]
    all_to_all x4 -> x3, starting transfers between devices: 28 us -> 21.5 us  [exchange(): return lax.all_to_all(a, axes, 0, 0, tiled=True)]
    all_to_all x4 -> x3, waiting for transfers between devices: 18.5 us -> 15.1 us  [exchange(): return lax.all_to_all(a, axes, 0, 0, tiled=True)]
  transfers between devices with their start and end apart: 17 -> 16, of which waited for: 11 -> 9; matrix products, arithmetic and copies ran while one was open for 3% -> 3% of each run, Pallas kernels for 0% -> 0%
where the time goes in v11:
time: 188 us; the launch traced here: 187 us
  starting transfers between devices  93.1 us (50%)
  blocking collectives  45.4 us (24%)
  waiting for transfers between devices  33.3 us (18%)
  local copies, waits for them, and re-layouts  6.56 us (3%)
  matrix products  5.54 us (3%)
  other arithmetic  2.13 us (1%)
    ppermute x7, starting transfers between devices, swap(): return lax.ppermute(a, axis, SWAP)  47.4 us
    all_to_all x2, blocking collectives, exchange(): return lax.all_to_all(a, axes, 0, 0, tiled=True)  45.4 us
    all_to_all x3, starting transfers between devices, exchange(): return lax.all_to_all(a, axes, 0, 0, tiled=True)  21.5 us
    all_to_all x3, waiting for transfers between devices, exchange(): return lax.all_to_all(a, axes, 0, 0, tiled=True)  15.1 us
    ppermute x3, starting transfers between devices, local(): came = lax.ppermute(group, 'x', [(i, i ^ 2 * step) for i in range(nx)])  12.9 us
    ppermute x7, waiting for transfers between devices, swap(): return lax.ppermute(a, axis, SWAP)  6.89 us
    ppermute x1, starting transfers between devices, local(): lax.ppermute(rows, 'x', [(i, i ^ 1) for i in range(nx)])  5.93 us
    ppermute x1, waiting for transfers between devices, local(): lax.ppermute(rows, 'x', [(i, i ^ 1) for i in range(nx)])  5.75 us
  transfers between devices with their start and end apart: 16, of which 9 were waited for; matrix products, arithmetic and copies ran while one was open for 3% of the time, Pallas kernels for 0%

profile of v11, /device:TPU:1, one launch (start us, length us, event | category | flops | bytes accessed | tf_op | source)
XLA Modules:
  0.0 187.3 jit_solution(4276811804473231070)
XLA Ops:
  0.6 0.0 copy-start
  0.6 16.2 %collective-permute-start.2 = (f32[512,512]{1,0:T(8,128)}, f32[512,512]{1,0:T(8,128)S(1)}, u32[]{:S(2)}, u32[]{:S(2)}) collective-permute-start(f32[512,512]{1,0:T(8,128)} %param.7), channel_id=1, source_target_pairs={{0,1},{1,0},{2,3},{3,2},{4,5},{5,4},{6,7},{7,6},{8,9},{9,8},{10,11... | collective-permute-start | bytes 3145736 | tf_op jit(solution)/shard_map/ppermute | solution.py:30
  16.9 0.7 copy-done.11
  17.6 0.1 fusion.14
  17.6 0.5 fusion.17
  18.2 0.2 copy-done.9
  18.4 0.0 copy-done.10
  18.4 1.3 broadcast_select_fusion.7
  19.7 1.9 %collective-permute-start.1 = (f32[16,256]{1,0:T(8,128)S(1)}, f32[16,256]{1,0:T(8,128)S(1)}, u32[]{:S(2)}, u32[]{:S(2)}) collective-permute-start(f32[16,256]{1,0:T(8,128)S(1)} %broadcast_select_fusion.6), channel_id=1, source_target_pairs={{0,1},{1,33},{2,65},{3,97},{4,129},{5,161},{6,193},{7,225},{8,257}... | collective-permute-start | bytes 49160 | tf_op jit(solution)/shard_map/ppermute | solution.py:68
  21.6 3.5 %collective-permute-start = (f32[16,256]{1,0:T(8,128)S(1)}, f32[16,256]{1,0:T(8,128)S(1)}, u32[]{:S(2)}, u32[]{:S(2)}) collective-permute-start(f32[16,256]{1,0:T(8,128)S(1)} %get-tuple-element.5), channel_id=1, source_target_pairs={{0,0},{1,32},{2,64},{3,96},{4,128},{5,160},{6,192},{7,224},{8,256}... | collective-permute-start | bytes 49160 | tf_op jit(solution)/shard_map/ppermute | solution.py:67
  25.2 8.2 %collective-permute-start.3 = (f32[16,512]{1,0:T(8,128)S(1)}, f32[16,512]{1,0:T(8,128)S(1)}, u32[]{:S(2)}, u32[]{:S(2)}) collective-permute-start(f32[16,512]{1,0:T(8,128)S(1)} %pad_maximum_fusion.7), channel_id=1, source_target_pairs={{0,2},{2,0},{1,3},{3,1},{4,6},{6,4},{5,7},{7,5},{8,10},{10,8},{9,1... | collective-permute-start | bytes 98312 | tf_op jit(solution)/shard_map/ppermute | solution.py:30
  33.5 0.0 collective-permute-done.1
  33.5 0.0 collective-permute-done
  33.5 1.1 broadcast_in_dim.39
  34.6 13.0 %all-to-all-start = ((f32[32,2,16,256]{3,2,1,0:T(8,128)}), f32[32,2,16,256]{3,2,1,0:T(8,128)S(1)}, u32[]{:S(2)}, u32[]{:S(2)}) async-start(f32[32,2,16,256]{3,2,1,0:T(8,128)} %broadcast_in_dim.39), calls=%async_computation | async-start | bytes 2097152 | tf_op jit(solution)/shard_map/all_to_all | solution.py:34
  47.6 0.0 collective-permute-done.3
  47.6 0.0 collective-permute-done.2
  47.7 5.8 %collective-permute-start.4 = (f32[2,16,512]{2,1,0:T(8,128)S(1)}, f32[2,16,512]{2,1,0:T(8,128)S(1)}, u32[]{:S(2)}, u32[]{:S(2)}) collective-permute-start(f32[2,16,512]{2,1,0:T(8,128)S(1)} %maximum_add_fusion.1), channel_id=1, source_target_pairs={{0,8},{4,12},{8,0},{12,4},{16,24},{20,28},{24,16},{28,20},{1,9},{5... | collective-permute-start | bytes 196616 | tf_op jit(solution)/shard_map/ppermute | solution.py:81
  53.5 4.9 %collective-permute-start.5 = (f32[2,16,512]{2,1,0:T(8,128)S(1)}, f32[2,16,512]{2,1,0:T(8,128)S(1)}, u32[]{:S(2)}, u32[]{:S(2)}) collective-permute-start(f32[2,16,512]{2,1,0:T(8,128)S(1)} %maximum_add_fusion.1), channel_id=1, source_target_pairs={{0,16},{4,20},{8,24},{12,28},{16,0},{20,4},{24,8},{28,12},{1,17},{... | collective-permute-start | bytes 196616 | tf_op jit(solution)/shard_map/ppermute | solution.py:81
  58.3 2.2 %collective-permute-start.6 = (f32[2,16,512]{2,1,0:T(8,128)S(1)}, f32[2,16,512]{2,1,0:T(8,128)S(1)}, u32[]{:S(2)}, u32[]{:S(2)}) collective-permute-start(f32[2,16,512]{2,1,0:T(8,128)S(1)} %maximum_add_fusion.1), channel_id=1, source_target_pairs={{0,24},{4,28},{8,16},{12,20},{16,8},{20,12},{24,0},{28,4},{1,25},{... | collective-permute-start | bytes 196616 | tf_op jit(solution)/shard_map/ppermute | solution.py:81
  60.6 0.0 collective-permute-done.4
  60.7 1.7 collective-permute-done.5
  62.4 3.9 %collective-permute-done.6 = f32[2,16,512]{2,1,0:T(8,128)S(1)} collective-permute-done((f32[2,16,512]{2,1,0:T(8,128)S(1)}, f32[2,16,512]{2,1,0:T(8,128)S(1)}, u32[]{:S(2)}, u32[]{:S(2)}) %collective-permute-start.6) | collective-permute-done | bytes 65568 | tf_op jit(solution)/shard_map/ppermute | solution.py:81
  66.3 5.9 %collective-permute-start.7 = (f32[4,2,16,512]{3,2,1,0:T(8,128)S(1)}, f32[4,2,16,512]{3,2,1,0:T(8,128)S(1)}, u32[]{:S(2)}, u32[]{:S(2)}) collective-permute-start(f32[4,2,16,512]{3,2,1,0:T(8,128)S(1)} %bitcast_dynamic-update-slice_fusion), channel_id=1, source_target_pairs={{0,4},{4,0},{8,12},{12,8},{16,20},{20,16},{24,28},{28,24},{1,5},{5... | collective-permute-start | bytes 786440 | tf_op jit(solution)/shard_map/ppermute | solution.py:83
  72.2 5.8 %collective-permute-done.7 = f32[4,2,16,512]{3,2,1,0:T(8,128)S(1)} collective-permute-done((f32[4,2,16,512]{3,2,1,0:T(8,128)S(1)}, f32[4,2,16,512]{3,2,1,0:T(8,128)S(1)}, u32[]{:S(2)}, u32[]{:S(2)}) %collective-permute-start.7) | collective-permute-done | bytes 262176 | tf_op jit(solution)/shard_map/ppermute | solution.py:83
  78.1 3.4 %collective-permute-start.8 = (f32[4,2,2,16,512]{4,3,2,1,0:T(8,128)S(1)}, f32[4,2,2,16,512]{4,3,2,1,0:T(8,128)S(1)}, u32[]{:S(2)}, u32[]{:S(2)}) collective-permute-start(f32[4,2,2,16,512]{4,3,2,1,0:T(8,128)S(1)} %pad_maximum_fusion.2), channel_id=1, source_target_pairs={{0,1},{1,0},{2,3},{3,2},{4,5},{5,4},{6,7},{7,6},{8,9},{9,8},{10,11... | collective-permute-start | bytes 1572872 | tf_op jit(solution)/shard_map/ppermute | solution.py:30
  81.5 1.5 collective-permute-done.8
  83.0 0.1 select_bitcast_fusion.1
  83.1 0.0 copy-start.3
  83.2 0.1 fusion.16
  83.2 1.1 copy-done.3
  84.4 1.0 fusion.18
  85.4 0.2 copy-done.2
  85.6 1.0 convolution_add_fusion
  86.7 2.3 %collective-permute-start.9 = (f32[512,128]{0,1:T(8,128)S(1)}, f32[512,128]{0,1:T(8,128)S(1)}, u32[]{:S(2)}, u32[]{:S(2)}) collective-permute-start(f32[512,128]{0,1:T(8,128)S(1)} %slice.75), channel_id=1, source_target_pairs={{0,1},{1,0},{2,3},{3,2},{4,5},{5,4},{6,7},{7,6},{8,9},{9,8},{10,11... | collective-permute-start | bytes 786440 | tf_op jit(solution)/shard_map/ppermute | solution.py:30
  89.0 0.1 pad_maximum_fusion
  89.1 0.2 copy.18
  89.3 0.6 fusion.2
  89.9 0.2 collective-permute-done.9
  90.1 0.3 fusion.3
  90.4 0.1 pad_maximum_fusion.1
  90.5 27.6 %all_to_all.25 = f32[8,112,256]{2,1,0:T(8,128)S(1)} all-to-all(f32[8,112,256]{2,1,0:T(8,128)S(1)} %pad_maximum_fusion.1), channel_id=1, replica_groups=mesh['zl'=4,'y'=8,'x'=8,'zh'=2,'core'=2] {'x'}, dimensions={0} | all-to-all | bytes 1835008 | tf_op jit(solution)/shard_map/all_to_all | solution.py:34
  118.2 0.1 reduce_sum.27
  118.3 17.7 %all_to_all.26 = f32[8,48,256]{2,1,0:T(8,128)S(1)} all-to-all(f32[8,48,256]{2,1,0:T(8,128)S(1)} %broadcast_in_dim.44), channel_id=1, replica_groups=mesh['zl'=4,'y'=8,'x'=8,'zh'=2,'core'=2] {'y'}, dimensions={0} | all-to-all | bytes 786432 | tf_op jit(solution)/shard_map/all_to_all | solution.py:34
  136.0 0.8 broadcast_in_dim.45
  136.8 4.2 %all-to-all-start.3 = ((f32[8,48,256]{2,1,0:T(8,128)}), f32[8,48,256]{2,1,0:T(8,128)S(1)}, u32[]{:S(2)}, u32[]{:S(2)}) async-start(f32[8,48,256]{2,1,0:T(8,128)} %broadcast_in_dim.45), calls=%async_computation.3 | async-start | bytes 786432 | tf_op jit(solution)/shard_map/all_to_all | solution.py:34
  141.1 7.3 %collective-permute-start.10 = (f32[32,256]{1,0:T(8,128)S(1)}, f32[32,256]{1,0:T(8,128)S(1)}, u32[]{:S(2)}, u32[]{:S(2)}) collective-permute-start(f32[32,256]{1,0:T(8,128)S(1)} %dynamic-slice_bitcast_fusion), channel_id=1, source_target_pairs={{0,2},{2,0},{1,3},{3,1},{4,6},{6,4},{5,7},{7,5},{8,10},{10,8},{9,1... | collective-permute-start | bytes 98312 | tf_op jit(solution)/shard_map/ppermute | solution.py:30
  148.3 3.9 %collective-permute-done.10 = f32[32,256]{1,0:T(8,128)S(1)} collective-permute-done((f32[32,256]{1,0:T(8,128)S(1)}, f32[32,256]{1,0:T(8,128)S(1)}, u32[]{:S(2)}, u32[]{:S(2)}) %collective-permute-start.10) | collective-permute-done | bytes 32800 | tf_op jit(solution)/shard_map/ppermute | solution.py:30
  152.2 7.6 %collective-permute-start.11 = (f32[32,256]{1,0:T(8,128)S(1)}, f32[32,256]{1,0:T(8,128)S(1)}, u32[]{:S(2)}, u32[]{:S(2)}) collective-permute-start(f32[32,256]{1,0:T(8,128)S(1)} %fusion.9), channel_id=1, source_target_pairs={{0,1},{1,0},{2,3},{3,2},{4,5},{5,4},{6,7},{7,6},{8,9},{9,8},{10,11... | collective-permute-start | bytes 98312 | tf_op jit(solution)/shard_map/ppermute | solution.py:30
  159.9 0.8 collective-permute-done.11
  160.7 0.8 broadcast_in_dim.46
  161.5 4.2 %all-to-all-start.4 = ((f32[8,48,256]{2,1,0:T(8,128)}), f32[8,48,256]{2,1,0:T(8,128)S(1)}, u32[]{:S(2)}, u32[]{:S(2)}) async-start(f32[8,48,256]{2,1,0:T(8,128)} %broadcast_in_dim.46), calls=%async_computation.4 | async-start | bytes 786432 | tf_op jit(solution)/shard_map/all_to_all | solution.py:34
  165.8 15.1 %all-to-all-done.4 = f32[8,48,256]{2,1,0:T(8,128)S(1)} async-done(((f32[8,48,256]{2,1,0:T(8,128)}), f32[8,48,256]{2,1,0:T(8,128)S(1)}, u32[]{:S(2)}, u32[]{:S(2)}) %all-to-all-start.4) | async-done | bytes 393248 | tf_op jit(solution)/shard_map/all_to_all | solution.py:34
  180.9 2.4 %collective-permute-start.12 = (f32[384,256]{1,0:T(8,128)S(1)}, f32[384,256]{1,0:T(8,128)S(1)}, u32[]{:S(2)}, u32[]{:S(2)}) collective-permute-start(f32[384,256]{1,0:T(8,128)S(1)} %bitcast.78), channel_id=1, source_target_pairs={{0,1},{1,0},{2,3},{3,2},{4,5},{5,4},{6,7},{7,6},{8,9},{9,8},{10,11... | collective-permute-start | bytes 1179656 | tf_op jit(solution)/shard_map/ppermute | solution.py:30
  183.4 0.0 copy-start.8
  183.4 0.8 bitcast_subtract_fusion
  184.2 0.5 collective-permute-done.12
  184.6 0.1 broadcast_select_fusion
  184.8 0.0 copy-start.4
  184.8 0.3 convolution_subtract_fusion.1
  185.1 0.4 copy-done.4
  185.5 0.4 convolution_bitcast_fusion
  185.9 0.3 copy-done.5
  186.2 1.1 fusion.1
  (46 shorter events, 0.5 us)
Async XLA Ops:
  0.6 182.7 %copy-start = (f32[256,256]{1,0:T(8,128)S(1)}, f32[256,256]{1,0:T(8,128)}, u32[]{:S(2)}) copy-start(f32[256,256]{1,0:T(8,128)} %param.13) | copy-start | bytes 786436
  0.6 47.0 %collective-permute-start.2 = (f32[512,512]{1,0:T(8,128)}, f32[512,512]{1,0:T(8,128)S(1)}, u32[]{:S(2)}, u32[]{:S(2)}) collective-permute-start(f32[512,512]{1,0:T(8,128)} %param.7), channel_id=1, source_target_pairs={{0,1},{1,0},{2,3},{3,2},{4,5},{5,4},{6,7},{7,6},{8,9},{9,8},{10,11... | collective-permute-start | bytes 3145736 | tf_op jit(solution)/shard_map/ppermute | solution.py:30
  16.9 0.7 copy-start.11
  17.6 0.7 copy-start.9
  17.6 0.7 copy-start.10
  19.7 13.8 %collective-permute-start.1 = (f32[16,256]{1,0:T(8,128)S(1)}, f32[16,256]{1,0:T(8,128)S(1)}, u32[]{:S(2)}, u32[]{:S(2)}) collective-permute-start(f32[16,256]{1,0:T(8,128)S(1)} %broadcast_select_fusion.6), channel_id=1, source_target_pairs={{0,1},{1,33},{2,65},{3,97},{4,129},{5,161},{6,193},{7,225},{8,257}... | collective-permute-start | bytes 49160 | tf_op jit(solution)/shard_map/ppermute | solution.py:68
  21.6 11.8 %collective-permute-start = (f32[16,256]{1,0:T(8,128)S(1)}, f32[16,256]{1,0:T(8,128)S(1)}, u32[]{:S(2)}, u32[]{:S(2)}) collective-permute-start(f32[16,256]{1,0:T(8,128)S(1)} %get-tuple-element.5), channel_id=1, source_target_pairs={{0,0},{1,32},{2,64},{3,96},{4,128},{5,160},{6,192},{7,224},{8,256}... | collective-permute-start | bytes 49160 | tf_op jit(solution)/shard_map/ppermute | solution.py:67
  25.2 22.4 %collective-permute-start.3 = (f32[16,512]{1,0:T(8,128)S(1)}, f32[16,512]{1,0:T(8,128)S(1)}, u32[]{:S(2)}, u32[]{:S(2)}) collective-permute-start(f32[16,512]{1,0:T(8,128)S(1)} %pad_maximum_fusion.7), channel_id=1, source_target_pairs={{0,2},{2,0},{1,3},{3,1},{4,6},{6,4},{5,7},{7,5},{8,10},{10,8},{9,1... | collective-permute-start | bytes 98312 | tf_op jit(solution)/shard_map/ppermute | solution.py:30
  34.6 48.5 %all-to-all-start = ((f32[32,2,16,256]{3,2,1,0:T(8,128)}), f32[32,2,16,256]{3,2,1,0:T(8,128)S(1)}, u32[]{:S(2)}, u32[]{:S(2)}) async-start(f32[32,2,16,256]{3,2,1,0:T(8,128)} %broadcast_in_dim.39), calls=%async_computation | async-start | bytes 2097152 | tf_op jit(solution)/shard_map/all_to_all | solution.py:34
  47.6 24.6 %copy-start.1 = (f32[512,512]{1,0:T(8,128)}, f32[512,512]{1,0:T(8,128)S(1)}, u32[]{:S(2)}) copy-start(f32[512,512]{1,0:T(8,128)S(1)} %collective-permute-done.2) | copy-start | bytes 3145732
  47.7 13.0 %collective-permute-start.4 = (f32[2,16,512]{2,1,0:T(8,128)S(1)}, f32[2,16,512]{2,1,0:T(8,128)S(1)}, u32[]{:S(2)}, u32[]{:S(2)}) collective-permute-start(f32[2,16,512]{2,1,0:T(8,128)S(1)} %maximum_add_fusion.1), channel_id=1, source_target_pairs={{0,8},{4,12},{8,0},{12,4},{16,24},{20,28},{24,16},{28,20},{1,9},{5... | collective-permute-start | bytes 196616 | tf_op jit(solution)/shard_map/ppermute | solution.py:81
  53.5 8.9 %collective-permute-start.5 = (f32[2,16,512]{2,1,0:T(8,128)S(1)}, f32[2,16,512]{2,1,0:T(8,128)S(1)}, u32[]{:S(2)}, u32[]{:S(2)}) collective-permute-start(f32[2,16,512]{2,1,0:T(8,128)S(1)} %maximum_add_fusion.1), channel_id=1, source_target_pairs={{0,16},{4,20},{8,24},{12,28},{16,0},{20,4},{24,8},{28,12},{1,17},{... | collective-permute-start | bytes 196616 | tf_op jit(solution)/shard_map/ppermute | solution.py:81
  58.3 7.9 %collective-permute-start.6 = (f32[2,16,512]{2,1,0:T(8,128)S(1)}, f32[2,16,512]{2,1,0:T(8,128)S(1)}, u32[]{:S(2)}, u32[]{:S(2)}) collective-permute-start(f32[2,16,512]{2,1,0:T(8,128)S(1)} %maximum_add_fusion.1), channel_id=1, source_target_pairs={{0,24},{4,28},{8,16},{12,20},{16,8},{20,12},{24,0},{28,4},{1,25},{... | collective-permute-start | bytes 196616 | tf_op jit(solution)/shard_map/ppermute | solution.py:81
  66.3 11.7 %collective-permute-start.7 = (f32[4,2,16,512]{3,2,1,0:T(8,128)S(1)}, f32[4,2,16,512]{3,2,1,0:T(8,128)S(1)}, u32[]{:S(2)}, u32[]{:S(2)}) collective-permute-start(f32[4,2,16,512]{3,2,1,0:T(8,128)S(1)} %bitcast_dynamic-update-slice_fusion), channel_id=1, source_target_pairs={{0,4},{4,0},{8,12},{12,8},{16,20},{20,16},{24,28},{28,24},{1,5},{5... | collective-permute-start | bytes 786440 | tf_op jit(solution)/shard_map/ppermute | solution.py:83
  78.1 4.9 %collective-permute-start.8 = (f32[4,2,2,16,512]{4,3,2,1,0:T(8,128)S(1)}, f32[4,2,2,16,512]{4,3,2,1,0:T(8,128)S(1)}, u32[]{:S(2)}, u32[]{:S(2)}) collective-permute-start(f32[4,2,2,16,512]{4,3,2,1,0:T(8,128)S(1)} %pad_maximum_fusion.2), channel_id=1, source_target_pairs={{0,1},{1,0},{2,3},{3,2},{4,5},{5,4},{6,7},{7,6},{8,9},{9,8},{10,11... | collective-permute-start | bytes 1572872 | tf_op jit(solution)/shard_map/ppermute | solution.py:30
  83.1 1.2 copy-start.3
  84.4 1.2 copy-start.2
  86.7 3.4 %collective-permute-start.9 = (f32[512,128]{0,1:T(8,128)S(1)}, f32[512,128]{0,1:T(8,128)S(1)}, u32[]{:S(2)}, u32[]{:S(2)}) collective-permute-start(f32[512,128]{0,1:T(8,128)S(1)} %slice.75), channel_id=1, source_target_pairs={{0,1},{1,0},{2,3},{3,2},{4,5},{5,4},{6,7},{7,6},{8,9},{9,8},{10,11... | collective-permute-start | bytes 786440 | tf_op jit(solution)/shard_map/ppermute | solution.py:30
  136.8 23.9 %all-to-all-start.3 = ((f32[8,48,256]{2,1,0:T(8,128)}), f32[8,48,256]{2,1,0:T(8,128)S(1)}, u32[]{:S(2)}, u32[]{:S(2)}) async-start(f32[8,48,256]{2,1,0:T(8,128)} %broadcast_in_dim.45), calls=%async_computation.3 | async-start | bytes 786432 | tf_op jit(solution)/shard_map/all_to_all | solution.py:34
  141.1 11.1 %collective-permute-start.10 = (f32[32,256]{1,0:T(8,128)S(1)}, f32[32,256]{1,0:T(8,128)S(1)}, u32[]{:S(2)}, u32[]{:S(2)}) collective-permute-start(f32[32,256]{1,0:T(8,128)S(1)} %dynamic-slice_bitcast_fusion), channel_id=1, source_target_pairs={{0,2},{2,0},{1,3},{3,1},{4,6},{6,4},{5,7},{7,5},{8,10},{10,8},{9,1... | collective-permute-start | bytes 98312 | tf_op jit(solution)/shard_map/ppermute | solution.py:30
  152.2 8.5 %collective-permute-start.11 = (f32[32,256]{1,0:T(8,128)S(1)}, f32[32,256]{1,0:T(8,128)S(1)}, u32[]{:S(2)}, u32[]{:S(2)}) collective-permute-start(f32[32,256]{1,0:T(8,128)S(1)} %fusion.9), channel_id=1, source_target_pairs={{0,1},{1,0},{2,3},{3,2},{4,5},{5,4},{6,7},{7,6},{8,9},{9,8},{10,11... | collective-permute-start | bytes 98312 | tf_op jit(solution)/shard_map/ppermute | solution.py:30
  161.5 4.2 %copy-start.6 = (f32[256,256]{1,0:T(8,128)S(1)}, f32[256,256]{1,0:T(8,128)}, u32[]{:S(2)}) copy-start(f32[256,256]{1,0:T(8,128)} %param.12) | copy-start | bytes 786436
  161.5 4.3 %copy-start.7 = (f32[256,256]{1,0:T(8,128)S(1)}, f32[256,256]{1,0:T(8,128)}, u32[]{:S(2)}) copy-start(f32[256,256]{1,0:T(8,128)} %param.11) | copy-start | bytes 786436
  161.5 19.4 %all-to-all-start.4 = ((f32[8,48,256]{2,1,0:T(8,128)}), f32[8,48,256]{2,1,0:T(8,128)S(1)}, u32[]{:S(2)}, u32[]{:S(2)}) async-start(f32[8,48,256]{2,1,0:T(8,128)} %broadcast_in_dim.46), calls=%async_computation.4 | async-start | bytes 786432 | tf_op jit(solution)/shard_map/all_to_all | solution.py:34
  180.9 3.7 %collective-permute-start.12 = (f32[384,256]{1,0:T(8,128)S(1)}, f32[384,256]{1,0:T(8,128)S(1)}, u32[]{:S(2)}, u32[]{:S(2)}) collective-permute-start(f32[384,256]{1,0:T(8,128)S(1)} %bitcast.78), channel_id=1, source_target_pairs={{0,1},{1,0},{2,3},{3,2},{4,5},{5,4},{6,7},{7,6},{8,9},{9,8},{10,11... | collective-permute-start | bytes 1179656 | tf_op jit(solution)/shard_map/ppermute | solution.py:30
  183.4 0.8 copy-start.8
  184.8 0.7 copy-start.4
  185.5 0.7 copy-start.5

commit v12 on v10

--- a/solution.py
+++ b/solution.py
@@ -109,7 +109,7 @@
     diag_two = lax.optimization_barrier(after(diag_two, column))
 
     grams = after(jnp.sum(gather(grams, "y"), axis=0), column)
-    grams = after(jnp.sum(gather(grams, ("zh", "zl")), axis=0), sibling)
+    grams = jnp.sum(gather(grams, ("zh", "zl")), axis=0)
     grams = gather(grams, "x").reshape(-1, width)
     came = swap(grams, "core")
     lower, upper = jnp.where(first, grams, came), jnp.where(first, came, grams)

time: 182 us -> 181 us (level)
  blocking collectives: 27.6 us -> 42.3 us
  waiting for transfers between devices: 37.8 us -> 26.2 us
  starting transfers between devices: 98.9 us -> 95.6 us
    all_to_all x1 -> x2, blocking collectives: 27.6 us -> 42.3 us  [exchange(): return lax.all_to_all(a, axes, 0, 0, tiled=True)]
    all_to_all x4 -> x3, waiting for transfers between devices: 18.5 us -> 7.81 us  [exchange(): return lax.all_to_all(a, axes, 0, 0, tiled=True)]
    all_to_all x4 -> x3, starting transfers between devices: 28 us -> 23.5 us  [exchange(): return lax.all_to_all(a, axes, 0, 0, tiled=True)]
  transfers between devices with their start and end apart: 17 -> 16, of which waited for: 11 -> 9; matrix products, arithmetic and copies ran while one was open for 3% -> 3% of each run, Pallas kernels for 0% -> 0%
where the time goes in v12:
time: 181 us; the launch traced here: 180 us
  starting transfers between devices  95.6 us (53%)
  blocking collectives  42.3 us (23%)
  waiting for transfers between devices  26.2 us (14%)
  local copies, waits for them, and re-layouts  6.56 us (4%)
  matrix products  5.54 us (3%)
  other arithmetic  2.13 us (1%)
    ppermute x7, starting transfers between devices, swap(): return lax.ppermute(a, axis, SWAP)  47.8 us
    all_to_all x2, blocking collectives, exchange(): return lax.all_to_all(a, axes, 0, 0, tiled=True)  42.3 us
    all_to_all x3, starting transfers between devices, exchange(): return lax.all_to_all(a, axes, 0, 0, tiled=True)  23.5 us
    ppermute x3, starting transfers between devices, local(): came = lax.ppermute(group, 'x', [(i, i ^ 2 * step) for i in range(nx)])  12.9 us
    all_to_all x3, waiting for transfers between devices, exchange(): return lax.all_to_all(a, axes, 0, 0, tiled=True)  7.81 us
    ppermute x7, waiting for transfers between devices, swap(): return lax.ppermute(a, axis, SWAP)  7.12 us
    ppermute x1, starting transfers between devices, local(): lax.ppermute(rows, 'x', [(i, i ^ 1) for i in range(nx)])  5.93 us
    ppermute x1, waiting for transfers between devices, local(): lax.ppermute(rows, 'x', [(i, i ^ 1) for i in range(nx)])  5.75 us
  transfers between devices with their start and end apart: 16, of which 9 were waited for; matrix products, arithmetic and copies ran while one was open for 3% of the time, Pallas kernels for 0%

profile of v12, /device:TPU:1, one launch (start us, length us, event | category | flops | bytes accessed | tf_op | source)
XLA Modules:
  0.0 179.6 jit_solution(817616345940053628)
XLA Ops:
  0.6 0.0 copy-start
  0.6 16.2 %collective-permute-start.2 = (f32[512,512]{1,0:T(8,128)}, f32[512,512]{1,0:T(8,128)S(1)}, u32[]{:S(2)}, u32[]{:S(2)}) collective-permute-start(f32[512,512]{1,0:T(8,128)} %param.7), channel_id=1, source_target_pairs={{0,1},{1,0},{2,3},{3,2},{4,5},{5,4},{6,7},{7,6},{8,9},{9,8},{10,11... | collective-permute-start | bytes 3145736 | tf_op jit(solution)/shard_map/ppermute | solution.py:30
  16.9 0.7 copy-done.11
  17.6 0.1 fusion.14
  17.6 0.5 fusion.17
  18.2 0.2 copy-done.9
  18.4 0.0 copy-done.10
  18.4 1.3 broadcast_select_fusion.7
  19.7 1.9 %collective-permute-start.1 = (f32[16,256]{1,0:T(8,128)S(1)}, f32[16,256]{1,0:T(8,128)S(1)}, u32[]{:S(2)}, u32[]{:S(2)}) collective-permute-start(f32[16,256]{1,0:T(8,128)S(1)} %broadcast_select_fusion.6), channel_id=1, source_target_pairs={{0,1},{1,33},{2,65},{3,97},{4,129},{5,161},{6,193},{7,225},{8,257}... | collective-permute-start | bytes 49160 | tf_op jit(solution)/shard_map/ppermute | solution.py:68
  21.6 3.5 %collective-permute-start = (f32[16,256]{1,0:T(8,128)S(1)}, f32[16,256]{1,0:T(8,128)S(1)}, u32[]{:S(2)}, u32[]{:S(2)}) collective-permute-start(f32[16,256]{1,0:T(8,128)S(1)} %get-tuple-element.5), channel_id=1, source_target_pairs={{0,0},{1,32},{2,64},{3,96},{4,128},{5,160},{6,192},{7,224},{8,256}... | collective-permute-start | bytes 49160 | tf_op jit(solution)/shard_map/ppermute | solution.py:67
  25.2 8.2 %collective-permute-start.3 = (f32[16,512]{1,0:T(8,128)S(1)}, f32[16,512]{1,0:T(8,128)S(1)}, u32[]{:S(2)}, u32[]{:S(2)}) collective-permute-start(f32[16,512]{1,0:T(8,128)S(1)} %pad_maximum_fusion.7), channel_id=1, source_target_pairs={{0,2},{2,0},{1,3},{3,1},{4,6},{6,4},{5,7},{7,5},{8,10},{10,8},{9,1... | collective-permute-start | bytes 98312 | tf_op jit(solution)/shard_map/ppermute | solution.py:30
  33.5 0.0 collective-permute-done.1
  33.5 0.0 collective-permute-done
  33.5 1.1 broadcast_in_dim.39
  34.6 13.0 %all-to-all-start = ((f32[32,2,16,256]{3,2,1,0:T(8,128)}), f32[32,2,16,256]{3,2,1,0:T(8,128)S(1)}, u32[]{:S(2)}, u32[]{:S(2)}) async-start(f32[32,2,16,256]{3,2,1,0:T(8,128)} %broadcast_in_dim.39), calls=%async_computation | async-start | bytes 2097152 | tf_op jit(solution)/shard_map/all_to_all | solution.py:34
  47.6 0.0 collective-permute-done.2
  47.7 5.8 %collective-permute-start.4 = (f32[2,16,512]{2,1,0:T(8,128)S(1)}, f32[2,16,512]{2,1,0:T(8,128)S(1)}, u32[]{:S(2)}, u32[]{:S(2)}) collective-permute-start(f32[2,16,512]{2,1,0:T(8,128)S(1)} %maximum_add_fusion.1), channel_id=1, source_target_pairs={{0,8},{4,12},{8,0},{12,4},{16,24},{20,28},{24,16},{28,20},{1,9},{5... | collective-permute-start | bytes 196616 | tf_op jit(solution)/shard_map/ppermute | solution.py:81
  53.5 4.9 %collective-permute-start.5 = (f32[2,16,512]{2,1,0:T(8,128)S(1)}, f32[2,16,512]{2,1,0:T(8,128)S(1)}, u32[]{:S(2)}, u32[]{:S(2)}) collective-permute-start(f32[2,16,512]{2,1,0:T(8,128)S(1)} %maximum_add_fusion.1), channel_id=1, source_target_pairs={{0,16},{4,20},{8,24},{12,28},{16,0},{20,4},{24,8},{28,12},{1,17},{... | collective-permute-start | bytes 196616 | tf_op jit(solution)/shard_map/ppermute | solution.py:81
  58.3 2.2 %collective-permute-start.6 = (f32[2,16,512]{2,1,0:T(8,128)S(1)}, f32[2,16,512]{2,1,0:T(8,128)S(1)}, u32[]{:S(2)}, u32[]{:S(2)}) collective-permute-start(f32[2,16,512]{2,1,0:T(8,128)S(1)} %maximum_add_fusion.1), channel_id=1, source_target_pairs={{0,24},{4,28},{8,16},{12,20},{16,8},{20,12},{24,0},{28,4},{1,25},{... | collective-permute-start | bytes 196616 | tf_op jit(solution)/shard_map/ppermute | solution.py:81
  60.7 1.7 collective-permute-done.5
  62.4 3.9 %collective-permute-done.6 = f32[2,16,512]{2,1,0:T(8,128)S(1)} collective-permute-done((f32[2,16,512]{2,1,0:T(8,128)S(1)}, f32[2,16,512]{2,1,0:T(8,128)S(1)}, u32[]{:S(2)}, u32[]{:S(2)}) %collective-permute-start.6) | collective-permute-done | bytes 65568 | tf_op jit(solution)/shard_map/ppermute | solution.py:81
  66.3 5.9 %collective-permute-start.7 = (f32[4,2,16,512]{3,2,1,0:T(8,128)S(1)}, f32[4,2,16,512]{3,2,1,0:T(8,128)S(1)}, u32[]{:S(2)}, u32[]{:S(2)}) collective-permute-start(f32[4,2,16,512]{3,2,1,0:T(8,128)S(1)} %bitcast_dynamic-update-slice_fusion), channel_id=1, source_target_pairs={{0,4},{4,0},{8,12},{12,8},{16,20},{20,16},{24,28},{28,24},{1,5},{5... | collective-permute-start | bytes 786440 | tf_op jit(solution)/shard_map/ppermute | solution.py:83
  72.2 5.8 %collective-permute-done.7 = f32[4,2,16,512]{3,2,1,0:T(8,128)S(1)} collective-permute-done((f32[4,2,16,512]{3,2,1,0:T(8,128)S(1)}, f32[4,2,16,512]{3,2,1,0:T(8,128)S(1)}, u32[]{:S(2)}, u32[]{:S(2)}) %collective-permute-start.7) | collective-permute-done | bytes 262176 | tf_op jit(solution)/shard_map/ppermute | solution.py:83
  78.1 3.4 %collective-permute-start.8 = (f32[4,2,2,16,512]{4,3,2,1,0:T(8,128)S(1)}, f32[4,2,2,16,512]{4,3,2,1,0:T(8,128)S(1)}, u32[]{:S(2)}, u32[]{:S(2)}) collective-permute-start(f32[4,2,2,16,512]{4,3,2,1,0:T(8,128)S(1)} %pad_maximum_fusion.2), channel_id=1, source_target_pairs={{0,1},{1,0},{2,3},{3,2},{4,5},{5,4},{6,7},{7,6},{8,9},{9,8},{10,11... | collective-permute-start | bytes 1572872 | tf_op jit(solution)/shard_map/ppermute | solution.py:30
  81.5 1.5 collective-permute-done.8
  83.0 0.1 select_bitcast_fusion.1
  83.1 0.0 all-to-all-done
  83.1 0.0 copy-start.3
  83.2 0.1 fusion.16
  83.2 1.1 copy-done.3
  84.4 1.0 fusion.18
  85.4 0.2 copy-done.2
  85.6 1.0 convolution_add_fusion
  86.7 2.3 %collective-permute-start.9 = (f32[512,128]{0,1:T(8,128)S(1)}, f32[512,128]{0,1:T(8,128)S(1)}, u32[]{:S(2)}, u32[]{:S(2)}) collective-permute-start(f32[512,128]{0,1:T(8,128)S(1)} %slice.72), channel_id=1, source_target_pairs={{0,1},{1,0},{2,3},{3,2},{4,5},{5,4},{6,7},{7,6},{8,9},{9,8},{10,11... | collective-permute-start | bytes 786440 | tf_op jit(solution)/shard_map/ppermute | solution.py:30
  89.0 0.1 pad_maximum_fusion
  89.1 0.2 copy.18
  89.3 0.6 fusion.2
  89.9 0.2 collective-permute-done.9
  90.1 0.3 fusion.3
  90.4 0.1 pad_maximum_fusion.1
  90.5 27.6 %all_to_all.25 = f32[8,112,256]{2,1,0:T(8,128)S(1)} all-to-all(f32[8,112,256]{2,1,0:T(8,128)S(1)} %pad_maximum_fusion.1), channel_id=1, replica_groups=mesh['zl'=4,'y'=8,'x'=8,'zh'=2,'core'=2] {'x'}, dimensions={0} | all-to-all | bytes 1835008 | tf_op jit(solution)/shard_map/all_to_all | solution.py:34
  118.2 0.1 reduce_sum.27
  118.2 0.8 broadcast_in_dim.44
  119.0 6.3 %all-to-all-start.2 = ((f32[8,48,256]{2,1,0:T(8,128)}), f32[8,48,256]{2,1,0:T(8,128)S(1)}, u32[]{:S(2)}, u32[]{:S(2)}) async-start(f32[8,48,256]{2,1,0:T(8,128)} %broadcast_in_dim.44), calls=%async_computation.2 | async-start | bytes 786432 | tf_op jit(solution)/shard_map/all_to_all | solution.py:34
  125.4 3.7 %collective-permute-start.10 = (f32[32,256]{1,0:T(8,128)S(1)}, f32[32,256]{1,0:T(8,128)S(1)}, u32[]{:S(2)}, u32[]{:S(2)}) collective-permute-start(f32[32,256]{1,0:T(8,128)S(1)} %dynamic-slice_bitcast_fusion), channel_id=1, source_target_pairs={{0,2},{2,0},{1,3},{3,1},{4,6},{6,4},{5,7},{7,5},{8,10},{10,8},{9,1... | collective-permute-start | bytes 98312 | tf_op jit(solution)/shard_map/ppermute | solution.py:30
  129.1 4.9 %collective-permute-done.10 = f32[32,256]{1,0:T(8,128)S(1)} collective-permute-done((f32[32,256]{1,0:T(8,128)S(1)}, f32[32,256]{1,0:T(8,128)S(1)}, u32[]{:S(2)}, u32[]{:S(2)}) %collective-permute-start.10) | collective-permute-done | bytes 32800 | tf_op jit(solution)/shard_map/ppermute | solution.py:30
  134.0 3.5 %all-to-all-done.2 = f32[8,48,256]{2,1,0:T(8,128)S(1)} async-done(((f32[8,48,256]{2,1,0:T(8,128)}), f32[8,48,256]{2,1,0:T(8,128)S(1)}, u32[]{:S(2)}, u32[]{:S(2)}) %all-to-all-start.2) | async-done | bytes 393248 | tf_op jit(solution)/shard_map/all_to_all | solution.py:34
  137.7 14.6 %all_to_all.26 = f32[8,48,256]{2,1,0:T(8,128)S(1)} all-to-all(f32[8,48,256]{2,1,0:T(8,128)S(1)} %broadcast_in_dim.45), channel_id=1, replica_groups=mesh['zl'=4,'y'=8,'x'=8,'zh'=2,'core'=2] {'zh','zl'}, dimensions={0} | all-to-all | bytes 786432 | tf_op jit(solution)/shard_map/all_to_all | solution.py:34
  152.3 0.8 broadcast_in_dim.46
  153.1 4.2 %all-to-all-start.4 = ((f32[8,48,256]{2,1,0:T(8,128)}), f32[8,48,256]{2,1,0:T(8,128)S(1)}, u32[]{:S(2)}, u32[]{:S(2)}) async-start(f32[8,48,256]{2,1,0:T(8,128)} %broadcast_in_dim.46), calls=%async_computation.4 | async-start | bytes 786432 | tf_op jit(solution)/shard_map/all_to_all | solution.py:34
  157.3 6.4 %collective-permute-start.11 = (f32[32,256]{1,0:T(8,128)S(1)}, f32[32,256]{1,0:T(8,128)S(1)}, u32[]{:S(2)}, u32[]{:S(2)}) collective-permute-start(f32[32,256]{1,0:T(8,128)S(1)} %fusion.9), channel_id=1, source_target_pairs={{0,1},{1,0},{2,3},{3,2},{4,5},{5,4},{6,7},{7,6},{8,9},{9,8},{10,11... | collective-permute-start | bytes 98312 | tf_op jit(solution)/shard_map/ppermute | solution.py:30
  163.8 4.3 %all-to-all-done.4 = f32[8,48,256]{2,1,0:T(8,128)S(1)} async-done(((f32[8,48,256]{2,1,0:T(8,128)}), f32[8,48,256]{2,1,0:T(8,128)S(1)}, u32[]{:S(2)}, u32[]{:S(2)}) %all-to-all-start.4) | async-done | bytes 393248 | tf_op jit(solution)/shard_map/all_to_all | solution.py:34
  168.1 7.5 %collective-permute-start.12 = (f32[384,256]{1,0:T(8,128)S(1)}, f32[384,256]{1,0:T(8,128)S(1)}, u32[]{:S(2)}, u32[]{:S(2)}) collective-permute-start(f32[384,256]{1,0:T(8,128)S(1)} %bitcast.77), channel_id=1, source_target_pairs={{0,1},{1,0},{2,3},{3,2},{4,5},{5,4},{6,7},{7,6},{8,9},{9,8},{10,11... | collective-permute-start | bytes 1179656 | tf_op jit(solution)/shard_map/ppermute | solution.py:30
  175.7 0.0 collective-permute-done.11
  175.7 0.0 copy-start.8
  175.7 0.8 bitcast_subtract_fusion
  176.5 0.5 collective-permute-done.12
  177.0 0.1 broadcast_select_fusion
  177.1 0.0 copy-start.4
  177.1 0.3 convolution_subtract_fusion.1
  177.4 0.4 copy-done.4
  177.8 0.4 convolution_bitcast_fusion
  178.2 0.3 copy-done.5
  178.5 1.1 fusion.1
  (45 shorter events, 0.5 us)
Async XLA Ops:
  0.6 175.1 %copy-start = (f32[256,256]{1,0:T(8,128)S(1)}, f32[256,256]{1,0:T(8,128)}, u32[]{:S(2)}) copy-start(f32[256,256]{1,0:T(8,128)} %param.13) | copy-start | bytes 786436
  0.6 47.0 %collective-permute-start.2 = (f32[512,512]{1,0:T(8,128)}, f32[512,512]{1,0:T(8,128)S(1)}, u32[]{:S(2)}, u32[]{:S(2)}) collective-permute-start(f32[512,512]{1,0:T(8,128)} %param.7), channel_id=1, source_target_pairs={{0,1},{1,0},{2,3},{3,2},{4,5},{5,4},{6,7},{7,6},{8,9},{9,8},{10,11... | collective-permute-start | bytes 3145736 | tf_op jit(solution)/shard_map/ppermute | solution.py:30
  16.9 0.7 copy-start.11
  17.6 0.7 copy-start.9
  17.6 0.7 copy-start.10
  19.7 13.8 %collective-permute-start.1 = (f32[16,256]{1,0:T(8,128)S(1)}, f32[16,256]{1,0:T(8,128)S(1)}, u32[]{:S(2)}, u32[]{:S(2)}) collective-permute-start(f32[16,256]{1,0:T(8,128)S(1)} %broadcast_select_fusion.6), channel_id=1, source_target_pairs={{0,1},{1,33},{2,65},{3,97},{4,129},{5,161},{6,193},{7,225},{8,257}... | collective-permute-start | bytes 49160 | tf_op jit(solution)/shard_map/ppermute | solution.py:68
  21.6 11.8 %collective-permute-start = (f32[16,256]{1,0:T(8,128)S(1)}, f32[16,256]{1,0:T(8,128)S(1)}, u32[]{:S(2)}, u32[]{:S(2)}) collective-permute-start(f32[16,256]{1,0:T(8,128)S(1)} %get-tuple-element.5), channel_id=1, source_target_pairs={{0,0},{1,32},{2,64},{3,96},{4,128},{5,160},{6,192},{7,224},{8,256}... | collective-permute-start | bytes 49160 | tf_op jit(solution)/shard_map/ppermute | solution.py:67
  25.2 22.4 %collective-permute-start.3 = (f32[16,512]{1,0:T(8,128)S(1)}, f32[16,512]{1,0:T(8,128)S(1)}, u32[]{:S(2)}, u32[]{:S(2)}) collective-permute-start(f32[16,512]{1,0:T(8,128)S(1)} %pad_maximum_fusion.7), channel_id=1, source_target_pairs={{0,2},{2,0},{1,3},{3,1},{4,6},{6,4},{5,7},{7,5},{8,10},{10,8},{9,1... | collective-permute-start | bytes 98312 | tf_op jit(solution)/shard_map/ppermute | solution.py:30
  34.6 48.5 %all-to-all-start = ((f32[32,2,16,256]{3,2,1,0:T(8,128)}), f32[32,2,16,256]{3,2,1,0:T(8,128)S(1)}, u32[]{:S(2)}, u32[]{:S(2)}) async-start(f32[32,2,16,256]{3,2,1,0:T(8,128)} %broadcast_in_dim.39), calls=%async_computation | async-start | bytes 2097152 | tf_op jit(solution)/shard_map/all_to_all | solution.py:34
  47.6 24.6 %copy-start.1 = (f32[512,512]{1,0:T(8,128)}, f32[512,512]{1,0:T(8,128)S(1)}, u32[]{:S(2)}) copy-start(f32[512,512]{1,0:T(8,128)S(1)} %collective-permute-done.2) | copy-start | bytes 3145732
  47.7 13.0 %collective-permute-start.4 = (f32[2,16,512]{2,1,0:T(8,128)S(1)}, f32[2,16,512]{2,1,0:T(8,128)S(1)}, u32[]{:S(2)}, u32[]{:S(2)}) collective-permute-start(f32[2,16,512]{2,1,0:T(8,128)S(1)} %maximum_add_fusion.1), channel_id=1, source_target_pairs={{0,8},{4,12},{8,0},{12,4},{16,24},{20,28},{24,16},{28,20},{1,9},{5... | collective-permute-start | bytes 196616 | tf_op jit(solution)/shard_map/ppermute | solution.py:81
  53.5 8.9 %collective-permute-start.5 = (f32[2,16,512]{2,1,0:T(8,128)S(1)}, f32[2,16,512]{2,1,0:T(8,128)S(1)}, u32[]{:S(2)}, u32[]{:S(2)}) collective-permute-start(f32[2,16,512]{2,1,0:T(8,128)S(1)} %maximum_add_fusion.1), channel_id=1, source_target_pairs={{0,16},{4,20},{8,24},{12,28},{16,0},{20,4},{24,8},{28,12},{1,17},{... | collective-permute-start | bytes 196616 | tf_op jit(solution)/shard_map/ppermute | solution.py:81
  58.3 7.9 %collective-permute-start.6 = (f32[2,16,512]{2,1,0:T(8,128)S(1)}, f32[2,16,512]{2,1,0:T(8,128)S(1)}, u32[]{:S(2)}, u32[]{:S(2)}) collective-permute-start(f32[2,16,512]{2,1,0:T(8,128)S(1)} %maximum_add_fusion.1), channel_id=1, source_target_pairs={{0,24},{4,28},{8,16},{12,20},{16,8},{20,12},{24,0},{28,4},{1,25},{... | collective-permute-start | bytes 196616 | tf_op jit(solution)/shard_map/ppermute | solution.py:81
  66.3 11.7 %collective-permute-start.7 = (f32[4,2,16,512]{3,2,1,0:T(8,128)S(1)}, f32[4,2,16,512]{3,2,1,0:T(8,128)S(1)}, u32[]{:S(2)}, u32[]{:S(2)}) collective-permute-start(f32[4,2,16,512]{3,2,1,0:T(8,128)S(1)} %bitcast_dynamic-update-slice_fusion), channel_id=1, source_target_pairs={{0,4},{4,0},{8,12},{12,8},{16,20},{20,16},{24,28},{28,24},{1,5},{5... | collective-permute-start | bytes 786440 | tf_op jit(solution)/shard_map/ppermute | solution.py:83
  78.1 4.9 %collective-permute-start.8 = (f32[4,2,2,16,512]{4,3,2,1,0:T(8,128)S(1)}, f32[4,2,2,16,512]{4,3,2,1,0:T(8,128)S(1)}, u32[]{:S(2)}, u32[]{:S(2)}) collective-permute-start(f32[4,2,2,16,512]{4,3,2,1,0:T(8,128)S(1)} %pad_maximum_fusion.2), channel_id=1, source_target_pairs={{0,1},{1,0},{2,3},{3,2},{4,5},{5,4},{6,7},{7,6},{8,9},{9,8},{10,11... | collective-permute-start | bytes 1572872 | tf_op jit(solution)/shard_map/ppermute | solution.py:30
  83.1 1.2 copy-start.3
  84.4 1.2 copy-start.2
  86.7 3.4 %collective-permute-start.9 = (f32[512,128]{0,1:T(8,128)S(1)}, f32[512,128]{0,1:T(8,128)S(1)}, u32[]{:S(2)}, u32[]{:S(2)}) collective-permute-start(f32[512,128]{0,1:T(8,128)S(1)} %slice.72), channel_id=1, source_target_pairs={{0,1},{1,0},{2,3},{3,2},{4,5},{5,4},{6,7},{7,6},{8,9},{9,8},{10,11... | collective-permute-start | bytes 786440 | tf_op jit(solution)/shard_map/ppermute | solution.py:30
  119.0 18.6 %all-to-all-start.2 = ((f32[8,48,256]{2,1,0:T(8,128)}), f32[8,48,256]{2,1,0:T(8,128)S(1)}, u32[]{:S(2)}, u32[]{:S(2)}) async-start(f32[8,48,256]{2,1,0:T(8,128)} %broadcast_in_dim.44), calls=%async_computation.2 | async-start | bytes 786432 | tf_op jit(solution)/shard_map/all_to_all | solution.py:34
  125.4 8.7 %collective-permute-start.10 = (f32[32,256]{1,0:T(8,128)S(1)}, f32[32,256]{1,0:T(8,128)S(1)}, u32[]{:S(2)}, u32[]{:S(2)}) collective-permute-start(f32[32,256]{1,0:T(8,128)S(1)} %dynamic-slice_bitcast_fusion), channel_id=1, source_target_pairs={{0,2},{2,0},{1,3},{3,1},{4,6},{6,4},{5,7},{7,5},{8,10},{10,8},{9,1... | collective-permute-start | bytes 98312 | tf_op jit(solution)/shard_map/ppermute | solution.py:30
  153.1 10.7 %copy-start.6 = (f32[256,256]{1,0:T(8,128)S(1)}, f32[256,256]{1,0:T(8,128)}, u32[]{:S(2)}) copy-start(f32[256,256]{1,0:T(8,128)} %param.12) | copy-start | bytes 786436
  153.1 10.7 %copy-start.7 = (f32[256,256]{1,0:T(8,128)S(1)}, f32[256,256]{1,0:T(8,128)}, u32[]{:S(2)}) copy-start(f32[256,256]{1,0:T(8,128)} %param.11) | copy-start | bytes 786436
  153.1 15.0 %all-to-all-start.4 = ((f32[8,48,256]{2,1,0:T(8,128)}), f32[8,48,256]{2,1,0:T(8,128)S(1)}, u32[]{:S(2)}, u32[]{:S(2)}) async-start(f32[8,48,256]{2,1,0:T(8,128)} %broadcast_in_dim.46), calls=%async_computation.4 | async-start | bytes 786432 | tf_op jit(solution)/shard_map/all_to_all | solution.py:34
  157.3 18.3 %collective-permute-start.11 = (f32[32,256]{1,0:T(8,128)S(1)}, f32[32,256]{1,0:T(8,128)S(1)}, u32[]{:S(2)}, u32[]{:S(2)}) collective-permute-start(f32[32,256]{1,0:T(8,128)S(1)} %fusion.9), channel_id=1, source_target_pairs={{0,1},{1,0},{2,3},{3,2},{4,5},{5,4},{6,7},{7,6},{8,9},{9,8},{10,11... | collective-permute-start | bytes 98312 | tf_op jit(solution)/shard_map/ppermute | solution.py:30
  168.1 8.9 %collective-permute-start.12 = (f32[384,256]{1,0:T(8,128)S(1)}, f32[384,256]{1,0:T(8,128)S(1)}, u32[]{:S(2)}, u32[]{:S(2)}) collective-permute-start(f32[384,256]{1,0:T(8,128)S(1)} %bitcast.77), channel_id=1, source_target_pairs={{0,1},{1,0},{2,3},{3,2},{4,5},{5,4},{6,7},{7,6},{8,9},{9,8},{10,11... | collective-permute-start | bytes 1179656 | tf_op jit(solution)/shard_map/ppermute | solution.py:30
  175.7 0.8 copy-start.8
  177.1 0.7 copy-start.4
  177.8 0.7 copy-start.5
